TPU v7x, 32 devices: a whole 2x2x4 slice. The times are simulated.
32 devices in a mesh: row: 8 (over y, x, core), col: 4 (over z).
Axes of the slice: x: 2, y: 2, z: 4, core: 2. Of those that a mesh axis runs over, the one named last changes fastest.
Arguments:
- similarity: float32 [2048, 2048], P('row', 'col'), may hold values from 0.1 to 500
- pattern: int32 [8, 8], P('row', 'col'), may hold values from 0 to 1, as said below
Outputs:
- clustered: float32 [2048, 2048], P('row', 'col')
Inputs may be any that keep to these rules, and one draw needn't show every extreme that they name: `pattern`: every diagonal tile (g, g) is stored.
All inputs are finite; a program needn't handle non-finite values.
Results may differ from a plain program's by a relative error of at most 0.0003.
Values may be sent and summed in bfloat16 or wider, within the bound.
No kernel may reach another device: no remote copies, remote signals or barrier semaphores. Data moves between devices by JAX's collectives and lax.ppermute only.
A program may use at most 64 MiB of HBM per device.

v0:
```python
import jax
import jax.numpy as jnp
from jax import lax
from jax.sharding import PartitionSpec as P

TILE = 256


def spread(pattern):
    rows, cols = pattern.shape
    values = pattern.astype(jnp.float32)
    return jnp.broadcast_to(values[:, None, :, None], (rows, TILE, cols, TILE)).reshape(
        rows * TILE, cols * TILE
    )


def tile_sum(left_part, right_part):
    return jnp.dot(left_part, right_part, preferred_element_type=jnp.float32)


def product(operand):
    left = lax.all_gather(operand, "col", axis=1, tiled=True)
    return tile_sum(left, lax.all_gather(operand, "row", axis=0, tiled=True))


def shards(similarity, pattern):
    cells = spread(pattern)
    total_rows = similarity.shape[0] * lax.axis_size("row")
    held = similarity * cells
    start_total = lax.psum(jnp.sum(held, axis=0), "row")
    matrix = held * (total_rows / start_total)[None, :]
    operand = matrix.astype(jnp.bfloat16)
    expanded = product(operand) * cells
    inflated = expanded * expanded
    sums = lax.psum(jnp.sum(inflated, axis=0), "row")
    matrix = inflated * (total_rows / sums)[None, :]
    return matrix


def solution(mesh):
    placed = (P("row", "col"), P("row", "col"))
    return jax.shard_map(
        shards, mesh=mesh, in_specs=placed, out_specs=P("row", "col"), check_vma=False
    )
```

profile of v0, /device:TPU:0, one launch (start us, length us, event | category | flops | bytes accessed | tf_op | source)
XLA Modules:
  0.0 105.6 jit_solution(12832644759939311599)
XLA Ops:
  6.5 0.0 all-gather.3.cloned.1.call-start
  6.5 0.7 convert_bitcast_fusion
  7.2 0.1 broadcast_bitcast_fusion
  7.3 1.1 %multiply_reduce_fusion = f32[512]{0:T(512)S(1)} fusion(f32[256,512]{1,0:T(8,128)} %param.2, f32[512]{0:T(512)S(1)} %bitcast.7), kind=kLoop, calls=%fused_computation.3 | loop fusion | flops 261632 | bytes 528384 | tf_op jit(solution)/shard_map/reduce_sum | solution.py:30
  8.4 15.1 %psum.14 = f32[512]{0:T(512)S(1)} all-reduce(f32[512]{0:T(512)S(1)} %multiply_reduce_fusion), channel_id=1, replica_groups=mesh['row'=8,'col'=4] {'row'}, use_global_device_ids=true, to_apply=%region_1.0 | all-reduce | flops 512 | bytes 4096 | tf_op jit(solution)/shard_map/psum | solution.py:30
  23.5 1.8 %multiply_convert_fusion = bf16[256,512]{1,0:T(8,128)(2,1)} fusion(f32[256,512]{1,0:T(8,128)} %param.2, f32[512]{0:T(512)S(1)} %broadcast_divide_fusion.1, f32[512]{0:T(512)S(1)} %bitcast.8), kind=kLoop, calls=%fused_computation.2 | loop fusion | flops 393216 | bytes 790528 | tf_op jit(solution)/shard_map/convert_element_type | solution.py:32
  25.3 0.0 all-gather.3.cloned.1.call-update
  25.3 0.0 all-gather.5.cloned.1.call-start
  25.4 0.7 all-gather.5.cloned.1.call-update
  26.1 26.7 %all-gather.3.cloned.1.call-done = bf16[256,2048]{1,0:T(8,128)(2,1)} async-done(((bf16[256,512]{1,0:T(8,128)(2,1)}), bf16[256,2048]{1,0:T(8,128)(2,1)}) %all-gather.3.cloned.1.call-update) | async-done | bytes 1048592 | tf_op jit(solution)/shard_map/all_gather | solution.py:22
  52.8 29.3 %all-gather.5.cloned.1.call-done = bf16[2048,512]{1,0:T(8,128)(2,1)} async-done(((bf16[256,512]{1,0:T(8,128)(2,1)}), bf16[2048,512]{1,0:T(8,128)(2,1)}) %all-gather.5.cloned.1.call-update) | async-done | bytes 2097168 | tf_op jit(solution)/shard_map/all_gather | solution.py:23
  82.1 2.6 %fusion.1 = (f32[512]{0:T(512)S(1)}, f32[256,512]{1,0:T(8,128)S(1)}) fusion(f32[512]{0:T(512)S(1)} %bitcast.9, bf16[256,2048]{1,0:T(8,128)(2,1)} %all-gather.3.cloned.1.call-done, bf16[2048,512]{1,0:T(8,128)(2,1)} %all-gather.5.cloned.1.call-done), kind=kOutput, calls=%fused_computation.9 | convolution fusion | flops 537263616 | bytes 3674112 | tf_op jit(solution)/shard_map/dot_general | solution.py:18
  84.7 13.1 %psum.15 = f32[512]{0:T(512)S(1)} all-reduce(f32[512]{0:T(512)S(1)} %get-tuple-element.5), channel_id=1, replica_groups=mesh['row'=8,'col'=4] {'row'}, use_global_device_ids=true, to_apply=%region_3.0 | all-reduce | flops 512 | bytes 4096 | tf_op jit(solution)/shard_map/psum | solution.py:35
  97.9 0.9 broadcast_multiply_fusion
  (3 shorter events, 0.0 us)
Async XLA Ops:
  6.5 46.2 %all-gather.3.cloned.1.call-start = ((), (), s32[]{:S(2)}) async-start(), calls=%async_computation | async-start | bytes 1310720 | tf_op jit(solution)/shard_map/all_gather | solution.py:22
  25.3 56.8 %all-gather.5.cloned.1.call-start = ((), (), s32[]{:S(2)}) async-start(), calls=%async_computation.1 | async-start | bytes 2359296 | tf_op jit(solution)/shard_map/all_gather | solution.py:23
Sparse Core Ops, SparseCore 0:
  25.4 27.2 all-gather.2
  54.7 27.3 all-gather.4
where the time goes:
time: 106 us
  waiting for transfers between devices  56.7 us (53%)
  blocking collectives  28.2 us (27%)
  between operations  13.4 us (13%)
  other arithmetic  4.45 us (4%)
  matrix products  2.64 us (2%)
    all_gather x1, waiting for transfers between devices, product(): return tile_sum(left, lax.all_gather(operand, 'row', axis=0, tiled=True))  29.3 us
    all_gather x1, waiting for transfers between devices, product(): left = lax.all_gather(operand, 'col', axis=1, tiled=True)  26.7 us
    psum x1, blocking collectives, shards(): start_total = lax.psum(jnp.sum(held, axis=0), 'row')  15.1 us
    psum x1, blocking collectives, shards(): sums = lax.psum(jnp.sum(inflated, axis=0), 'row')  13.1 us
    dot_general x1, matrix products, tile_sum(): return jnp.dot(left_part, right_part, preferred_element_type=jnp.float32)  2.64 us
  transfers between devices with their start and end apart: 2, of which 2 were waited for; matrix products, arithmetic and copies ran while one was open for 0% of the time, Pallas kernels for 0%

commit v1 on v0

v1 whole, which is shorter than its diff:
```python
import jax
import jax.numpy as jnp
from jax import lax
from jax.sharding import PartitionSpec as P

TILE = 256


def spread(pattern):
    rows, cols = pattern.shape
    values = pattern.astype(jnp.float32)
    return jnp.broadcast_to(values[:, None, :, None], (rows, TILE, cols, TILE)).reshape(
        rows * TILE, cols * TILE
    )


def swap(x, axis, mask):
    size = lax.axis_size(axis)
    return lax.ppermute(x, axis, [(i, i ^ mask) for i in range(size)])


def total(x, axis):
    mask = 1
    while mask < lax.axis_size(axis):
        x = x + swap(x, axis, mask)
        mask *= 2
    return x


def gather_rows(x):
    size, me = lax.axis_size("row"), lax.axis_index("row")
    depth = x.shape[0]
    got = {0: x}
    for mask in sorted(range(2, size, 2), reverse=True):
        got[mask] = swap(x, "row", mask)
    for mask in range(0, size, 2):
        got[mask + 1] = swap(got[mask], "row", 1)
    whole = jnp.zeros((size * depth, x.shape[1]), x.dtype)
    for mask in range(size):
        whole = lax.dynamic_update_slice(whole, got[mask], ((me ^ mask) * depth, 0))
    return whole


def gather_columns(x):
    size, me = lax.axis_size("col"), lax.axis_index("col")
    width = x.shape[1]
    whole = jnp.zeros((x.shape[0], size * width), x.dtype)
    got = {0: x}
    for mask in range(1, size):
        got[mask] = swap(x, "col", mask)
    for mask in range(size):
        whole = lax.dynamic_update_slice(whole, got[mask], (0, (me ^ mask) * width))
    return whole


def product(operand):
    left = gather_columns(operand)
    right = gather_rows(operand)
    return jnp.dot(left, right, preferred_element_type=jnp.float32)


def shards(similarity, pattern):
    cells = spread(pattern)
    total_rows = similarity.shape[0] * lax.axis_size("row")
    held = similarity * cells
    start_total = total(jnp.sum(held, axis=0), "row")
    matrix = held * (total_rows / start_total)[None, :]
    operand = matrix.astype(jnp.bfloat16)
    expanded = product(operand) * cells
    inflated = expanded * expanded
    sums = total(jnp.sum(inflated, axis=0), "row")
    return inflated * (total_rows / sums)[None, :]


def solution(mesh):
    placed = (P("row", "col"), P("row", "col"))
    return jax.shard_map(
        shards, mesh=mesh, in_specs=placed, out_specs=P("row", "col"), check_vma=False
    )
```

time: 106 us -> 50.7 us (0.48)
  the two profiles are of different devices: /device:TPU:0 before, /device:TPU:10 now
where the time goes in v1:
time: 50.7 us; the launch traced here: 50.5 us
  waiting for transfers between devices  33.2 us (65%)
  starting transfers between devices  13.1 us (26%)
  other arithmetic  2.78 us (5%)
  matrix products  0.72 us (1%)
  local copies, waits for them, and re-layouts  0.59 us (1%)
    ppermute x16, waiting for transfers between devices, swap(): return lax.ppermute(x, axis, [(i, i ^ mask) for i in range(size)])  33.2 us
    ppermute x16, starting transfers between devices, swap(): return lax.ppermute(x, axis, [(i, i ^ mask) for i in range(size)])  13.1 us
    reduce_sum x1, other arithmetic, shards(): start_total = total(jnp.sum(held, axis=0), 'row')  1.1 us
  transfers between devices with their start and end apart: 16, of which 11 were waited for; matrix products, arithmetic and copies ran while one was open for 1% of the time, Pallas kernels for 0%

profile of v1, /device:TPU:10, one launch (start us, length us, event | category | flops | bytes accessed | tf_op | source)
XLA Modules:
  0.0 50.5 jit_solution(1365097251230756567)
XLA Ops:
  0.0 0.0 copy-start
  0.0 0.7 %convert_bitcast_fusion = f32[2]{0:T(128)S(1)} fusion(s32[1,2]{1,0:T(1,128)} %param.3), kind=kLoop, calls=%fused_computation.20 | loop fusion | flops 2 | bytes 16 | tf_op jit(solution)/shard_map/broadcast_in_dim | solution.py:12
  0.7 0.1 broadcast_bitcast_fusion
  0.8 1.1 %multiply_reduce_fusion = f32[512]{0:T(512)S(1)} fusion(f32[256,512]{1,0:T(8,128)} %param.2, f32[512]{0:T(512)S(1)} %bitcast.7), kind=kLoop, calls=%fused_computation.3 | loop fusion | flops 261632 | bytes 528384 | tf_op jit(solution)/shard_map/reduce_sum | solution.py:66
  1.9 0.1 collective-permute-start
  2.0 1.1 %collective-permute-done = f32[512]{0:T(512)S(1)} collective-permute-done((f32[512]{0:T(512)S(1)}, f32[512]{0:T(512)S(1)}, u32[]{:S(2)}, u32[]{:S(2)}) %collective-permute-start) | collective-permute-done | bytes 2080 | tf_op jit(solution)/shard_map/ppermute | solution.py:19
  3.1 0.5 %collective-permute-start.1 = (f32[512]{0:T(512)S(1)}, f32[512]{0:T(512)S(1)}, u32[]{:S(2)}, u32[]{:S(2)}) collective-permute-start(f32[512]{0:T(512)S(1)} %add.54), channel_id=1, source_target_pairs={{0,8},{4,12},{8,0},{12,4},{16,24},{20,28},{24,16},{28,20},{1,9},{5... | collective-permute-start | bytes 6152 | tf_op jit(solution)/shard_map/ppermute | solution.py:19
  3.7 3.0 %collective-permute-done.1 = f32[512]{0:T(512)S(1)} collective-permute-done((f32[512]{0:T(512)S(1)}, f32[512]{0:T(512)S(1)}, u32[]{:S(2)}, u32[]{:S(2)}) %collective-permute-start.1) | collective-permute-done | bytes 2080 | tf_op jit(solution)/shard_map/ppermute | solution.py:19
  6.7 1.5 %collective-permute-start.2 = (f32[512]{0:T(512)S(1)}, f32[512]{0:T(512)S(1)}, u32[]{:S(2)}, u32[]{:S(2)}) collective-permute-start(f32[512]{0:T(512)S(1)} %add.55), channel_id=1, source_target_pairs={{0,16},{4,20},{8,24},{12,28},{16,0},{20,4},{24,8},{28,12},{1,17},{... | collective-permute-start | bytes 6152 | tf_op jit(solution)/shard_map/ppermute | solution.py:19
  8.2 2.1 %collective-permute-done.2 = f32[512]{0:T(512)S(1)} collective-permute-done((f32[512]{0:T(512)S(1)}, f32[512]{0:T(512)S(1)}, u32[]{:S(2)}, u32[]{:S(2)}) %collective-permute-start.2) | collective-permute-done | bytes 2080 | tf_op jit(solution)/shard_map/ppermute | solution.py:19
  10.3 0.1 broadcast_in_dim.25
  10.4 0.0 copy-done
  10.5 0.1 constant_dynamic-update-slice_fusion.7
  10.5 0.1 collective-permute-start.6
  10.6 0.6 %collective-permute-start.7 = (bf16[256,512]{1,0:T(8,128)(2,1)S(1)}, bf16[256,512]{1,0:T(8,128)(2,1)S(1)}, u32[]{:S(2)}, u32[]{:S(2)}) collective-permute-start(bf16[256,512]{1,0:T(8,128)(2,1)S(1)} %get-tuple-element.6), channel_id=1, source_target_pairs={{0,8},{4,12},{8,0},{12,4},{16,24},{20,28},{24,16},{28,20},{1,9},{5... | collective-permute-start | bytes 786440 | tf_op jit(solution)/shard_map/ppermute | solution.py:19
  11.2 1.5 %collective-permute-start.9 = (bf16[256,512]{1,0:T(8,128)(2,1)S(1)}, bf16[256,512]{1,0:T(8,128)(2,1)S(1)}, u32[]{:S(2)}, u32[]{:S(2)}) collective-permute-start(bf16[256,512]{1,0:T(8,128)(2,1)S(1)} %get-tuple-element.6), channel_id=1, source_target_pairs={{0,16},{4,20},{8,24},{12,28},{16,0},{20,4},{24,8},{28,12},{1,17},{... | collective-permute-start | bytes 786440 | tf_op jit(solution)/shard_map/ppermute | solution.py:19
  12.7 1.4 %collective-permute-start.11 = (bf16[256,512]{1,0:T(8,128)(2,1)S(1)}, bf16[256,512]{1,0:T(8,128)(2,1)S(1)}, u32[]{:S(2)}, u32[]{:S(2)}) collective-permute-start(bf16[256,512]{1,0:T(8,128)(2,1)S(1)} %get-tuple-element.6), channel_id=1, source_target_pairs={{0,24},{4,28},{8,16},{12,20},{16,8},{20,12},{24,0},{28,4},{1,25},{... | collective-permute-start | bytes 786440 | tf_op jit(solution)/shard_map/ppermute | solution.py:19
  14.2 0.4 collective-permute-start.3
  14.6 0.1 broadcast_in_dim.20
  14.8 0.0 collective-permute-done.6
  14.8 2.7 %collective-permute-start.4 = (bf16[256,512]{1,0:T(8,128)(2,1)S(1)}, bf16[256,512]{1,0:T(8,128)(2,1)S(1)}, u32[]{:S(2)}, u32[]{:S(2)}) collective-permute-start(bf16[256,512]{1,0:T(8,128)(2,1)S(1)} %get-tuple-element.6), channel_id=1, source_target_pairs={{0,2},{1,3},{2,0},{3,1},{4,6},{5,7},{6,4},{7,5},{8,10},{9,11},{10,... | collective-permute-start | bytes 786440 | tf_op jit(solution)/shard_map/ppermute | solution.py:19
  17.5 2.3 %collective-permute-done.7 = bf16[256,512]{1,0:T(8,128)(2,1)S(1)} collective-permute-done((bf16[256,512]{1,0:T(8,128)(2,1)S(1)}, bf16[256,512]{1,0:T(8,128)(2,1)S(1)}, u32[]{:S(2)}, u32[]{:S(2)}) %collective-permute-start.7) | collective-permute-done | bytes 262176 | tf_op jit(solution)/shard_map/ppermute | solution.py:19
  19.8 1.6 %collective-permute-start.5 = (bf16[256,512]{1,0:T(8,128)(2,1)S(1)}, bf16[256,512]{1,0:T(8,128)(2,1)S(1)}, u32[]{:S(2)}, u32[]{:S(2)}) collective-permute-start(bf16[256,512]{1,0:T(8,128)(2,1)S(1)} %get-tuple-element.6), channel_id=1, source_target_pairs={{0,3},{1,2},{2,1},{3,0},{4,7},{5,6},{6,5},{7,4},{8,11},{9,10},{10,... | collective-permute-start | bytes 786440 | tf_op jit(solution)/shard_map/ppermute | solution.py:19
  21.4 2.9 %collective-permute-done.9 = bf16[256,512]{1,0:T(8,128)(2,1)S(1)} collective-permute-done((bf16[256,512]{1,0:T(8,128)(2,1)S(1)}, bf16[256,512]{1,0:T(8,128)(2,1)S(1)}, u32[]{:S(2)}, u32[]{:S(2)}) %collective-permute-start.9) | collective-permute-done | bytes 262176 | tf_op jit(solution)/shard_map/ppermute | solution.py:19
  24.3 0.0 collective-permute-start.8
  24.3 1.6 %collective-permute-done.11 = bf16[256,512]{1,0:T(8,128)(2,1)S(1)} collective-permute-done((bf16[256,512]{1,0:T(8,128)(2,1)S(1)}, bf16[256,512]{1,0:T(8,128)(2,1)S(1)}, u32[]{:S(2)}, u32[]{:S(2)}) %collective-permute-start.11) | collective-permute-done | bytes 262176 | tf_op jit(solution)/shard_map/ppermute | solution.py:19
  25.9 0.0 collective-permute-start.10
  25.9 0.0 collective-permute-done.3
  25.9 0.5 %collective-permute-start.12 = (bf16[256,512]{1,0:T(8,128)(2,1)S(1)}, bf16[256,512]{1,0:T(8,128)(2,1)S(1)}, u32[]{:S(2)}, u32[]{:S(2)}) collective-permute-start(bf16[256,512]{1,0:T(8,128)(2,1)S(1)} %collective-permute-done.11), channel_id=1, source_target_pairs={{0,4},{4,0},{8,12},{12,8},{16,20},{20,16},{24,28},{28,24},{1,5},{5... | collective-permute-start | bytes 786440 | tf_op jit(solution)/shard_map/ppermute | solution.py:19
  26.5 9.0 %collective-permute-done.4 = bf16[256,512]{1,0:T(8,128)(2,1)S(1)} collective-permute-done((bf16[256,512]{1,0:T(8,128)(2,1)S(1)}, bf16[256,512]{1,0:T(8,128)(2,1)S(1)}, u32[]{:S(2)}, u32[]{:S(2)}) %collective-permute-start.4) | collective-permute-done | bytes 262176 | tf_op jit(solution)/shard_map/ppermute | solution.py:19
  35.5 4.8 %collective-permute-done.5 = bf16[256,512]{1,0:T(8,128)(2,1)S(1)} collective-permute-done((bf16[256,512]{1,0:T(8,128)(2,1)S(1)}, bf16[256,512]{1,0:T(8,128)(2,1)S(1)}, u32[]{:S(2)}, u32[]{:S(2)}) %collective-permute-start.5) | collective-permute-done | bytes 262176 | tf_op jit(solution)/shard_map/ppermute | solution.py:19
  40.3 0.0 collective-permute-done.8
  40.4 0.0 collective-permute-done.10
  40.5 0.0 collective-permute-done.12
  40.5 0.7 %fusion.1 = (f32[512]{0:T(512)S(1)}, f32[256,512]{1,0:T(8,128)S(1)}) fusion(f32[512]{0:T(512)S(1)} %bitcast.9, bf16[256,2048]{1,0:T(8,128)(2,1)S(1)} %constant_dynamic-update-slice_fusion.8, bf16[2048,512]{1,0:T(8,128)(2,1)S(1)} %constant_dynamic-update-slice_fusion), kind=kOutput, calls=%fused_computation.21 | convolution fusion | flops 537263616 | bytes 3674112 | tf_op jit(solution)/shard_map/dot_general | solution.py:59
  41.3 0.1 collective-permute-start.13
  41.3 1.1 %collective-permute-done.13 = f32[512]{0:T(512)S(1)} collective-permute-done((f32[512]{0:T(512)S(1)}, f32[512]{0:T(512)S(1)}, u32[]{:S(2)}, u32[]{:S(2)}) %collective-permute-start.13) | collective-permute-done | bytes 2080 | tf_op jit(solution)/shard_map/ppermute | solution.py:19
  42.5 0.5 %collective-permute-start.14 = (f32[512]{0:T(512)S(1)}, f32[512]{0:T(512)S(1)}, u32[]{:S(2)}, u32[]{:S(2)}) collective-permute-start(f32[512]{0:T(512)S(1)} %add.69), channel_id=1, source_target_pairs={{0,8},{4,12},{8,0},{12,4},{16,24},{20,28},{24,16},{28,20},{1,9},{5... | collective-permute-start | bytes 6152 | tf_op jit(solution)/shard_map/ppermute | solution.py:19
  43.0 3.1 %collective-permute-done.14 = f32[512]{0:T(512)S(1)} collective-permute-done((f32[512]{0:T(512)S(1)}, f32[512]{0:T(512)S(1)}, u32[]{:S(2)}, u32[]{:S(2)}) %collective-permute-start.14) | collective-permute-done | bytes 2080 | tf_op jit(solution)/shard_map/ppermute | solution.py:19
  46.1 1.5 %collective-permute-start.15 = (f32[512]{0:T(512)S(1)}, f32[512]{0:T(512)S(1)}, u32[]{:S(2)}, u32[]{:S(2)}) collective-permute-start(f32[512]{0:T(512)S(1)} %add.70), channel_id=1, source_target_pairs={{0,16},{4,20},{8,24},{12,28},{16,0},{20,4},{24,8},{28,12},{1,17},{... | collective-permute-start | bytes 6152 | tf_op jit(solution)/shard_map/ppermute | solution.py:19
  47.6 2.1 %collective-permute-done.15 = f32[512]{0:T(512)S(1)} collective-permute-done((f32[512]{0:T(512)S(1)}, f32[512]{0:T(512)S(1)}, u32[]{:S(2)}, u32[]{:S(2)}) %collective-permute-start.15) | collective-permute-done | bytes 2080 | tf_op jit(solution)/shard_map/ppermute | solution.py:19
  49.7 0.9 %broadcast_multiply_fusion = f32[256,512]{1,0:T(8,128)} fusion(f32[256,512]{1,0:T(8,128)S(1)} %get-tuple-element.8, f32[512]{0:T(512)S(1)} %add_divide_fusion), kind=kLoop, calls=%fused_computation.4 | loop fusion | flops 131072 | bytes 1050624 | tf_op jit(solution)/shard_map/mul | solution.py:72
  (18 shorter events, 0.3 us)
Async XLA Ops:
  0.0 10.4 %copy-start = (f32[256,512]{1,0:T(8,128)S(1)}, f32[256,512]{1,0:T(8,128)}, u32[]{:S(2)}) copy-start(f32[256,512]{1,0:T(8,128)} %param.2) | copy-start | bytes 1572868
  1.9 1.2 %collective-permute-start = (f32[512]{0:T(512)S(1)}, f32[512]{0:T(512)S(1)}, u32[]{:S(2)}, u32[]{:S(2)}) collective-permute-start(f32[512]{0:T(512)S(1)} %multiply_reduce_fusion), channel_id=1, source_target_pairs={{0,4},{4,0},{8,12},{12,8},{16,20},{20,16},{24,28},{28,24},{1,5},{5... | collective-permute-start | bytes 6152 | tf_op jit(solution)/shard_map/ppermute | solution.py:19
  3.1 3.6 %collective-permute-start.1 = (f32[512]{0:T(512)S(1)}, f32[512]{0:T(512)S(1)}, u32[]{:S(2)}, u32[]{:S(2)}) collective-permute-start(f32[512]{0:T(512)S(1)} %add.54), channel_id=1, source_target_pairs={{0,8},{4,12},{8,0},{12,4},{16,24},{20,28},{24,16},{28,20},{1,9},{5... | collective-permute-start | bytes 6152 | tf_op jit(solution)/shard_map/ppermute | solution.py:19
  6.7 3.6 %collective-permute-start.2 = (f32[512]{0:T(512)S(1)}, f32[512]{0:T(512)S(1)}, u32[]{:S(2)}, u32[]{:S(2)}) collective-permute-start(f32[512]{0:T(512)S(1)} %add.55), channel_id=1, source_target_pairs={{0,16},{4,20},{8,24},{12,28},{16,0},{20,4},{24,8},{28,12},{1,17},{... | collective-permute-start | bytes 6152 | tf_op jit(solution)/shard_map/ppermute | solution.py:19
  10.5 4.2 %collective-permute-start.6 = (bf16[256,512]{1,0:T(8,128)(2,1)S(1)}, bf16[256,512]{1,0:T(8,128)(2,1)S(1)}, u32[]{:S(2)}, u32[]{:S(2)}) collective-permute-start(bf16[256,512]{1,0:T(8,128)(2,1)S(1)} %get-tuple-element.6), channel_id=1, source_target_pairs={{0,4},{4,0},{8,12},{12,8},{16,20},{20,16},{24,28},{28,24},{1,5},{5... | collective-permute-start | bytes 786440 | tf_op jit(solution)/shard_map/ppermute | solution.py:19
  10.6 9.2 %collective-permute-start.7 = (bf16[256,512]{1,0:T(8,128)(2,1)S(1)}, bf16[256,512]{1,0:T(8,128)(2,1)S(1)}, u32[]{:S(2)}, u32[]{:S(2)}) collective-permute-start(bf16[256,512]{1,0:T(8,128)(2,1)S(1)} %get-tuple-element.6), channel_id=1, source_target_pairs={{0,8},{4,12},{8,0},{12,4},{16,24},{20,28},{24,16},{28,20},{1,9},{5... | collective-permute-start | bytes 786440 | tf_op jit(solution)/shard_map/ppermute | solution.py:19
  11.2 13.1 %collective-permute-start.9 = (bf16[256,512]{1,0:T(8,128)(2,1)S(1)}, bf16[256,512]{1,0:T(8,128)(2,1)S(1)}, u32[]{:S(2)}, u32[]{:S(2)}) collective-permute-start(bf16[256,512]{1,0:T(8,128)(2,1)S(1)} %get-tuple-element.6), channel_id=1, source_target_pairs={{0,16},{4,20},{8,24},{12,28},{16,0},{20,4},{24,8},{28,12},{1,17},{... | collective-permute-start | bytes 786440 | tf_op jit(solution)/shard_map/ppermute | solution.py:19
  12.7 13.2 %collective-permute-start.11 = (bf16[256,512]{1,0:T(8,128)(2,1)S(1)}, bf16[256,512]{1,0:T(8,128)(2,1)S(1)}, u32[]{:S(2)}, u32[]{:S(2)}) collective-permute-start(bf16[256,512]{1,0:T(8,128)(2,1)S(1)} %get-tuple-element.6), channel_id=1, source_target_pairs={{0,24},{4,28},{8,16},{12,20},{16,8},{20,12},{24,0},{28,4},{1,25},{... | collective-permute-start | bytes 786440 | tf_op jit(solution)/shard_map/ppermute | solution.py:19
  14.2 11.7 %collective-permute-start.3 = (bf16[256,512]{1,0:T(8,128)(2,1)S(1)}, bf16[256,512]{1,0:T(8,128)(2,1)S(1)}, u32[]{:S(2)}, u32[]{:S(2)}) collective-permute-start(bf16[256,512]{1,0:T(8,128)(2,1)S(1)} %get-tuple-element.6), channel_id=1, source_target_pairs={{0,1},{1,0},{2,3},{3,2},{4,5},{5,4},{6,7},{7,6},{8,9},{9,8},{10,11... | collective-permute-start | bytes 786440 | tf_op jit(solution)/shard_map/ppermute | solution.py:19
  14.8 20.7 %collective-permute-start.4 = (bf16[256,512]{1,0:T(8,128)(2,1)S(1)}, bf16[256,512]{1,0:T(8,128)(2,1)S(1)}, u32[]{:S(2)}, u32[]{:S(2)}) collective-permute-start(bf16[256,512]{1,0:T(8,128)(2,1)S(1)} %get-tuple-element.6), channel_id=1, source_target_pairs={{0,2},{1,3},{2,0},{3,1},{4,6},{5,7},{6,4},{7,5},{8,10},{9,11},{10,... | collective-permute-start | bytes 786440 | tf_op jit(solution)/shard_map/ppermute | solution.py:19
  19.8 20.5 %collective-permute-start.5 = (bf16[256,512]{1,0:T(8,128)(2,1)S(1)}, bf16[256,512]{1,0:T(8,128)(2,1)S(1)}, u32[]{:S(2)}, u32[]{:S(2)}) collective-permute-start(bf16[256,512]{1,0:T(8,128)(2,1)S(1)} %get-tuple-element.6), channel_id=1, source_target_pairs={{0,3},{1,2},{2,1},{3,0},{4,7},{5,6},{6,5},{7,4},{8,11},{9,10},{10,... | collective-permute-start | bytes 786440 | tf_op jit(solution)/shard_map/ppermute | solution.py:19
  24.3 16.1 %collective-permute-start.8 = (bf16[256,512]{1,0:T(8,128)(2,1)S(1)}, bf16[256,512]{1,0:T(8,128)(2,1)S(1)}, u32[]{:S(2)}, u32[]{:S(2)}) collective-permute-start(bf16[256,512]{1,0:T(8,128)(2,1)S(1)} %collective-permute-done.7), channel_id=1, source_target_pairs={{0,4},{4,0},{8,12},{12,8},{16,20},{20,16},{24,28},{28,24},{1,5},{5... | collective-permute-start | bytes 786440 | tf_op jit(solution)/shard_map/ppermute | solution.py:19
  25.9 14.5 %collective-permute-start.10 = (bf16[256,512]{1,0:T(8,128)(2,1)S(1)}, bf16[256,512]{1,0:T(8,128)(2,1)S(1)}, u32[]{:S(2)}, u32[]{:S(2)}) collective-permute-start(bf16[256,512]{1,0:T(8,128)(2,1)S(1)} %collective-permute-done.9), channel_id=1, source_target_pairs={{0,4},{4,0},{8,12},{12,8},{16,20},{20,16},{24,28},{28,24},{1,5},{5... | collective-permute-start | bytes 786440 | tf_op jit(solution)/shard_map/ppermute | solution.py:19
  25.9 14.6 %collective-permute-start.12 = (bf16[256,512]{1,0:T(8,128)(2,1)S(1)}, bf16[256,512]{1,0:T(8,128)(2,1)S(1)}, u32[]{:S(2)}, u32[]{:S(2)}) collective-permute-start(bf16[256,512]{1,0:T(8,128)(2,1)S(1)} %collective-permute-done.11), channel_id=1, source_target_pairs={{0,4},{4,0},{8,12},{12,8},{16,20},{20,16},{24,28},{28,24},{1,5},{5... | collective-permute-start | bytes 786440 | tf_op jit(solution)/shard_map/ppermute | solution.py:19
  41.3 1.2 %collective-permute-start.13 = (f32[512]{0:T(512)S(1)}, f32[512]{0:T(512)S(1)}, u32[]{:S(2)}, u32[]{:S(2)}) collective-permute-start(f32[512]{0:T(512)S(1)} %get-tuple-element.7), channel_id=1, source_target_pairs={{0,4},{4,0},{8,12},{12,8},{16,20},{20,16},{24,28},{28,24},{1,5},{5... | collective-permute-start | bytes 6152 | tf_op jit(solution)/shard_map/ppermute | solution.py:19
  42.5 3.6 %collective-permute-start.14 = (f32[512]{0:T(512)S(1)}, f32[512]{0:T(512)S(1)}, u32[]{:S(2)}, u32[]{:S(2)}) collective-permute-start(f32[512]{0:T(512)S(1)} %add.69), channel_id=1, source_target_pairs={{0,8},{4,12},{8,0},{12,4},{16,24},{20,28},{24,16},{28,20},{1,9},{5... | collective-permute-start | bytes 6152 | tf_op jit(solution)/shard_map/ppermute | solution.py:19
  46.1 3.6 %collective-permute-start.15 = (f32[512]{0:T(512)S(1)}, f32[512]{0:T(512)S(1)}, u32[]{:S(2)}, u32[]{:S(2)}) collective-permute-start(f32[512]{0:T(512)S(1)} %add.70), channel_id=1, source_target_pairs={{0,16},{4,20},{8,24},{12,28},{16,0},{20,4},{24,8},{28,12},{1,17},{... | collective-permute-start | bytes 6152 | tf_op jit(solution)/shard_map/ppermute | solution.py:19

commit v2 on v1

v2 whole, which is shorter than its diff:
```python
import jax
import jax.numpy as jnp
from jax import lax
from jax.sharding import PartitionSpec as P

TILE = 256


def spread(pattern):
    rows, cols = pattern.shape
    values = pattern.astype(jnp.float32)
    return jnp.broadcast_to(values[:, None, :, None], (rows, TILE, cols, TILE)).reshape(
        rows * TILE, cols * TILE
    )


def swap(x, axis, mask):
    size = lax.axis_size(axis)
    return lax.ppermute(x, axis, [(i, i ^ mask) for i in range(size)])


def total(x, axis):
    mask = 1
    while mask < lax.axis_size(axis):
        x = x + swap(x, axis, mask)
        mask *= 2
    return x


def join_rows(blocks):
    size, me = lax.axis_size("row"), lax.axis_index("row")
    depth, width = blocks[0].shape
    whole = jnp.zeros((size * depth, width), blocks[0].dtype)
    for mask in range(size):
        whole = lax.dynamic_update_slice(whole, blocks[mask], ((me ^ mask) * depth, 0))
    return whole


def join_columns(blocks):
    size, me = lax.axis_size("col"), lax.axis_index("col")
    depth, width = blocks[0].shape
    whole = jnp.zeros((depth, size * width), blocks[0].dtype)
    for mask in range(size):
        whole = lax.dynamic_update_slice(whole, blocks[mask], (0, (me ^ mask) * width))
    return whole


def scaled(held, scale):
    return (held * scale[None, :]).astype(jnp.bfloat16)


def gather_columns(x):
    got = {0: x}
    for mask in range(1, lax.axis_size("col")):
        low = mask & -mask
        got[mask] = swap(got[mask - low], "col", low)
    return join_columns(got)


def gather_rows(x):
    got = {0: x}
    for mask in range(2, lax.axis_size("row"), 2):
        got[mask] = swap(x, "row", mask)
    for mask in range(0, lax.axis_size("row"), 2):
        got[mask + 1] = swap(got[mask], "row", 1)
    return join_rows(got)


def shards(similarity, pattern):
    cells = spread(pattern)
    total_rows = similarity.shape[0] * lax.axis_size("row")
    held = similarity * cells
    scale = total_rows / total(jnp.sum(held, axis=0), "row")
    operand = scaled(held, scale)

    left, right = gather_columns(operand), gather_rows(operand)
    expanded = jnp.dot(left, right, preferred_element_type=jnp.float32) * cells
    inflated = expanded * expanded
    sums = total(jnp.sum(inflated, axis=0), "row")
    return inflated * (total_rows / sums)[None, :]


def solution(mesh):
    placed = (P("row", "col"), P("row", "col"))
    return jax.shard_map(
        shards, mesh=mesh, in_specs=placed, out_specs=P("row", "col"), check_vma=False
    )
```

time: 50.7 us -> 47.4 us (0.935)
  the two profiles are of different devices: /device:TPU:10 before, /device:TPU:0 now
where the time goes in v2:
time: 47.4 us; the launch traced here: 47.2 us
  waiting for transfers between devices  24.1 us (51%)
  starting transfers between devices  17.8 us (38%)
  other arithmetic  2.78 us (6%)
  local copies, waits for them, and re-layouts  1.55 us (3%)
  matrix products  0.72 us (2%)
    ppermute x16, waiting for transfers between devices, swap(): return lax.ppermute(x, axis, [(i, i ^ mask) for i in range(size)])  24.1 us
    ppermute x16, starting transfers between devices, swap(): return lax.ppermute(x, axis, [(i, i ^ mask) for i in range(size)])  17.8 us
    dynamic_update_slice x7, local copies, waits for them, and re-layouts, join_rows(): lax.dynamic_update_slice(whole, blocks[mask], ((me ^ mask) * depth, 0))  1.12 us
    reduce_sum x1, other arithmetic, shards(): scale = total_rows / total(jnp.sum(held, axis=0), 'row')  1.1 us
  transfers between devices with their start and end apart: 16, of which 10 were waited for; matrix products, arithmetic and copies ran while one was open for 3% of the time, Pallas kernels for 0%

profile of v2, /device:TPU:0, one launch (start us, length us, event | category | flops | bytes accessed | tf_op | source)
XLA Modules:
  0.0 47.2 jit_solution(18067575051101830686)
XLA Ops:
  0.0 0.0 copy-start
  0.0 0.7 %convert_bitcast_fusion = f32[2]{0:T(128)S(1)} fusion(s32[1,2]{1,0:T(1,128)} %param.3), kind=kLoop, calls=%fused_computation.20 | loop fusion | flops 2 | bytes 16 | tf_op jit(solution)/shard_map/broadcast_in_dim | solution.py:12
  0.7 0.1 broadcast_bitcast_fusion
  0.8 1.1 %multiply_reduce_fusion = f32[512]{0:T(512)S(1)} fusion(f32[256,512]{1,0:T(8,128)} %param.2, f32[512]{0:T(512)S(1)} %bitcast.7), kind=kLoop, calls=%fused_computation.3 | loop fusion | flops 261632 | bytes 528384 | tf_op jit(solution)/shard_map/reduce_sum | solution.py:73
  1.9 0.5 %collective-permute-start = (f32[512]{0:T(512)S(1)}, f32[512]{0:T(512)S(1)}, u32[]{:S(2)}, u32[]{:S(2)}) collective-permute-start(f32[512]{0:T(512)S(1)} %multiply_reduce_fusion), channel_id=1, source_target_pairs={{0,4},{4,0},{8,12},{12,8},{16,20},{20,16},{24,28},{28,24},{1,5},{5... | collective-permute-start | bytes 6152 | tf_op jit(solution)/shard_map/ppermute | solution.py:19
  2.4 0.8 %collective-permute-done = f32[512]{0:T(512)S(1)} collective-permute-done((f32[512]{0:T(512)S(1)}, f32[512]{0:T(512)S(1)}, u32[]{:S(2)}, u32[]{:S(2)}) %collective-permute-start) | collective-permute-done | bytes 2080 | tf_op jit(solution)/shard_map/ppermute | solution.py:19
  3.2 2.8 %collective-permute-start.1 = (f32[512]{0:T(512)S(1)}, f32[512]{0:T(512)S(1)}, u32[]{:S(2)}, u32[]{:S(2)}) collective-permute-start(f32[512]{0:T(512)S(1)} %add.54), channel_id=1, source_target_pairs={{0,8},{4,12},{8,0},{12,4},{16,24},{20,28},{24,16},{28,20},{1,9},{5... | collective-permute-start | bytes 6152 | tf_op jit(solution)/shard_map/ppermute | solution.py:19
  6.1 1.6 %collective-permute-done.1 = f32[512]{0:T(512)S(1)} collective-permute-done((f32[512]{0:T(512)S(1)}, f32[512]{0:T(512)S(1)}, u32[]{:S(2)}, u32[]{:S(2)}) %collective-permute-start.1) | collective-permute-done | bytes 2080 | tf_op jit(solution)/shard_map/ppermute | solution.py:19
  7.6 2.1 %collective-permute-start.2 = (f32[512]{0:T(512)S(1)}, f32[512]{0:T(512)S(1)}, u32[]{:S(2)}, u32[]{:S(2)}) collective-permute-start(f32[512]{0:T(512)S(1)} %add.55), channel_id=1, source_target_pairs={{0,16},{4,20},{8,24},{12,28},{16,0},{20,4},{24,8},{28,12},{1,17},{... | collective-permute-start | bytes 6152 | tf_op jit(solution)/shard_map/ppermute | solution.py:19
  9.7 1.6 %collective-permute-done.2 = f32[512]{0:T(512)S(1)} collective-permute-done((f32[512]{0:T(512)S(1)}, f32[512]{0:T(512)S(1)}, u32[]{:S(2)}, u32[]{:S(2)}) %collective-permute-start.2) | collective-permute-done | bytes 2080 | tf_op jit(solution)/shard_map/ppermute | solution.py:19
  11.2 0.1 broadcast_in_dim.25
  11.4 0.0 copy-done
  11.4 0.1 constant_dynamic-update-slice_fusion.7
  11.5 0.1 collective-permute-start.6
  11.6 2.1 %collective-permute-start.7 = (bf16[256,512]{1,0:T(8,128)(2,1)S(1)}, bf16[256,512]{1,0:T(8,128)(2,1)S(1)}, u32[]{:S(2)}, u32[]{:S(2)}) collective-permute-start(bf16[256,512]{1,0:T(8,128)(2,1)S(1)} %get-tuple-element.6), channel_id=1, source_target_pairs={{0,8},{4,12},{8,0},{12,4},{16,24},{20,28},{24,16},{28,20},{1,9},{5... | collective-permute-start | bytes 786440 | tf_op jit(solution)/shard_map/ppermute | solution.py:19
  13.6 1.5 %collective-permute-start.9 = (bf16[256,512]{1,0:T(8,128)(2,1)S(1)}, bf16[256,512]{1,0:T(8,128)(2,1)S(1)}, u32[]{:S(2)}, u32[]{:S(2)}) collective-permute-start(bf16[256,512]{1,0:T(8,128)(2,1)S(1)} %get-tuple-element.6), channel_id=1, source_target_pairs={{0,16},{4,20},{8,24},{12,28},{16,0},{20,4},{24,8},{28,12},{1,17},{... | collective-permute-start | bytes 786440 | tf_op jit(solution)/shard_map/ppermute | solution.py:19
  15.1 0.0 collective-permute-start.11
  15.2 3.0 %collective-permute-start.4 = (bf16[256,512]{1,0:T(8,128)(2,1)S(1)}, bf16[256,512]{1,0:T(8,128)(2,1)S(1)}, u32[]{:S(2)}, u32[]{:S(2)}) collective-permute-start(bf16[256,512]{1,0:T(8,128)(2,1)S(1)} %get-tuple-element.6), channel_id=1, source_target_pairs={{0,2},{1,3},{2,0},{3,1},{4,6},{5,7},{6,4},{7,5},{8,10},{9,11},{10,... | collective-permute-start | bytes 786440 | tf_op jit(solution)/shard_map/ppermute | solution.py:19
  18.2 0.0 collective-permute-done.6
  18.2 1.6 %collective-permute-start.3 = (bf16[256,512]{1,0:T(8,128)(2,1)S(1)}, bf16[256,512]{1,0:T(8,128)(2,1)S(1)}, u32[]{:S(2)}, u32[]{:S(2)}) collective-permute-start(bf16[256,512]{1,0:T(8,128)(2,1)S(1)} %get-tuple-element.6), channel_id=1, source_target_pairs={{0,1},{1,0},{2,3},{3,2},{4,5},{5,4},{6,7},{7,6},{8,9},{9,8},{10,11... | collective-permute-start | bytes 786440 | tf_op jit(solution)/shard_map/ppermute | solution.py:19
  19.8 0.1 broadcast_in_dim.20
  19.9 0.9 %collective-permute-done.7 = bf16[256,512]{1,0:T(8,128)(2,1)S(1)} collective-permute-done((bf16[256,512]{1,0:T(8,128)(2,1)S(1)}, bf16[256,512]{1,0:T(8,128)(2,1)S(1)}, u32[]{:S(2)}, u32[]{:S(2)}) %collective-permute-start.7) | collective-permute-done | bytes 262176 | tf_op jit(solution)/shard_map/ppermute | solution.py:19
  20.8 0.0 collective-permute-start.8
  20.8 6.8 %collective-permute-done.9 = bf16[256,512]{1,0:T(8,128)(2,1)S(1)} collective-permute-done((bf16[256,512]{1,0:T(8,128)(2,1)S(1)}, bf16[256,512]{1,0:T(8,128)(2,1)S(1)}, u32[]{:S(2)}, u32[]{:S(2)}) %collective-permute-start.9) | collective-permute-done | bytes 262176 | tf_op jit(solution)/shard_map/ppermute | solution.py:19
  27.6 0.0 collective-permute-start.10
  27.6 0.0 collective-permute-done.11
  27.6 0.5 %collective-permute-start.12 = (bf16[256,512]{1,0:T(8,128)(2,1)S(1)}, bf16[256,512]{1,0:T(8,128)(2,1)S(1)}, u32[]{:S(2)}, u32[]{:S(2)}) collective-permute-start(bf16[256,512]{1,0:T(8,128)(2,1)S(1)} %collective-permute-done.11), channel_id=1, source_target_pairs={{0,4},{4,0},{8,12},{12,8},{16,20},{20,16},{24,28},{28,24},{1,5},{5... | collective-permute-start | bytes 786440 | tf_op jit(solution)/shard_map/ppermute | solution.py:19
  28.1 1.9 %collective-permute-done.4 = bf16[256,512]{1,0:T(8,128)(2,1)S(1)} collective-permute-done((bf16[256,512]{1,0:T(8,128)(2,1)S(1)}, bf16[256,512]{1,0:T(8,128)(2,1)S(1)}, u32[]{:S(2)}, u32[]{:S(2)}) %collective-permute-start.4) | collective-permute-done | bytes 262176 | tf_op jit(solution)/shard_map/ppermute | solution.py:19
  30.0 0.6 %collective-permute-start.5 = (bf16[256,512]{1,0:T(8,128)(2,1)S(1)}, bf16[256,512]{1,0:T(8,128)(2,1)S(1)}, u32[]{:S(2)}, u32[]{:S(2)}) collective-permute-start(bf16[256,512]{1,0:T(8,128)(2,1)S(1)} %collective-permute-done.4), channel_id=1, source_target_pairs={{0,1},{1,0},{2,3},{3,2},{4,5},{5,4},{6,7},{7,6},{8,9},{9,8},{10,11... | collective-permute-start | bytes 786440 | tf_op jit(solution)/shard_map/ppermute | solution.py:19
  30.6 1.0 %constant_dynamic-update-slice_fusion.6 = bf16[2048,512]{1,0:T(8,128)(2,1)S(1)} fusion(bf16[2048,512]{1,0:T(8,128)(2,1)S(1)} %get-tuple-element.5, bf16[256,512]{1,0:T(8,128)(2,1)} %collective-permute-done.6, s32[]{:T(128)S(6)} %select_n.41), kind=kLoop, calls=%fused_computation.11 | loop fusion | bytes 524292 | tf_op jit(solution)/shard_map/dynamic_update_slice | solution.py:35
  31.6 0.0 collective-permute-done.3
  31.7 0.0 collective-permute-done.8
  31.8 0.0 collective-permute-done.10
  31.9 0.0 collective-permute-done.12
  31.9 5.3 %collective-permute-done.5 = bf16[256,512]{1,0:T(8,128)(2,1)S(1)} collective-permute-done((bf16[256,512]{1,0:T(8,128)(2,1)S(1)}, bf16[256,512]{1,0:T(8,128)(2,1)S(1)}, u32[]{:S(2)}, u32[]{:S(2)}) %collective-permute-start.5) | collective-permute-done | bytes 262176 | tf_op jit(solution)/shard_map/ppermute | solution.py:19
  37.2 0.7 %fusion.1 = (f32[512]{0:T(512)S(1)}, f32[256,512]{1,0:T(8,128)S(1)}) fusion(f32[512]{0:T(512)S(1)} %bitcast.9, bf16[256,2048]{1,0:T(8,128)(2,1)S(1)} %constant_dynamic-update-slice_fusion.8, bf16[2048,512]{1,0:T(8,128)(2,1)S(1)} %constant_dynamic-update-slice_fusion), kind=kOutput, calls=%fused_computation.21 | convolution fusion | flops 537263616 | bytes 3674112 | tf_op jit(solution)/shard_map/dot_general | solution.py:77
  37.9 0.1 collective-permute-start.13
  38.0 1.1 %collective-permute-done.13 = f32[512]{0:T(512)S(1)} collective-permute-done((f32[512]{0:T(512)S(1)}, f32[512]{0:T(512)S(1)}, u32[]{:S(2)}, u32[]{:S(2)}) %collective-permute-start.13) | collective-permute-done | bytes 2080 | tf_op jit(solution)/shard_map/ppermute | solution.py:19
  39.2 1.5 %collective-permute-start.14 = (f32[512]{0:T(512)S(1)}, f32[512]{0:T(512)S(1)}, u32[]{:S(2)}, u32[]{:S(2)}) collective-permute-start(f32[512]{0:T(512)S(1)} %add.69), channel_id=1, source_target_pairs={{0,8},{4,12},{8,0},{12,4},{16,24},{20,28},{24,16},{28,20},{1,9},{5... | collective-permute-start | bytes 6152 | tf_op jit(solution)/shard_map/ppermute | solution.py:19
  40.6 2.1 %collective-permute-done.14 = f32[512]{0:T(512)S(1)} collective-permute-done((f32[512]{0:T(512)S(1)}, f32[512]{0:T(512)S(1)}, u32[]{:S(2)}, u32[]{:S(2)}) %collective-permute-start.14) | collective-permute-done | bytes 2080 | tf_op jit(solution)/shard_map/ppermute | solution.py:19
  42.8 1.5 %collective-permute-start.15 = (f32[512]{0:T(512)S(1)}, f32[512]{0:T(512)S(1)}, u32[]{:S(2)}, u32[]{:S(2)}) collective-permute-start(f32[512]{0:T(512)S(1)} %add.70), channel_id=1, source_target_pairs={{0,16},{4,20},{8,24},{12,28},{16,0},{20,4},{24,8},{28,12},{1,17},{... | collective-permute-start | bytes 6152 | tf_op jit(solution)/shard_map/ppermute | solution.py:19
  44.3 2.1 %collective-permute-done.15 = f32[512]{0:T(512)S(1)} collective-permute-done((f32[512]{0:T(512)S(1)}, f32[512]{0:T(512)S(1)}, u32[]{:S(2)}, u32[]{:S(2)}) %collective-permute-start.15) | collective-permute-done | bytes 2080 | tf_op jit(solution)/shard_map/ppermute | solution.py:19
  46.4 0.9 %broadcast_multiply_fusion = f32[256,512]{1,0:T(8,128)} fusion(f32[256,512]{1,0:T(8,128)S(1)} %get-tuple-element.8, f32[512]{0:T(512)S(1)} %add_divide_fusion), kind=kLoop, calls=%fused_computation.4 | loop fusion | flops 131072 | bytes 1050624 | tf_op jit(solution)/shard_map/mul | solution.py:80
  (17 shorter events, 0.3 us)
Async XLA Ops:
  0.0 11.4 %copy-start = (f32[256,512]{1,0:T(8,128)S(1)}, f32[256,512]{1,0:T(8,128)}, u32[]{:S(2)}) copy-start(f32[256,512]{1,0:T(8,128)} %param.2) | copy-start | bytes 1572868
  1.9 1.3 %collective-permute-start = (f32[512]{0:T(512)S(1)}, f32[512]{0:T(512)S(1)}, u32[]{:S(2)}, u32[]{:S(2)}) collective-permute-start(f32[512]{0:T(512)S(1)} %multiply_reduce_fusion), channel_id=1, source_target_pairs={{0,4},{4,0},{8,12},{12,8},{16,20},{20,16},{24,28},{28,24},{1,5},{5... | collective-permute-start | bytes 6152 | tf_op jit(solution)/shard_map/ppermute | solution.py:19
  3.2 4.4 %collective-permute-start.1 = (f32[512]{0:T(512)S(1)}, f32[512]{0:T(512)S(1)}, u32[]{:S(2)}, u32[]{:S(2)}) collective-permute-start(f32[512]{0:T(512)S(1)} %add.54), channel_id=1, source_target_pairs={{0,8},{4,12},{8,0},{12,4},{16,24},{20,28},{24,16},{28,20},{1,9},{5... | collective-permute-start | bytes 6152 | tf_op jit(solution)/shard_map/ppermute | solution.py:19
  7.6 3.6 %collective-permute-start.2 = (f32[512]{0:T(512)S(1)}, f32[512]{0:T(512)S(1)}, u32[]{:S(2)}, u32[]{:S(2)}) collective-permute-start(f32[512]{0:T(512)S(1)} %add.55), channel_id=1, source_target_pairs={{0,16},{4,20},{8,24},{12,28},{16,0},{20,4},{24,8},{28,12},{1,17},{... | collective-permute-start | bytes 6152 | tf_op jit(solution)/shard_map/ppermute | solution.py:19
  11.5 6.7 %collective-permute-start.6 = (bf16[256,512]{1,0:T(8,128)(2,1)S(1)}, bf16[256,512]{1,0:T(8,128)(2,1)}, u32[]{:S(2)}, u32[]{:S(2)}) collective-permute-start(bf16[256,512]{1,0:T(8,128)(2,1)S(1)} %get-tuple-element.6), channel_id=1, source_target_pairs={{0,4},{4,0},{8,12},{12,8},{16,20},{20,16},{24,28},{28,24},{1,5},{5... | collective-permute-start | bytes 786440 | tf_op jit(solution)/shard_map/ppermute | solution.py:19
  11.6 9.2 %collective-permute-start.7 = (bf16[256,512]{1,0:T(8,128)(2,1)S(1)}, bf16[256,512]{1,0:T(8,128)(2,1)S(1)}, u32[]{:S(2)}, u32[]{:S(2)}) collective-permute-start(bf16[256,512]{1,0:T(8,128)(2,1)S(1)} %get-tuple-element.6), channel_id=1, source_target_pairs={{0,8},{4,12},{8,0},{12,4},{16,24},{20,28},{24,16},{28,20},{1,9},{5... | collective-permute-start | bytes 786440 | tf_op jit(solution)/shard_map/ppermute | solution.py:19
  13.6 14.0 %collective-permute-start.9 = (bf16[256,512]{1,0:T(8,128)(2,1)S(1)}, bf16[256,512]{1,0:T(8,128)(2,1)S(1)}, u32[]{:S(2)}, u32[]{:S(2)}) collective-permute-start(bf16[256,512]{1,0:T(8,128)(2,1)S(1)} %get-tuple-element.6), channel_id=1, source_target_pairs={{0,16},{4,20},{8,24},{12,28},{16,0},{20,4},{24,8},{28,12},{1,17},{... | collective-permute-start | bytes 786440 | tf_op jit(solution)/shard_map/ppermute | solution.py:19
  15.1 12.5 %collective-permute-start.11 = (bf16[256,512]{1,0:T(8,128)(2,1)S(1)}, bf16[256,512]{1,0:T(8,128)(2,1)S(1)}, u32[]{:S(2)}, u32[]{:S(2)}) collective-permute-start(bf16[256,512]{1,0:T(8,128)(2,1)S(1)} %get-tuple-element.6), channel_id=1, source_target_pairs={{0,24},{4,28},{8,16},{12,20},{16,8},{20,12},{24,0},{28,4},{1,25},{... | collective-permute-start | bytes 786440 | tf_op jit(solution)/shard_map/ppermute | solution.py:19
  15.2 14.8 %collective-permute-start.4 = (bf16[256,512]{1,0:T(8,128)(2,1)S(1)}, bf16[256,512]{1,0:T(8,128)(2,1)S(1)}, u32[]{:S(2)}, u32[]{:S(2)}) collective-permute-start(bf16[256,512]{1,0:T(8,128)(2,1)S(1)} %get-tuple-element.6), channel_id=1, source_target_pairs={{0,2},{1,3},{2,0},{3,1},{4,6},{5,7},{6,4},{7,5},{8,10},{9,11},{10,... | collective-permute-start | bytes 786440 | tf_op jit(solution)/shard_map/ppermute | solution.py:19
  18.2 13.4 %collective-permute-start.3 = (bf16[256,512]{1,0:T(8,128)(2,1)S(1)}, bf16[256,512]{1,0:T(8,128)(2,1)S(1)}, u32[]{:S(2)}, u32[]{:S(2)}) collective-permute-start(bf16[256,512]{1,0:T(8,128)(2,1)S(1)} %get-tuple-element.6), channel_id=1, source_target_pairs={{0,1},{1,0},{2,3},{3,2},{4,5},{5,4},{6,7},{7,6},{8,9},{9,8},{10,11... | collective-permute-start | bytes 786440 | tf_op jit(solution)/shard_map/ppermute | solution.py:19
  20.8 10.9 %collective-permute-start.8 = (bf16[256,512]{1,0:T(8,128)(2,1)S(1)}, bf16[256,512]{1,0:T(8,128)(2,1)S(1)}, u32[]{:S(2)}, u32[]{:S(2)}) collective-permute-start(bf16[256,512]{1,0:T(8,128)(2,1)S(1)} %collective-permute-done.7), channel_id=1, source_target_pairs={{0,4},{4,0},{8,12},{12,8},{16,20},{20,16},{24,28},{28,24},{1,5},{5... | collective-permute-start | bytes 786440 | tf_op jit(solution)/shard_map/ppermute | solution.py:19
  27.6 4.2 %collective-permute-start.10 = (bf16[256,512]{1,0:T(8,128)(2,1)S(1)}, bf16[256,512]{1,0:T(8,128)(2,1)S(1)}, u32[]{:S(2)}, u32[]{:S(2)}) collective-permute-start(bf16[256,512]{1,0:T(8,128)(2,1)S(1)} %collective-permute-done.9), channel_id=1, source_target_pairs={{0,4},{4,0},{8,12},{12,8},{16,20},{20,16},{24,28},{28,24},{1,5},{5... | collective-permute-start | bytes 786440 | tf_op jit(solution)/shard_map/ppermute | solution.py:19
  27.6 4.2 %collective-permute-start.12 = (bf16[256,512]{1,0:T(8,128)(2,1)S(1)}, bf16[256,512]{1,0:T(8,128)(2,1)S(1)}, u32[]{:S(2)}, u32[]{:S(2)}) collective-permute-start(bf16[256,512]{1,0:T(8,128)(2,1)S(1)} %collective-permute-done.11), channel_id=1, source_target_pairs={{0,4},{4,0},{8,12},{12,8},{16,20},{20,16},{24,28},{28,24},{1,5},{5... | collective-permute-start | bytes 786440 | tf_op jit(solution)/shard_map/ppermute | solution.py:19
  30.0 7.2 %collective-permute-start.5 = (bf16[256,512]{1,0:T(8,128)(2,1)S(1)}, bf16[256,512]{1,0:T(8,128)(2,1)S(1)}, u32[]{:S(2)}, u32[]{:S(2)}) collective-permute-start(bf16[256,512]{1,0:T(8,128)(2,1)S(1)} %collective-permute-done.4), channel_id=1, source_target_pairs={{0,1},{1,0},{2,3},{3,2},{4,5},{5,4},{6,7},{7,6},{8,9},{9,8},{10,11... | collective-permute-start | bytes 786440 | tf_op jit(solution)/shard_map/ppermute | solution.py:19
  37.9 1.2 %collective-permute-start.13 = (f32[512]{0:T(512)S(1)}, f32[512]{0:T(512)S(1)}, u32[]{:S(2)}, u32[]{:S(2)}) collective-permute-start(f32[512]{0:T(512)S(1)} %get-tuple-element.7), channel_id=1, source_target_pairs={{0,4},{4,0},{8,12},{12,8},{16,20},{20,16},{24,28},{28,24},{1,5},{5... | collective-permute-start | bytes 6152 | tf_op jit(solution)/shard_map/ppermute | solution.py:19
  39.2 3.6 %collective-permute-start.14 = (f32[512]{0:T(512)S(1)}, f32[512]{0:T(512)S(1)}, u32[]{:S(2)}, u32[]{:S(2)}) collective-permute-start(f32[512]{0:T(512)S(1)} %add.69), channel_id=1, source_target_pairs={{0,8},{4,12},{8,0},{12,4},{16,24},{20,28},{24,16},{28,20},{1,9},{5... | collective-permute-start | bytes 6152 | tf_op jit(solution)/shard_map/ppermute | solution.py:19
  42.8 3.6 %collective-permute-start.15 = (f32[512]{0:T(512)S(1)}, f32[512]{0:T(512)S(1)}, u32[]{:S(2)}, u32[]{:S(2)}) collective-permute-start(f32[512]{0:T(512)S(1)} %add.70), channel_id=1, source_target_pairs={{0,16},{4,20},{8,24},{12,28},{16,0},{20,4},{24,8},{28,12},{1,17},{... | collective-permute-start | bytes 6152 | tf_op jit(solution)/shard_map/ppermute | solution.py:19

commit v3 on v2

--- a/solution.py
+++ b/solution.py
@@ -66,14 +66,34 @@
     return join_rows(got)
 
 
+def after(x, other):
+    return lax.optimization_barrier((x, other))[0]
+
+
+def gather(x):
+    first = x.shape[0] * 5 // 8 // 16 * 16
+    far = [swap(x[:first], "col", 2), swap(x[first:], "col", 2)]
+    rows = {0: x, 2: swap(x, "row", 2), 4: swap(x, "row", 4)}
+    rows[6] = swap(after(x, far[0]), "row", 6)
+    near = swap(x, "col", 1)
+    rows[1] = swap(after(x, near), "row", 1)
+    passed = [swap(after(far[0], rows[2]), "col", 1), swap(far[1], "col", 1)]
+    for mask in (2, 4, 6):
+        rows[mask + 1] = swap(rows[mask], "row", 1)
+    columns = [x, near, jnp.concatenate(far), jnp.concatenate(passed)]
+    return join_columns(columns), join_rows(rows)
+
+
 def shards(similarity, pattern):
     cells = spread(pattern)
     total_rows = similarity.shape[0] * lax.axis_size("row")
     held = similarity * cells
     scale = total_rows / total(jnp.sum(held, axis=0), "row")
     operand = scaled(held, scale)
-
-    left, right = gather_columns(operand), gather_rows(operand)
+    if (lax.axis_size("row"), lax.axis_size("col")) == (8, 4):
+        left, right = gather(operand)
+    else:
+        left, right = gather_columns(operand), gather_rows(operand)
     expanded = jnp.dot(left, right, preferred_element_type=jnp.float32) * cells
     inflated = expanded * expanded
     sums = total(jnp.sum(inflated, axis=0), "row")

time: 47.4 us -> 44.5 us (0.939)
  waiting for transfers between devices: 24.1 us -> 17.9 us
  starting transfers between devices: 17.8 us -> 22.1 us
  local copies, waits for them, and re-layouts: 1.55 us -> 0.57 us
    ppermute x16 -> x18, waiting for transfers between devices: 24.1 us -> 17.9 us  [swap(): return lax.ppermute(x, axis, [(i, i ^ mask) for i in range(size)])]
    ppermute x16 -> x18, starting transfers between devices: 17.8 us -> 22.1 us  [swap(): return lax.ppermute(x, axis, [(i, i ^ mask) for i in range(size)])]
    dynamic_update_slice x7, local copies, waits for them, and re-layouts: 1.12 us -> 0.17 us  [join_rows(): lax.dynamic_update_slice(whole, blocks[mask], ((me ^ mask) * depth, 0))]
  transfers between devices with their start and end apart: 16 -> 18, of which waited for: 10 -> 10; matrix products, arithmetic and copies ran while one was open for 3% -> 1% of each run, Pallas kernels for 0% -> 0%
where the time goes in v3:
time: 44.5 us; the launch traced here: 44.4 us
  starting transfers between devices  22.1 us (50%)
  waiting for transfers between devices  17.9 us (40%)
  other arithmetic  2.83 us (6%)
  matrix products  0.72 us (2%)
  local copies, waits for them, and re-layouts  0.57 us (1%)
    ppermute x18, starting transfers between devices, swap(): return lax.ppermute(x, axis, [(i, i ^ mask) for i in range(size)])  22.1 us
    ppermute x18, waiting for transfers between devices, swap(): return lax.ppermute(x, axis, [(i, i ^ mask) for i in range(size)])  17.9 us
    reduce_sum x1, other arithmetic, shards(): scale = total_rows / total(jnp.sum(held, axis=0), 'row')  1.1 us
  transfers between devices with their start and end apart: 18, of which 10 were waited for; matrix products, arithmetic and copies ran while one was open for 1% of the time, Pallas kernels for 0%

profile of v3, /device:TPU:0, one launch (start us, length us, event | category | flops | bytes accessed | tf_op | source)
XLA Modules:
  0.0 44.4 jit_solution(14244745993006692419)
XLA Ops:
  0.0 0.0 copy-start
  0.0 0.7 %convert_bitcast_fusion = f32[2]{0:T(128)S(1)} fusion(s32[1,2]{1,0:T(1,128)} %param.3), kind=kLoop, calls=%fused_computation.20 | loop fusion | flops 2 | bytes 16 | tf_op jit(solution)/shard_map/broadcast_in_dim | solution.py:12
  0.7 0.1 broadcast_bitcast_fusion
  0.8 1.1 %multiply_reduce_fusion = f32[512]{0:T(512)S(1)} fusion(f32[256,512]{1,0:T(8,128)} %param.2, f32[512]{0:T(512)S(1)} %bitcast.7), kind=kLoop, calls=%fused_computation.3 | loop fusion | flops 261632 | bytes 528384 | tf_op jit(solution)/shard_map/reduce_sum | solution.py:91
  1.9 0.5 %collective-permute-start = (f32[512]{0:T(512)S(1)}, f32[512]{0:T(512)S(1)}, u32[]{:S(2)}, u32[]{:S(2)}) collective-permute-start(f32[512]{0:T(512)S(1)} %multiply_reduce_fusion), channel_id=1, source_target_pairs={{0,4},{4,0},{8,12},{12,8},{16,20},{20,16},{24,28},{28,24},{1,5},{5... | collective-permute-start | bytes 6152 | tf_op jit(solution)/shard_map/ppermute | solution.py:19
  2.4 0.8 %collective-permute-done = f32[512]{0:T(512)S(1)} collective-permute-done((f32[512]{0:T(512)S(1)}, f32[512]{0:T(512)S(1)}, u32[]{:S(2)}, u32[]{:S(2)}) %collective-permute-start) | collective-permute-done | bytes 2080 | tf_op jit(solution)/shard_map/ppermute | solution.py:19
  3.2 2.8 %collective-permute-start.1 = (f32[512]{0:T(512)S(1)}, f32[512]{0:T(512)S(1)}, u32[]{:S(2)}, u32[]{:S(2)}) collective-permute-start(f32[512]{0:T(512)S(1)} %add.54), channel_id=1, source_target_pairs={{0,8},{4,12},{8,0},{12,4},{16,24},{20,28},{24,16},{28,20},{1,9},{5... | collective-permute-start | bytes 6152 | tf_op jit(solution)/shard_map/ppermute | solution.py:19
  6.1 1.6 %collective-permute-done.1 = f32[512]{0:T(512)S(1)} collective-permute-done((f32[512]{0:T(512)S(1)}, f32[512]{0:T(512)S(1)}, u32[]{:S(2)}, u32[]{:S(2)}) %collective-permute-start.1) | collective-permute-done | bytes 2080 | tf_op jit(solution)/shard_map/ppermute | solution.py:19
  7.6 2.1 %collective-permute-start.2 = (f32[512]{0:T(512)S(1)}, f32[512]{0:T(512)S(1)}, u32[]{:S(2)}, u32[]{:S(2)}) collective-permute-start(f32[512]{0:T(512)S(1)} %add.55), channel_id=1, source_target_pairs={{0,16},{4,20},{8,24},{12,28},{16,0},{20,4},{24,8},{28,12},{1,17},{... | collective-permute-start | bytes 6152 | tf_op jit(solution)/shard_map/ppermute | solution.py:19
  9.7 1.6 %collective-permute-done.2 = f32[512]{0:T(512)S(1)} collective-permute-done((f32[512]{0:T(512)S(1)}, f32[512]{0:T(512)S(1)}, u32[]{:S(2)}, u32[]{:S(2)}) %collective-permute-start.2) | collective-permute-done | bytes 2080 | tf_op jit(solution)/shard_map/ppermute | solution.py:19
  11.2 0.1 broadcast_in_dim.25
  11.4 0.0 copy-done
  11.4 0.1 constant_dynamic-update-slice_fusion.7
  11.5 3.2 %collective-permute-start.4 = (bf16[160,512]{1,0:T(8,128)(2,1)S(1)}, bf16[160,512]{1,0:T(8,128)(2,1)S(1)}, u32[]{:S(2)}, u32[]{:S(2)}) collective-permute-start(bf16[160,512]{1,0:T(8,128)(2,1)S(1)} %slice.8), channel_id=1, source_target_pairs={{0,2},{1,3},{2,0},{3,1},{4,6},{5,7},{6,4},{7,5},{8,10},{9,11},{10,... | collective-permute-start | bytes 491528 | tf_op jit(solution)/shard_map/ppermute | solution.py:19
  14.7 1.6 %collective-permute-start.3 = (bf16[256,512]{1,0:T(8,128)(2,1)S(1)}, bf16[256,512]{1,0:T(8,128)(2,1)S(1)}, u32[]{:S(2)}, u32[]{:S(2)}) collective-permute-start(bf16[256,512]{1,0:T(8,128)(2,1)S(1)} %get-tuple-element.10), channel_id=1, source_target_pairs={{0,1},{1,0},{2,3},{3,2},{4,5},{5,4},{6,7},{7,6},{8,9},{9,8},{10,11... | collective-permute-start | bytes 786440 | tf_op jit(solution)/shard_map/ppermute | solution.py:19
  16.2 1.5 %collective-permute-start.6 = (bf16[256,512]{1,0:T(8,128)(2,1)S(1)}, bf16[256,512]{1,0:T(8,128)(2,1)S(1)}, u32[]{:S(2)}, u32[]{:S(2)}) collective-permute-start(bf16[256,512]{1,0:T(8,128)(2,1)S(1)} %get-tuple-element.10), channel_id=1, source_target_pairs={{0,8},{4,12},{8,0},{12,4},{16,24},{20,28},{24,16},{28,20},{1,9},{5... | collective-permute-start | bytes 786440 | tf_op jit(solution)/shard_map/ppermute | solution.py:19
  17.7 1.5 %collective-permute-start.11 = (bf16[256,512]{1,0:T(8,128)(2,1)S(1)}, bf16[256,512]{1,0:T(8,128)(2,1)S(1)}, u32[]{:S(2)}, u32[]{:S(2)}) collective-permute-start(bf16[256,512]{1,0:T(8,128)(2,1)S(1)} %get-tuple-element.10), channel_id=1, source_target_pairs={{0,16},{4,20},{8,24},{12,28},{16,0},{20,4},{24,8},{28,12},{1,17},{... | collective-permute-start | bytes 786440 | tf_op jit(solution)/shard_map/ppermute | solution.py:19
  19.3 0.4 collective-permute-start.5
  19.7 0.2 collective-permute-done.4
  19.9 5.2 %collective-permute-start.13 = (bf16[256,512]{1,0:T(8,128)(2,1)S(1)}, bf16[256,512]{1,0:T(8,128)(2,1)S(1)}, u32[]{:S(2)}, u32[]{:S(2)}) collective-permute-start(bf16[256,512]{1,0:T(8,128)(2,1)S(1)} %get-tuple-element.10), channel_id=1, source_target_pairs={{0,24},{4,28},{8,16},{12,20},{16,8},{20,12},{24,0},{28,4},{1,25},{... | collective-permute-start | bytes 786440 | tf_op jit(solution)/shard_map/ppermute | solution.py:19
  25.0 0.1 broadcast_in_dim.20
  25.2 0.8 %collective-permute-done.5 = bf16[96,512]{1,0:T(8,128)(2,1)S(1)} collective-permute-done((bf16[96,512]{1,0:T(8,128)(2,1)S(1)}, bf16[96,512]{1,0:T(8,128)(2,1)S(1)}, u32[]{:S(2)}, u32[]{:S(2)}) %collective-permute-start.5) | collective-permute-done | bytes 98336 | tf_op jit(solution)/shard_map/ppermute | solution.py:19
  26.0 0.4 collective-permute-start.8
  26.4 0.0 collective-permute-done.3
  26.4 0.0 collective-permute-start.9
  26.4 0.0 collective-permute-done.6
  26.4 1.7 %collective-permute-start.7 = (bf16[160,512]{1,0:T(8,128)(2,1)S(1)}, bf16[160,512]{1,0:T(8,128)(2,1)S(1)}, u32[]{:S(2)}, u32[]{:S(2)}) collective-permute-start(bf16[160,512]{1,0:T(8,128)(2,1)S(1)} %collective-permute-done.4), channel_id=1, source_target_pairs={{0,1},{1,0},{2,3},{3,2},{4,5},{5,4},{6,7},{7,6},{8,9},{9,8},{10,11... | collective-permute-start | bytes 491528 | tf_op jit(solution)/shard_map/ppermute | solution.py:19
  28.2 3.5 %collective-permute-done.8 = bf16[96,512]{1,0:T(8,128)(2,1)S(1)} collective-permute-done((bf16[96,512]{1,0:T(8,128)(2,1)S(1)}, bf16[96,512]{1,0:T(8,128)(2,1)S(1)}, u32[]{:S(2)}, u32[]{:S(2)}) %collective-permute-start.8) | collective-permute-done | bytes 98336 | tf_op jit(solution)/shard_map/ppermute | solution.py:19
  31.7 0.0 collective-permute-start.10
  31.7 0.0 collective-permute-done.11
  31.7 0.5 %collective-permute-start.12 = (bf16[256,512]{1,0:T(8,128)(2,1)S(1)}, bf16[256,512]{1,0:T(8,128)(2,1)S(1)}, u32[]{:S(2)}, u32[]{:S(2)}) collective-permute-start(bf16[256,512]{1,0:T(8,128)(2,1)S(1)} %collective-permute-done.11), channel_id=1, source_target_pairs={{0,4},{4,0},{8,12},{12,8},{16,20},{20,16},{24,28},{28,24},{1,5},{5... | collective-permute-start | bytes 786440 | tf_op jit(solution)/shard_map/ppermute | solution.py:19
  32.2 0.0 collective-permute-done.13
  32.2 0.1 collective-permute-start.14
  32.2 1.8 %collective-permute-done.7 = bf16[160,512]{1,0:T(8,128)(2,1)S(1)} collective-permute-done((bf16[160,512]{1,0:T(8,128)(2,1)S(1)}, bf16[160,512]{1,0:T(8,128)(2,1)S(1)}, u32[]{:S(2)}, u32[]{:S(2)}) %collective-permute-start.7) | collective-permute-done | bytes 163872 | tf_op jit(solution)/shard_map/ppermute | solution.py:19
  34.1 0.0 collective-permute-done.9
  34.2 0.0 collective-permute-done.10
  34.3 0.0 collective-permute-done.12
  34.3 0.0 collective-permute-done.14
  34.4 0.7 %fusion.1 = (f32[512]{0:T(512)S(1)}, f32[256,512]{1,0:T(8,128)S(1)}) fusion(f32[512]{0:T(512)S(1)} %bitcast.9, bf16[256,2048]{1,0:T(8,128)(2,1)S(1)} %maximum_dynamic-update-slice_fusion.1, bf16[2048,512]{1,0:T(8,128)(2,1)S(1)} %constant_dynamic-update-slice_fusion), kind=kOutput, calls=%fused_computation.21 | convolution fusion | flops 537263616 | bytes 3674112 | tf_op jit(solution)/shard_map/dot_general | solution.py:97
  35.1 0.1 collective-permute-start.15
  35.2 1.1 %collective-permute-done.15 = f32[512]{0:T(512)S(1)} collective-permute-done((f32[512]{0:T(512)S(1)}, f32[512]{0:T(512)S(1)}, u32[]{:S(2)}, u32[]{:S(2)}) %collective-permute-start.15) | collective-permute-done | bytes 2080 | tf_op jit(solution)/shard_map/ppermute | solution.py:19
  36.3 0.3 collective-permute-start.16
  36.7 3.2 %collective-permute-done.16 = f32[512]{0:T(512)S(1)} collective-permute-done((f32[512]{0:T(512)S(1)}, f32[512]{0:T(512)S(1)}, u32[]{:S(2)}, u32[]{:S(2)}) %collective-permute-start.16) | collective-permute-done | bytes 2080 | tf_op jit(solution)/shard_map/ppermute | solution.py:19
  39.9 0.4 collective-permute-start.17
  40.3 3.2 %collective-permute-done.17 = f32[512]{0:T(512)S(1)} collective-permute-done((f32[512]{0:T(512)S(1)}, f32[512]{0:T(512)S(1)}, u32[]{:S(2)}, u32[]{:S(2)}) %collective-permute-start.17) | collective-permute-done | bytes 2080 | tf_op jit(solution)/shard_map/ppermute | solution.py:19
  43.5 0.9 %broadcast_multiply_fusion = f32[256,512]{1,0:T(8,128)} fusion(f32[256,512]{1,0:T(8,128)S(1)} %get-tuple-element.14, f32[512]{0:T(512)S(1)} %add_divide_fusion), kind=kLoop, calls=%fused_computation.6 | loop fusion | flops 131072 | bytes 1050624 | tf_op jit(solution)/shard_map/mul | solution.py:100
  (20 shorter events, 0.3 us)
Async XLA Ops:
  0.0 11.4 %copy-start = (f32[256,512]{1,0:T(8,128)S(1)}, f32[256,512]{1,0:T(8,128)}, u32[]{:S(2)}) copy-start(f32[256,512]{1,0:T(8,128)} %param.2) | copy-start | bytes 1572868
  1.9 1.3 %collective-permute-start = (f32[512]{0:T(512)S(1)}, f32[512]{0:T(512)S(1)}, u32[]{:S(2)}, u32[]{:S(2)}) collective-permute-start(f32[512]{0:T(512)S(1)} %multiply_reduce_fusion), channel_id=1, source_target_pairs={{0,4},{4,0},{8,12},{12,8},{16,20},{20,16},{24,28},{28,24},{1,5},{5... | collective-permute-start | bytes 6152 | tf_op jit(solution)/shard_map/ppermute | solution.py:19
  3.2 4.4 %collective-permute-start.1 = (f32[512]{0:T(512)S(1)}, f32[512]{0:T(512)S(1)}, u32[]{:S(2)}, u32[]{:S(2)}) collective-permute-start(f32[512]{0:T(512)S(1)} %add.54), channel_id=1, source_target_pairs={{0,8},{4,12},{8,0},{12,4},{16,24},{20,28},{24,16},{28,20},{1,9},{5... | collective-permute-start | bytes 6152 | tf_op jit(solution)/shard_map/ppermute | solution.py:19
  7.6 3.6 %collective-permute-start.2 = (f32[512]{0:T(512)S(1)}, f32[512]{0:T(512)S(1)}, u32[]{:S(2)}, u32[]{:S(2)}) collective-permute-start(f32[512]{0:T(512)S(1)} %add.55), channel_id=1, source_target_pairs={{0,16},{4,20},{8,24},{12,28},{16,0},{20,4},{24,8},{28,12},{1,17},{... | collective-permute-start | bytes 6152 | tf_op jit(solution)/shard_map/ppermute | solution.py:19
  11.5 8.4 %collective-permute-start.4 = (bf16[160,512]{1,0:T(8,128)(2,1)S(1)}, bf16[160,512]{1,0:T(8,128)(2,1)S(1)}, u32[]{:S(2)}, u32[]{:S(2)}) collective-permute-start(bf16[160,512]{1,0:T(8,128)(2,1)S(1)} %slice.8), channel_id=1, source_target_pairs={{0,2},{1,3},{2,0},{3,1},{4,6},{5,7},{6,4},{7,5},{8,10},{9,11},{10,... | collective-permute-start | bytes 491528 | tf_op jit(solution)/shard_map/ppermute | solution.py:19
  14.7 11.7 %collective-permute-start.3 = (bf16[256,512]{1,0:T(8,128)(2,1)S(1)}, bf16[256,512]{1,0:T(8,128)(2,1)S(1)}, u32[]{:S(2)}, u32[]{:S(2)}) collective-permute-start(bf16[256,512]{1,0:T(8,128)(2,1)S(1)} %get-tuple-element.10), channel_id=1, source_target_pairs={{0,1},{1,0},{2,3},{3,2},{4,5},{5,4},{6,7},{7,6},{8,9},{9,8},{10,11... | collective-permute-start | bytes 786440 | tf_op jit(solution)/shard_map/ppermute | solution.py:19
  16.2 10.2 %collective-permute-start.6 = (bf16[256,512]{1,0:T(8,128)(2,1)S(1)}, bf16[256,512]{1,0:T(8,128)(2,1)S(1)}, u32[]{:S(2)}, u32[]{:S(2)}) collective-permute-start(bf16[256,512]{1,0:T(8,128)(2,1)S(1)} %get-tuple-element.10), channel_id=1, source_target_pairs={{0,8},{4,12},{8,0},{12,4},{16,24},{20,28},{24,16},{28,20},{1,9},{5... | collective-permute-start | bytes 786440 | tf_op jit(solution)/shard_map/ppermute | solution.py:19
  17.7 13.9 %collective-permute-start.11 = (bf16[256,512]{1,0:T(8,128)(2,1)S(1)}, bf16[256,512]{1,0:T(8,128)(2,1)S(1)}, u32[]{:S(2)}, u32[]{:S(2)}) collective-permute-start(bf16[256,512]{1,0:T(8,128)(2,1)S(1)} %get-tuple-element.10), channel_id=1, source_target_pairs={{0,16},{4,20},{8,24},{12,28},{16,0},{20,4},{24,8},{28,12},{1,17},{... | collective-permute-start | bytes 786440 | tf_op jit(solution)/shard_map/ppermute | solution.py:19
  19.3 6.7 %collective-permute-start.5 = (bf16[96,512]{1,0:T(8,128)(2,1)S(1)}, bf16[96,512]{1,0:T(8,128)(2,1)S(1)}, u32[]{:S(2)}, u32[]{:S(2)}) collective-permute-start(bf16[96,512]{1,0:T(8,128)(2,1)S(1)} %slice.9), channel_id=1, source_target_pairs={{0,2},{1,3},{2,0},{3,1},{4,6},{5,7},{6,4},{7,5},{8,10},{9,11},{10,... | collective-permute-start | bytes 294920 | tf_op jit(solution)/shard_map/ppermute | solution.py:19
  19.9 12.3 %collective-permute-start.13 = (bf16[256,512]{1,0:T(8,128)(2,1)S(1)}, bf16[256,512]{1,0:T(8,128)(2,1)S(1)}, u32[]{:S(2)}, u32[]{:S(2)}) collective-permute-start(bf16[256,512]{1,0:T(8,128)(2,1)S(1)} %get-tuple-element.10), channel_id=1, source_target_pairs={{0,24},{4,28},{8,16},{12,20},{16,8},{20,12},{24,0},{28,4},{1,25},{... | collective-permute-start | bytes 786440 | tf_op jit(solution)/shard_map/ppermute | solution.py:19
  26.0 5.7 %collective-permute-start.8 = (bf16[96,512]{1,0:T(8,128)(2,1)S(1)}, bf16[96,512]{1,0:T(8,128)(2,1)S(1)}, u32[]{:S(2)}, u32[]{:S(2)}) collective-permute-start(bf16[96,512]{1,0:T(8,128)(2,1)S(1)} %collective-permute-done.5), channel_id=1, source_target_pairs={{0,1},{1,0},{2,3},{3,2},{4,5},{5,4},{6,7},{7,6},{8,9},{9,8},{10,11... | collective-permute-start | bytes 294920 | tf_op jit(solution)/shard_map/ppermute | solution.py:19
  26.4 7.7 %collective-permute-start.9 = (bf16[256,512]{1,0:T(8,128)(2,1)S(1)}, bf16[256,512]{1,0:T(8,128)(2,1)S(1)}, u32[]{:S(2)}, u32[]{:S(2)}) collective-permute-start(bf16[256,512]{1,0:T(8,128)(2,1)S(1)} %get-tuple-element.10), channel_id=1, source_target_pairs={{0,4},{4,0},{8,12},{12,8},{16,20},{20,16},{24,28},{28,24},{1,5},{5... | collective-permute-start | bytes 786440 | tf_op jit(solution)/shard_map/ppermute | solution.py:19
  26.4 7.7 %collective-permute-start.7 = (bf16[160,512]{1,0:T(8,128)(2,1)S(1)}, bf16[160,512]{1,0:T(8,128)(2,1)S(1)}, u32[]{:S(2)}, u32[]{:S(2)}) collective-permute-start(bf16[160,512]{1,0:T(8,128)(2,1)S(1)} %collective-permute-done.4), channel_id=1, source_target_pairs={{0,1},{1,0},{2,3},{3,2},{4,5},{5,4},{6,7},{7,6},{8,9},{9,8},{10,11... | collective-permute-start | bytes 491528 | tf_op jit(solution)/shard_map/ppermute | solution.py:19
  31.7 2.5 %collective-permute-start.10 = (bf16[256,512]{1,0:T(8,128)(2,1)S(1)}, bf16[256,512]{1,0:T(8,128)(2,1)S(1)}, u32[]{:S(2)}, u32[]{:S(2)}) collective-permute-start(bf16[256,512]{1,0:T(8,128)(2,1)S(1)} %collective-permute-done.6), channel_id=1, source_target_pairs={{0,4},{4,0},{8,12},{12,8},{16,20},{20,16},{24,28},{28,24},{1,5},{5... | collective-permute-start | bytes 786440 | tf_op jit(solution)/shard_map/ppermute | solution.py:19
  31.7 2.6 %collective-permute-start.12 = (bf16[256,512]{1,0:T(8,128)(2,1)S(1)}, bf16[256,512]{1,0:T(8,128)(2,1)S(1)}, u32[]{:S(2)}, u32[]{:S(2)}) collective-permute-start(bf16[256,512]{1,0:T(8,128)(2,1)S(1)} %collective-permute-done.11), channel_id=1, source_target_pairs={{0,4},{4,0},{8,12},{12,8},{16,20},{20,16},{24,28},{28,24},{1,5},{5... | collective-permute-start | bytes 786440 | tf_op jit(solution)/shard_map/ppermute | solution.py:19
  32.2 2.2 %collective-permute-start.14 = (bf16[256,512]{1,0:T(8,128)(2,1)S(1)}, bf16[256,512]{1,0:T(8,128)(2,1)S(1)}, u32[]{:S(2)}, u32[]{:S(2)}) collective-permute-start(bf16[256,512]{1,0:T(8,128)(2,1)S(1)} %collective-permute-done.13), channel_id=1, source_target_pairs={{0,4},{4,0},{8,12},{12,8},{16,20},{20,16},{24,28},{28,24},{1,5},{5... | collective-permute-start | bytes 786440 | tf_op jit(solution)/shard_map/ppermute | solution.py:19
  35.1 1.2 %collective-permute-start.15 = (f32[512]{0:T(512)S(1)}, f32[512]{0:T(512)S(1)}, u32[]{:S(2)}, u32[]{:S(2)}) collective-permute-start(f32[512]{0:T(512)S(1)} %get-tuple-element.13), channel_id=1, source_target_pairs={{0,4},{4,0},{8,12},{12,8},{16,20},{20,16},{24,28},{28,24},{1,5},{5... | collective-permute-start | bytes 6152 | tf_op jit(solution)/shard_map/ppermute | solution.py:19
  36.3 3.6 %collective-permute-start.16 = (f32[512]{0:T(512)S(1)}, f32[512]{0:T(512)S(1)}, u32[]{:S(2)}, u32[]{:S(2)}) collective-permute-start(f32[512]{0:T(512)S(1)} %add.69), channel_id=1, source_target_pairs={{0,8},{4,12},{8,0},{12,4},{16,24},{20,28},{24,16},{28,20},{1,9},{5... | collective-permute-start | bytes 6152 | tf_op jit(solution)/shard_map/ppermute | solution.py:19
  39.9 3.6 %collective-permute-start.17 = (f32[512]{0:T(512)S(1)}, f32[512]{0:T(512)S(1)}, u32[]{:S(2)}, u32[]{:S(2)}) collective-permute-start(f32[512]{0:T(512)S(1)} %add.70), channel_id=1, source_target_pairs={{0,16},{4,20},{8,24},{12,28},{16,0},{20,4},{24,8},{28,12},{1,17},{... | collective-permute-start | bytes 6152 | tf_op jit(solution)/shard_map/ppermute | solution.py:19

commit v4 on v3

--- a/solution.py
+++ b/solution.py
@@ -72,12 +72,15 @@
 
 def gather(x):
     first = x.shape[0] * 5 // 8 // 16 * 16
-    far = [swap(x[:first], "col", 2), swap(x[first:], "col", 2)]
-    rows = {0: x, 2: swap(x, "row", 2), 4: swap(x, "row", 4)}
-    rows[6] = swap(after(x, far[0]), "row", 6)
+    rows = {0: x}
+    for mask in (2, 4, 6):
+        rows[mask] = swap(x, "row", mask)
     near = swap(x, "col", 1)
     rows[1] = swap(after(x, near), "row", 1)
-    passed = [swap(after(far[0], rows[2]), "col", 1), swap(far[1], "col", 1)]
+    far = [swap(x[:first], "col", 2)]
+    passed = [swap(far[0], "col", 1)]
+    far.append(swap(after(x, far[0])[first:], "col", 2))
+    passed.append(swap(after(far[1], rows[2]), "col", 1))
     for mask in (2, 4, 6):
         rows[mask + 1] = swap(rows[mask], "row", 1)
     columns = [x, near, jnp.concatenate(far), jnp.concatenate(passed)]

time: 44.5 us -> 41.9 us (0.942)
  waiting for transfers between devices: 17.9 us -> 12.7 us
  starting transfers between devices: 22.1 us -> 24.7 us
    ppermute x18, waiting for transfers between devices: 17.9 us -> 12.7 us  [swap(): return lax.ppermute(x, axis, [(i, i ^ mask) for i in range(size)])]
    ppermute x18, starting transfers between devices: 22.1 us -> 24.7 us  [swap(): return lax.ppermute(x, axis, [(i, i ^ mask) for i in range(size)])]
  transfers between devices with their start and end apart: 18 -> 18, of which waited for: 10 -> 11; matrix products, arithmetic and copies ran while one was open for 1% -> 1% of each run, Pallas kernels for 0% -> 0%
where the time goes in v4:
time: 41.9 us; the launch traced here: 41.8 us
  starting transfers between devices  24.7 us (59%)
  waiting for transfers between devices  12.7 us (30%)
  other arithmetic  2.83 us (7%)
  matrix products  0.72 us (2%)
  local copies, waits for them, and re-layouts  0.57 us (1%)
    ppermute x18, starting transfers between devices, swap(): return lax.ppermute(x, axis, [(i, i ^ mask) for i in range(size)])  24.7 us
    ppermute x18, waiting for transfers between devices, swap(): return lax.ppermute(x, axis, [(i, i ^ mask) for i in range(size)])  12.7 us
    reduce_sum x1, other arithmetic, shards(): scale = total_rows / total(jnp.sum(held, axis=0), 'row')  1.1 us
    mul x1, other arithmetic, shards(): return inflated * (total_rows / sums)[None, :]  0.87 us
  transfers between devices with their start and end apart: 18, of which 11 were waited for; matrix products, arithmetic and copies ran while one was open for 1% of the time, Pallas kernels for 0%

profile of v4, /device:TPU:0, one launch (start us, length us, event | category | flops | bytes accessed | tf_op | source)
XLA Modules:
  0.0 41.8 jit_solution(4300225286014766103)
XLA Ops:
  0.0 0.0 copy-start
  0.0 0.7 %convert_bitcast_fusion = f32[2]{0:T(128)S(1)} fusion(s32[1,2]{1,0:T(1,128)} %param.3), kind=kLoop, calls=%fused_computation.20 | loop fusion | flops 2 | bytes 16 | tf_op jit(solution)/shard_map/broadcast_in_dim | solution.py:12
  0.7 0.1 broadcast_bitcast_fusion
  0.8 1.1 %multiply_reduce_fusion = f32[512]{0:T(512)S(1)} fusion(f32[256,512]{1,0:T(8,128)} %param.2, f32[512]{0:T(512)S(1)} %bitcast.7), kind=kLoop, calls=%fused_computation.3 | loop fusion | flops 261632 | bytes 528384 | tf_op jit(solution)/shard_map/reduce_sum | solution.py:94
  1.9 0.5 %collective-permute-start = (f32[512]{0:T(512)S(1)}, f32[512]{0:T(512)S(1)}, u32[]{:S(2)}, u32[]{:S(2)}) collective-permute-start(f32[512]{0:T(512)S(1)} %multiply_reduce_fusion), channel_id=1, source_target_pairs={{0,4},{4,0},{8,12},{12,8},{16,20},{20,16},{24,28},{28,24},{1,5},{5... | collective-permute-start | bytes 6152 | tf_op jit(solution)/shard_map/ppermute | solution.py:19
  2.4 0.8 %collective-permute-done = f32[512]{0:T(512)S(1)} collective-permute-done((f32[512]{0:T(512)S(1)}, f32[512]{0:T(512)S(1)}, u32[]{:S(2)}, u32[]{:S(2)}) %collective-permute-start) | collective-permute-done | bytes 2080 | tf_op jit(solution)/shard_map/ppermute | solution.py:19
  3.2 2.8 %collective-permute-start.1 = (f32[512]{0:T(512)S(1)}, f32[512]{0:T(512)S(1)}, u32[]{:S(2)}, u32[]{:S(2)}) collective-permute-start(f32[512]{0:T(512)S(1)} %add.54), channel_id=1, source_target_pairs={{0,8},{4,12},{8,0},{12,4},{16,24},{20,28},{24,16},{28,20},{1,9},{5... | collective-permute-start | bytes 6152 | tf_op jit(solution)/shard_map/ppermute | solution.py:19
  6.1 1.6 %collective-permute-done.1 = f32[512]{0:T(512)S(1)} collective-permute-done((f32[512]{0:T(512)S(1)}, f32[512]{0:T(512)S(1)}, u32[]{:S(2)}, u32[]{:S(2)}) %collective-permute-start.1) | collective-permute-done | bytes 2080 | tf_op jit(solution)/shard_map/ppermute | solution.py:19
  7.6 2.1 %collective-permute-start.2 = (f32[512]{0:T(512)S(1)}, f32[512]{0:T(512)S(1)}, u32[]{:S(2)}, u32[]{:S(2)}) collective-permute-start(f32[512]{0:T(512)S(1)} %add.55), channel_id=1, source_target_pairs={{0,16},{4,20},{8,24},{12,28},{16,0},{20,4},{24,8},{28,12},{1,17},{... | collective-permute-start | bytes 6152 | tf_op jit(solution)/shard_map/ppermute | solution.py:19
  9.7 1.6 %collective-permute-done.2 = f32[512]{0:T(512)S(1)} collective-permute-done((f32[512]{0:T(512)S(1)}, f32[512]{0:T(512)S(1)}, u32[]{:S(2)}, u32[]{:S(2)}) %collective-permute-start.2) | collective-permute-done | bytes 2080 | tf_op jit(solution)/shard_map/ppermute | solution.py:19
  11.2 0.1 broadcast_in_dim.25
  11.4 0.0 copy-done
  11.4 0.1 constant_dynamic-update-slice_fusion.7
  11.5 3.2 %collective-permute-start.4 = (bf16[160,512]{1,0:T(8,128)(2,1)S(1)}, bf16[160,512]{1,0:T(8,128)(2,1)S(1)}, u32[]{:S(2)}, u32[]{:S(2)}) collective-permute-start(bf16[160,512]{1,0:T(8,128)(2,1)S(1)} %slice.8), channel_id=1, source_target_pairs={{0,2},{1,3},{2,0},{3,1},{4,6},{5,7},{6,4},{7,5},{8,10},{9,11},{10,... | collective-permute-start | bytes 491528 | tf_op jit(solution)/shard_map/ppermute | solution.py:19
  14.7 1.6 %collective-permute-start.3 = (bf16[256,512]{1,0:T(8,128)(2,1)S(1)}, bf16[256,512]{1,0:T(8,128)(2,1)S(1)}, u32[]{:S(2)}, u32[]{:S(2)}) collective-permute-start(bf16[256,512]{1,0:T(8,128)(2,1)S(1)} %get-tuple-element.10), channel_id=1, source_target_pairs={{0,1},{1,0},{2,3},{3,2},{4,5},{5,4},{6,7},{7,6},{8,9},{9,8},{10,11... | collective-permute-start | bytes 786440 | tf_op jit(solution)/shard_map/ppermute | solution.py:19
  16.2 1.5 %collective-permute-start.7 = (bf16[256,512]{1,0:T(8,128)(2,1)S(1)}, bf16[256,512]{1,0:T(8,128)(2,1)S(1)}, u32[]{:S(2)}, u32[]{:S(2)}) collective-permute-start(bf16[256,512]{1,0:T(8,128)(2,1)S(1)} %get-tuple-element.10), channel_id=1, source_target_pairs={{0,8},{4,12},{8,0},{12,4},{16,24},{20,28},{24,16},{28,20},{1,9},{5... | collective-permute-start | bytes 786440 | tf_op jit(solution)/shard_map/ppermute | solution.py:19
  17.7 1.5 %collective-permute-start.11 = (bf16[256,512]{1,0:T(8,128)(2,1)S(1)}, bf16[256,512]{1,0:T(8,128)(2,1)S(1)}, u32[]{:S(2)}, u32[]{:S(2)}) collective-permute-start(bf16[256,512]{1,0:T(8,128)(2,1)S(1)} %get-tuple-element.10), channel_id=1, source_target_pairs={{0,16},{4,20},{8,24},{12,28},{16,0},{20,4},{24,8},{28,12},{1,17},{... | collective-permute-start | bytes 786440 | tf_op jit(solution)/shard_map/ppermute | solution.py:19
  19.2 0.5 %collective-permute-start.13 = (bf16[256,512]{1,0:T(8,128)(2,1)S(1)}, bf16[256,512]{1,0:T(8,128)(2,1)S(1)}, u32[]{:S(2)}, u32[]{:S(2)}) collective-permute-start(bf16[256,512]{1,0:T(8,128)(2,1)S(1)} %get-tuple-element.10), channel_id=1, source_target_pairs={{0,24},{4,28},{8,16},{12,20},{16,8},{20,12},{24,0},{28,4},{1,25},{... | collective-permute-start | bytes 786440 | tf_op jit(solution)/shard_map/ppermute | solution.py:19
  19.7 0.1 collective-permute-done.4
  19.8 3.1 %collective-permute-start.5 = (bf16[96,512]{1,0:T(8,128)(2,1)S(1)}, bf16[96,512]{1,0:T(8,128)(2,1)S(1)}, u32[]{:S(2)}, u32[]{:S(2)}) collective-permute-start(bf16[96,512]{1,0:T(8,128)(2,1)S(1)} %slice.7), channel_id=1, source_target_pairs={{0,2},{1,3},{2,0},{3,1},{4,6},{5,7},{6,4},{7,5},{8,10},{9,11},{10,... | collective-permute-start | bytes 294920 | tf_op jit(solution)/shard_map/ppermute | solution.py:19
  22.9 0.1 broadcast_in_dim.20
  23.0 1.0 %collective-permute-done.3 = bf16[256,512]{1,0:T(8,128)(2,1)S(1)} collective-permute-done((bf16[256,512]{1,0:T(8,128)(2,1)S(1)}, bf16[256,512]{1,0:T(8,128)(2,1)S(1)}, u32[]{:S(2)}, u32[]{:S(2)}) %collective-permute-start.3) | collective-permute-done | bytes 262176 | tf_op jit(solution)/shard_map/ppermute | solution.py:19
  24.0 2.0 %collective-permute-start.6 = (bf16[160,512]{1,0:T(8,128)(2,1)S(1)}, bf16[160,512]{1,0:T(8,128)(2,1)S(1)}, u32[]{:S(2)}, u32[]{:S(2)}) collective-permute-start(bf16[160,512]{1,0:T(8,128)(2,1)S(1)} %collective-permute-done.4), channel_id=1, source_target_pairs={{0,1},{1,0},{2,3},{3,2},{4,5},{5,4},{6,7},{7,6},{8,9},{9,8},{10,11... | collective-permute-start | bytes 491528 | tf_op jit(solution)/shard_map/ppermute | solution.py:19
  26.0 0.0 collective-permute-done.7
  26.0 0.0 collective-permute-start.9
  26.0 0.0 collective-permute-done.5
  26.0 2.4 %collective-permute-start.8 = (bf16[96,512]{1,0:T(8,128)(2,1)S(1)}, bf16[96,512]{1,0:T(8,128)(2,1)S(1)}, u32[]{:S(2)}, u32[]{:S(2)}) collective-permute-start(bf16[96,512]{1,0:T(8,128)(2,1)S(1)} %collective-permute-done.5), channel_id=1, source_target_pairs={{0,1},{1,0},{2,3},{3,2},{4,5},{5,4},{6,7},{7,6},{8,9},{9,8},{10,11... | collective-permute-start | bytes 294920 | tf_op jit(solution)/shard_map/ppermute | solution.py:19
  28.4 0.1 collective-permute-done.11
  28.6 0.0 collective-permute-start.10
  28.6 0.0 collective-permute-done.13
  28.6 0.5 %collective-permute-start.12 = (bf16[256,512]{1,0:T(8,128)(2,1)S(1)}, bf16[256,512]{1,0:T(8,128)(2,1)S(1)}, u32[]{:S(2)}, u32[]{:S(2)}) collective-permute-start(bf16[256,512]{1,0:T(8,128)(2,1)S(1)} %collective-permute-done.11), channel_id=1, source_target_pairs={{0,4},{4,0},{8,12},{12,8},{16,20},{20,16},{24,28},{28,24},{1,5},{5... | collective-permute-start | bytes 786440 | tf_op jit(solution)/shard_map/ppermute | solution.py:19
  29.1 0.6 %collective-permute-done.6 = bf16[160,512]{1,0:T(8,128)(2,1)S(1)} collective-permute-done((bf16[160,512]{1,0:T(8,128)(2,1)S(1)}, bf16[160,512]{1,0:T(8,128)(2,1)S(1)}, u32[]{:S(2)}, u32[]{:S(2)}) %collective-permute-start.6) | collective-permute-done | bytes 163872 | tf_op jit(solution)/shard_map/ppermute | solution.py:19
  29.7 0.0 collective-permute-start.14
  29.7 1.7 %collective-permute-done.8 = bf16[96,512]{1,0:T(8,128)(2,1)S(1)} collective-permute-done((bf16[96,512]{1,0:T(8,128)(2,1)S(1)}, bf16[96,512]{1,0:T(8,128)(2,1)S(1)}, u32[]{:S(2)}, u32[]{:S(2)}) %collective-permute-start.8) | collective-permute-done | bytes 98336 | tf_op jit(solution)/shard_map/ppermute | solution.py:19
  31.5 0.0 collective-permute-done.9
  31.6 0.0 collective-permute-done.10
  31.6 0.0 collective-permute-done.12
  31.7 0.0 collective-permute-done.14
  31.8 0.7 %fusion.1 = (f32[512]{0:T(512)S(1)}, f32[256,512]{1,0:T(8,128)S(1)}) fusion(f32[512]{0:T(512)S(1)} %bitcast.9, bf16[256,2048]{1,0:T(8,128)(2,1)S(1)} %maximum_dynamic-update-slice_fusion.1, bf16[2048,512]{1,0:T(8,128)(2,1)S(1)} %constant_dynamic-update-slice_fusion), kind=kOutput, calls=%fused_computation.21 | convolution fusion | flops 537263616 | bytes 3674112 | tf_op jit(solution)/shard_map/dot_general | solution.py:100
  32.5 0.1 collective-permute-start.15
  32.6 1.1 %collective-permute-done.15 = f32[512]{0:T(512)S(1)} collective-permute-done((f32[512]{0:T(512)S(1)}, f32[512]{0:T(512)S(1)}, u32[]{:S(2)}, u32[]{:S(2)}) %collective-permute-start.15) | collective-permute-done | bytes 2080 | tf_op jit(solution)/shard_map/ppermute | solution.py:19
  33.7 1.5 %collective-permute-start.16 = (f32[512]{0:T(512)S(1)}, f32[512]{0:T(512)S(1)}, u32[]{:S(2)}, u32[]{:S(2)}) collective-permute-start(f32[512]{0:T(512)S(1)} %add.69), channel_id=1, source_target_pairs={{0,8},{4,12},{8,0},{12,4},{16,24},{20,28},{24,16},{28,20},{1,9},{5... | collective-permute-start | bytes 6152 | tf_op jit(solution)/shard_map/ppermute | solution.py:19
  35.2 2.0 %collective-permute-done.16 = f32[512]{0:T(512)S(1)} collective-permute-done((f32[512]{0:T(512)S(1)}, f32[512]{0:T(512)S(1)}, u32[]{:S(2)}, u32[]{:S(2)}) %collective-permute-start.16) | collective-permute-done | bytes 2080 | tf_op jit(solution)/shard_map/ppermute | solution.py:19
  37.3 1.6 %collective-permute-start.17 = (f32[512]{0:T(512)S(1)}, f32[512]{0:T(512)S(1)}, u32[]{:S(2)}, u32[]{:S(2)}) collective-permute-start(f32[512]{0:T(512)S(1)} %add.70), channel_id=1, source_target_pairs={{0,16},{4,20},{8,24},{12,28},{16,0},{20,4},{24,8},{28,12},{1,17},{... | collective-permute-start | bytes 6152 | tf_op jit(solution)/shard_map/ppermute | solution.py:19
  38.9 2.0 %collective-permute-done.17 = f32[512]{0:T(512)S(1)} collective-permute-done((f32[512]{0:T(512)S(1)}, f32[512]{0:T(512)S(1)}, u32[]{:S(2)}, u32[]{:S(2)}) %collective-permute-start.17) | collective-permute-done | bytes 2080 | tf_op jit(solution)/shard_map/ppermute | solution.py:19
  40.9 0.9 %broadcast_multiply_fusion = f32[256,512]{1,0:T(8,128)} fusion(f32[256,512]{1,0:T(8,128)S(1)} %get-tuple-element.14, f32[512]{0:T(512)S(1)} %add_divide_fusion), kind=kLoop, calls=%fused_computation.6 | loop fusion | flops 131072 | bytes 1050624 | tf_op jit(solution)/shard_map/mul | solution.py:103
  (20 shorter events, 0.3 us)
Async XLA Ops:
  0.0 11.4 %copy-start = (f32[256,512]{1,0:T(8,128)S(1)}, f32[256,512]{1,0:T(8,128)}, u32[]{:S(2)}) copy-start(f32[256,512]{1,0:T(8,128)} %param.2) | copy-start | bytes 1572868
  1.9 1.3 %collective-permute-start = (f32[512]{0:T(512)S(1)}, f32[512]{0:T(512)S(1)}, u32[]{:S(2)}, u32[]{:S(2)}) collective-permute-start(f32[512]{0:T(512)S(1)} %multiply_reduce_fusion), channel_id=1, source_target_pairs={{0,4},{4,0},{8,12},{12,8},{16,20},{20,16},{24,28},{28,24},{1,5},{5... | collective-permute-start | bytes 6152 | tf_op jit(solution)/shard_map/ppermute | solution.py:19
  3.2 4.4 %collective-permute-start.1 = (f32[512]{0:T(512)S(1)}, f32[512]{0:T(512)S(1)}, u32[]{:S(2)}, u32[]{:S(2)}) collective-permute-start(f32[512]{0:T(512)S(1)} %add.54), channel_id=1, source_target_pairs={{0,8},{4,12},{8,0},{12,4},{16,24},{20,28},{24,16},{28,20},{1,9},{5... | collective-permute-start | bytes 6152 | tf_op jit(solution)/shard_map/ppermute | solution.py:19
  7.6 3.6 %collective-permute-start.2 = (f32[512]{0:T(512)S(1)}, f32[512]{0:T(512)S(1)}, u32[]{:S(2)}, u32[]{:S(2)}) collective-permute-start(f32[512]{0:T(512)S(1)} %add.55), channel_id=1, source_target_pairs={{0,16},{4,20},{8,24},{12,28},{16,0},{20,4},{24,8},{28,12},{1,17},{... | collective-permute-start | bytes 6152 | tf_op jit(solution)/shard_map/ppermute | solution.py:19
  11.5 8.3 %collective-permute-start.4 = (bf16[160,512]{1,0:T(8,128)(2,1)S(1)}, bf16[160,512]{1,0:T(8,128)(2,1)S(1)}, u32[]{:S(2)}, u32[]{:S(2)}) collective-permute-start(bf16[160,512]{1,0:T(8,128)(2,1)S(1)} %slice.8), channel_id=1, source_target_pairs={{0,2},{1,3},{2,0},{3,1},{4,6},{5,7},{6,4},{7,5},{8,10},{9,11},{10,... | collective-permute-start | bytes 491528 | tf_op jit(solution)/shard_map/ppermute | solution.py:19
  14.7 9.4 %collective-permute-start.3 = (bf16[256,512]{1,0:T(8,128)(2,1)S(1)}, bf16[256,512]{1,0:T(8,128)(2,1)S(1)}, u32[]{:S(2)}, u32[]{:S(2)}) collective-permute-start(bf16[256,512]{1,0:T(8,128)(2,1)S(1)} %get-tuple-element.10), channel_id=1, source_target_pairs={{0,1},{1,0},{2,3},{3,2},{4,5},{5,4},{6,7},{7,6},{8,9},{9,8},{10,11... | collective-permute-start | bytes 786440 | tf_op jit(solution)/shard_map/ppermute | solution.py:19
  16.2 9.8 %collective-permute-start.7 = (bf16[256,512]{1,0:T(8,128)(2,1)S(1)}, bf16[256,512]{1,0:T(8,128)(2,1)S(1)}, u32[]{:S(2)}, u32[]{:S(2)}) collective-permute-start(bf16[256,512]{1,0:T(8,128)(2,1)S(1)} %get-tuple-element.10), channel_id=1, source_target_pairs={{0,8},{4,12},{8,0},{12,4},{16,24},{20,28},{24,16},{28,20},{1,9},{5... | collective-permute-start | bytes 786440 | tf_op jit(solution)/shard_map/ppermute | solution.py:19
  17.7 10.9 %collective-permute-start.11 = (bf16[256,512]{1,0:T(8,128)(2,1)S(1)}, bf16[256,512]{1,0:T(8,128)(2,1)S(1)}, u32[]{:S(2)}, u32[]{:S(2)}) collective-permute-start(bf16[256,512]{1,0:T(8,128)(2,1)S(1)} %get-tuple-element.10), channel_id=1, source_target_pairs={{0,16},{4,20},{8,24},{12,28},{16,0},{20,4},{24,8},{28,12},{1,17},{... | collective-permute-start | bytes 786440 | tf_op jit(solution)/shard_map/ppermute | solution.py:19
  19.2 9.4 %collective-permute-start.13 = (bf16[256,512]{1,0:T(8,128)(2,1)S(1)}, bf16[256,512]{1,0:T(8,128)(2,1)S(1)}, u32[]{:S(2)}, u32[]{:S(2)}) collective-permute-start(bf16[256,512]{1,0:T(8,128)(2,1)S(1)} %get-tuple-element.10), channel_id=1, source_target_pairs={{0,24},{4,28},{8,16},{12,20},{16,8},{20,12},{24,0},{28,4},{1,25},{... | collective-permute-start | bytes 786440 | tf_op jit(solution)/shard_map/ppermute | solution.py:19
  19.8 6.2 %collective-permute-start.5 = (bf16[96,512]{1,0:T(8,128)(2,1)S(1)}, bf16[96,512]{1,0:T(8,128)(2,1)S(1)}, u32[]{:S(2)}, u32[]{:S(2)}) collective-permute-start(bf16[96,512]{1,0:T(8,128)(2,1)S(1)} %slice.7), channel_id=1, source_target_pairs={{0,2},{1,3},{2,0},{3,1},{4,6},{5,7},{6,4},{7,5},{8,10},{9,11},{10,... | collective-permute-start | bytes 294920 | tf_op jit(solution)/shard_map/ppermute | solution.py:19
  24.0 5.7 %collective-permute-start.6 = (bf16[160,512]{1,0:T(8,128)(2,1)S(1)}, bf16[160,512]{1,0:T(8,128)(2,1)S(1)}, u32[]{:S(2)}, u32[]{:S(2)}) collective-permute-start(bf16[160,512]{1,0:T(8,128)(2,1)S(1)} %collective-permute-done.4), channel_id=1, source_target_pairs={{0,1},{1,0},{2,3},{3,2},{4,5},{5,4},{6,7},{7,6},{8,9},{9,8},{10,11... | collective-permute-start | bytes 491528 | tf_op jit(solution)/shard_map/ppermute | solution.py:19
  26.0 5.5 %collective-permute-start.9 = (bf16[256,512]{1,0:T(8,128)(2,1)S(1)}, bf16[256,512]{1,0:T(8,128)(2,1)S(1)}, u32[]{:S(2)}, u32[]{:S(2)}) collective-permute-start(bf16[256,512]{1,0:T(8,128)(2,1)S(1)} %get-tuple-element.10), channel_id=1, source_target_pairs={{0,4},{4,0},{8,12},{12,8},{16,20},{20,16},{24,28},{28,24},{1,5},{5... | collective-permute-start | bytes 786440 | tf_op jit(solution)/shard_map/ppermute | solution.py:19
  26.0 5.4 %collective-permute-start.8 = (bf16[96,512]{1,0:T(8,128)(2,1)S(1)}, bf16[96,512]{1,0:T(8,128)(2,1)S(1)}, u32[]{:S(2)}, u32[]{:S(2)}) collective-permute-start(bf16[96,512]{1,0:T(8,128)(2,1)S(1)} %collective-permute-done.5), channel_id=1, source_target_pairs={{0,1},{1,0},{2,3},{3,2},{4,5},{5,4},{6,7},{7,6},{8,9},{9,8},{10,11... | collective-permute-start | bytes 294920 | tf_op jit(solution)/shard_map/ppermute | solution.py:19
  28.6 3.0 %collective-permute-start.10 = (bf16[256,512]{1,0:T(8,128)(2,1)S(1)}, bf16[256,512]{1,0:T(8,128)(2,1)S(1)}, u32[]{:S(2)}, u32[]{:S(2)}) collective-permute-start(bf16[256,512]{1,0:T(8,128)(2,1)S(1)} %collective-permute-done.7), channel_id=1, source_target_pairs={{0,4},{4,0},{8,12},{12,8},{16,20},{20,16},{24,28},{28,24},{1,5},{5... | collective-permute-start | bytes 786440 | tf_op jit(solution)/shard_map/ppermute | solution.py:19
  28.6 3.0 %collective-permute-start.12 = (bf16[256,512]{1,0:T(8,128)(2,1)S(1)}, bf16[256,512]{1,0:T(8,128)(2,1)S(1)}, u32[]{:S(2)}, u32[]{:S(2)}) collective-permute-start(bf16[256,512]{1,0:T(8,128)(2,1)S(1)} %collective-permute-done.11), channel_id=1, source_target_pairs={{0,4},{4,0},{8,12},{12,8},{16,20},{20,16},{24,28},{28,24},{1,5},{5... | collective-permute-start | bytes 786440 | tf_op jit(solution)/shard_map/ppermute | solution.py:19
  29.7 2.0 %collective-permute-start.14 = (bf16[256,512]{1,0:T(8,128)(2,1)S(1)}, bf16[256,512]{1,0:T(8,128)(2,1)S(1)}, u32[]{:S(2)}, u32[]{:S(2)}) collective-permute-start(bf16[256,512]{1,0:T(8,128)(2,1)S(1)} %collective-permute-done.13), channel_id=1, source_target_pairs={{0,4},{4,0},{8,12},{12,8},{16,20},{20,16},{24,28},{28,24},{1,5},{5... | collective-permute-start | bytes 786440 | tf_op jit(solution)/shard_map/ppermute | solution.py:19
  32.5 1.2 %collective-permute-start.15 = (f32[512]{0:T(512)S(1)}, f32[512]{0:T(512)S(1)}, u32[]{:S(2)}, u32[]{:S(2)}) collective-permute-start(f32[512]{0:T(512)S(1)} %get-tuple-element.13), channel_id=1, source_target_pairs={{0,4},{4,0},{8,12},{12,8},{16,20},{20,16},{24,28},{28,24},{1,5},{5... | collective-permute-start | bytes 6152 | tf_op jit(solution)/shard_map/ppermute | solution.py:19
  33.7 3.6 %collective-permute-start.16 = (f32[512]{0:T(512)S(1)}, f32[512]{0:T(512)S(1)}, u32[]{:S(2)}, u32[]{:S(2)}) collective-permute-start(f32[512]{0:T(512)S(1)} %add.69), channel_id=1, source_target_pairs={{0,8},{4,12},{8,0},{12,4},{16,24},{20,28},{24,16},{28,20},{1,9},{5... | collective-permute-start | bytes 6152 | tf_op jit(solution)/shard_map/ppermute | solution.py:19
  37.3 3.6 %collective-permute-start.17 = (f32[512]{0:T(512)S(1)}, f32[512]{0:T(512)S(1)}, u32[]{:S(2)}, u32[]{:S(2)}) collective-permute-start(f32[512]{0:T(512)S(1)} %add.70), channel_id=1, source_target_pairs={{0,16},{4,20},{8,24},{12,28},{16,0},{20,4},{24,8},{28,12},{1,17},{... | collective-permute-start | bytes 6152 | tf_op jit(solution)/shard_map/ppermute | solution.py:19

commit v5 on v4

--- a/solution.py
+++ b/solution.py
@@ -71,7 +71,7 @@
 
 
 def gather(x):
-    first = x.shape[0] * 5 // 8 // 16 * 16
+    first = x.shape[0] * 9 // 16 // 16 * 16
     rows = {0: x}
     for mask in (2, 4, 6):
         rows[mask] = swap(x, "row", mask)

time: 41.9 us -> 41.7 us (level)
  transfers between devices with their start and end apart: 18 -> 18, of which waited for: 11 -> 10; matrix products, arithmetic and copies ran while one was open for 1% -> 1% of each run, Pallas kernels for 0% -> 0%
where the time goes in v5:
time: 41.7 us; the launch traced here: 41.6 us
  starting transfers between devices  24.4 us (59%)
  waiting for transfers between devices  12.8 us (31%)
  other arithmetic  2.83 us (7%)
  matrix products  0.72 us (2%)
  local copies, waits for them, and re-layouts  0.57 us (1%)
    ppermute x18, starting transfers between devices, swap(): return lax.ppermute(x, axis, [(i, i ^ mask) for i in range(size)])  24.4 us
    ppermute x18, waiting for transfers between devices, swap(): return lax.ppermute(x, axis, [(i, i ^ mask) for i in range(size)])  12.8 us
    reduce_sum x1, other arithmetic, shards(): scale = total_rows / total(jnp.sum(held, axis=0), 'row')  1.1 us
    mul x1, other arithmetic, shards(): return inflated * (total_rows / sums)[None, :]  0.87 us
  transfers between devices with their start and end apart: 18, of which 10 were waited for; matrix products, arithmetic and copies ran while one was open for 1% of the time, Pallas kernels for 0%

profile of v5, /device:TPU:0, one launch (start us, length us, event | category | flops | bytes accessed | tf_op | source)
XLA Modules:
  0.0 41.6 jit_solution(1437668777684594413)
XLA Ops:
  0.0 0.0 copy-start
  0.0 0.7 %convert_bitcast_fusion = f32[2]{0:T(128)S(1)} fusion(s32[1,2]{1,0:T(1,128)} %param.3), kind=kLoop, calls=%fused_computation.20 | loop fusion | flops 2 | bytes 16 | tf_op jit(solution)/shard_map/broadcast_in_dim | solution.py:12
  0.7 0.1 broadcast_bitcast_fusion
  0.8 1.1 %multiply_reduce_fusion = f32[512]{0:T(512)S(1)} fusion(f32[256,512]{1,0:T(8,128)} %param.2, f32[512]{0:T(512)S(1)} %bitcast.7), kind=kLoop, calls=%fused_computation.3 | loop fusion | flops 261632 | bytes 528384 | tf_op jit(solution)/shard_map/reduce_sum | solution.py:94
  1.9 0.5 %collective-permute-start = (f32[512]{0:T(512)S(1)}, f32[512]{0:T(512)S(1)}, u32[]{:S(2)}, u32[]{:S(2)}) collective-permute-start(f32[512]{0:T(512)S(1)} %multiply_reduce_fusion), channel_id=1, source_target_pairs={{0,4},{4,0},{8,12},{12,8},{16,20},{20,16},{24,28},{28,24},{1,5},{5... | collective-permute-start | bytes 6152 | tf_op jit(solution)/shard_map/ppermute | solution.py:19
  2.4 0.8 %collective-permute-done = f32[512]{0:T(512)S(1)} collective-permute-done((f32[512]{0:T(512)S(1)}, f32[512]{0:T(512)S(1)}, u32[]{:S(2)}, u32[]{:S(2)}) %collective-permute-start) | collective-permute-done | bytes 2080 | tf_op jit(solution)/shard_map/ppermute | solution.py:19
  3.2 2.8 %collective-permute-start.1 = (f32[512]{0:T(512)S(1)}, f32[512]{0:T(512)S(1)}, u32[]{:S(2)}, u32[]{:S(2)}) collective-permute-start(f32[512]{0:T(512)S(1)} %add.54), channel_id=1, source_target_pairs={{0,8},{4,12},{8,0},{12,4},{16,24},{20,28},{24,16},{28,20},{1,9},{5... | collective-permute-start | bytes 6152 | tf_op jit(solution)/shard_map/ppermute | solution.py:19
  6.1 1.6 %collective-permute-done.1 = f32[512]{0:T(512)S(1)} collective-permute-done((f32[512]{0:T(512)S(1)}, f32[512]{0:T(512)S(1)}, u32[]{:S(2)}, u32[]{:S(2)}) %collective-permute-start.1) | collective-permute-done | bytes 2080 | tf_op jit(solution)/shard_map/ppermute | solution.py:19
  7.6 2.1 %collective-permute-start.2 = (f32[512]{0:T(512)S(1)}, f32[512]{0:T(512)S(1)}, u32[]{:S(2)}, u32[]{:S(2)}) collective-permute-start(f32[512]{0:T(512)S(1)} %add.55), channel_id=1, source_target_pairs={{0,16},{4,20},{8,24},{12,28},{16,0},{20,4},{24,8},{28,12},{1,17},{... | collective-permute-start | bytes 6152 | tf_op jit(solution)/shard_map/ppermute | solution.py:19
  9.7 1.6 %collective-permute-done.2 = f32[512]{0:T(512)S(1)} collective-permute-done((f32[512]{0:T(512)S(1)}, f32[512]{0:T(512)S(1)}, u32[]{:S(2)}, u32[]{:S(2)}) %collective-permute-start.2) | collective-permute-done | bytes 2080 | tf_op jit(solution)/shard_map/ppermute | solution.py:19
  11.2 0.1 broadcast_in_dim.25
  11.4 0.0 copy-done
  11.4 0.1 constant_dynamic-update-slice_fusion.7
  11.5 3.2 %collective-permute-start.4 = (bf16[144,512]{1,0:T(8,128)(2,1)S(1)}, bf16[144,512]{1,0:T(8,128)(2,1)S(1)}, u32[]{:S(2)}, u32[]{:S(2)}) collective-permute-start(bf16[144,512]{1,0:T(8,128)(2,1)S(1)} %slice.8), channel_id=1, source_target_pairs={{0,2},{1,3},{2,0},{3,1},{4,6},{5,7},{6,4},{7,5},{8,10},{9,11},{10,... | collective-permute-start | bytes 442376 | tf_op jit(solution)/shard_map/ppermute | solution.py:19
  14.7 1.6 %collective-permute-start.3 = (bf16[256,512]{1,0:T(8,128)(2,1)S(1)}, bf16[256,512]{1,0:T(8,128)(2,1)S(1)}, u32[]{:S(2)}, u32[]{:S(2)}) collective-permute-start(bf16[256,512]{1,0:T(8,128)(2,1)S(1)} %get-tuple-element.10), channel_id=1, source_target_pairs={{0,1},{1,0},{2,3},{3,2},{4,5},{5,4},{6,7},{7,6},{8,9},{9,8},{10,11... | collective-permute-start | bytes 786440 | tf_op jit(solution)/shard_map/ppermute | solution.py:19
  16.2 1.5 %collective-permute-start.7 = (bf16[256,512]{1,0:T(8,128)(2,1)S(1)}, bf16[256,512]{1,0:T(8,128)(2,1)S(1)}, u32[]{:S(2)}, u32[]{:S(2)}) collective-permute-start(bf16[256,512]{1,0:T(8,128)(2,1)S(1)} %get-tuple-element.10), channel_id=1, source_target_pairs={{0,8},{4,12},{8,0},{12,4},{16,24},{20,28},{24,16},{28,20},{1,9},{5... | collective-permute-start | bytes 786440 | tf_op jit(solution)/shard_map/ppermute | solution.py:19
  17.7 1.5 %collective-permute-start.11 = (bf16[256,512]{1,0:T(8,128)(2,1)S(1)}, bf16[256,512]{1,0:T(8,128)(2,1)S(1)}, u32[]{:S(2)}, u32[]{:S(2)}) collective-permute-start(bf16[256,512]{1,0:T(8,128)(2,1)S(1)} %get-tuple-element.10), channel_id=1, source_target_pairs={{0,16},{4,20},{8,24},{12,28},{16,0},{20,4},{24,8},{28,12},{1,17},{... | collective-permute-start | bytes 786440 | tf_op jit(solution)/shard_map/ppermute | solution.py:19
  19.2 0.5 %collective-permute-start.13 = (bf16[256,512]{1,0:T(8,128)(2,1)S(1)}, bf16[256,512]{1,0:T(8,128)(2,1)S(1)}, u32[]{:S(2)}, u32[]{:S(2)}) collective-permute-start(bf16[256,512]{1,0:T(8,128)(2,1)S(1)} %get-tuple-element.10), channel_id=1, source_target_pairs={{0,24},{4,28},{8,16},{12,20},{16,8},{20,12},{24,0},{28,4},{1,25},{... | collective-permute-start | bytes 786440 | tf_op jit(solution)/shard_map/ppermute | solution.py:19
  19.7 0.0 collective-permute-done.4
  19.7 2.8 %collective-permute-start.5 = (bf16[112,512]{1,0:T(8,128)(2,1)S(1)}, bf16[112,512]{1,0:T(8,128)(2,1)S(1)}, u32[]{:S(2)}, u32[]{:S(2)}) collective-permute-start(bf16[112,512]{1,0:T(8,128)(2,1)S(1)} %slice.7), channel_id=1, source_target_pairs={{0,2},{1,3},{2,0},{3,1},{4,6},{5,7},{6,4},{7,5},{8,10},{9,11},{10,... | collective-permute-start | bytes 344072 | tf_op jit(solution)/shard_map/ppermute | solution.py:19
  22.5 0.1 broadcast_in_dim.20
  22.7 1.0 %collective-permute-done.3 = bf16[256,512]{1,0:T(8,128)(2,1)S(1)} collective-permute-done((bf16[256,512]{1,0:T(8,128)(2,1)S(1)}, bf16[256,512]{1,0:T(8,128)(2,1)S(1)}, u32[]{:S(2)}, u32[]{:S(2)}) %collective-permute-start.3) | collective-permute-done | bytes 262176 | tf_op jit(solution)/shard_map/ppermute | solution.py:19
  23.7 2.0 %collective-permute-start.6 = (bf16[144,512]{1,0:T(8,128)(2,1)S(1)}, bf16[144,512]{1,0:T(8,128)(2,1)S(1)}, u32[]{:S(2)}, u32[]{:S(2)}) collective-permute-start(bf16[144,512]{1,0:T(8,128)(2,1)S(1)} %collective-permute-done.4), channel_id=1, source_target_pairs={{0,1},{1,0},{2,3},{3,2},{4,5},{5,4},{6,7},{7,6},{8,9},{9,8},{10,11... | collective-permute-start | bytes 442376 | tf_op jit(solution)/shard_map/ppermute | solution.py:19
  25.7 0.0 collective-permute-done.7
  25.7 0.0 collective-permute-start.9
  25.7 0.0 collective-permute-done.5
  25.7 2.4 %collective-permute-start.8 = (bf16[112,512]{1,0:T(8,128)(2,1)S(1)}, bf16[112,512]{1,0:T(8,128)(2,1)S(1)}, u32[]{:S(2)}, u32[]{:S(2)}) collective-permute-start(bf16[112,512]{1,0:T(8,128)(2,1)S(1)} %collective-permute-done.5), channel_id=1, source_target_pairs={{0,1},{1,0},{2,3},{3,2},{4,5},{5,4},{6,7},{7,6},{8,9},{9,8},{10,11... | collective-permute-start | bytes 344072 | tf_op jit(solution)/shard_map/ppermute | solution.py:19
  28.1 0.5 %collective-permute-done.11 = bf16[256,512]{1,0:T(8,128)(2,1)S(1)} collective-permute-done((bf16[256,512]{1,0:T(8,128)(2,1)S(1)}, bf16[256,512]{1,0:T(8,128)(2,1)S(1)}, u32[]{:S(2)}, u32[]{:S(2)}) %collective-permute-start.11) | collective-permute-done | bytes 262176 | tf_op jit(solution)/shard_map/ppermute | solution.py:19
  28.6 0.0 collective-permute-start.10
  28.6 0.0 collective-permute-done.13
  28.6 0.5 %collective-permute-start.12 = (bf16[256,512]{1,0:T(8,128)(2,1)S(1)}, bf16[256,512]{1,0:T(8,128)(2,1)S(1)}, u32[]{:S(2)}, u32[]{:S(2)}) collective-permute-start(bf16[256,512]{1,0:T(8,128)(2,1)S(1)} %collective-permute-done.11), channel_id=1, source_target_pairs={{0,4},{4,0},{8,12},{12,8},{16,20},{20,16},{24,28},{28,24},{1,5},{5... | collective-permute-start | bytes 786440 | tf_op jit(solution)/shard_map/ppermute | solution.py:19
  29.1 0.3 collective-permute-done.6
  29.4 0.0 collective-permute-start.14
  29.4 1.9 %collective-permute-done.8 = bf16[112,512]{1,0:T(8,128)(2,1)S(1)} collective-permute-done((bf16[112,512]{1,0:T(8,128)(2,1)S(1)}, bf16[112,512]{1,0:T(8,128)(2,1)S(1)}, u32[]{:S(2)}, u32[]{:S(2)}) %collective-permute-start.8) | collective-permute-done | bytes 114720 | tf_op jit(solution)/shard_map/ppermute | solution.py:19
  31.3 0.0 collective-permute-done.9
  31.4 0.0 collective-permute-done.10
  31.5 0.0 collective-permute-done.12
  31.6 0.0 collective-permute-done.14
  31.6 0.7 %fusion.1 = (f32[512]{0:T(512)S(1)}, f32[256,512]{1,0:T(8,128)S(1)}) fusion(f32[512]{0:T(512)S(1)} %bitcast.9, bf16[256,2048]{1,0:T(8,128)(2,1)S(1)} %maximum_dynamic-update-slice_fusion.1, bf16[2048,512]{1,0:T(8,128)(2,1)S(1)} %constant_dynamic-update-slice_fusion), kind=kOutput, calls=%fused_computation.21 | convolution fusion | flops 537263616 | bytes 3674112 | tf_op jit(solution)/shard_map/dot_general | solution.py:100
  32.3 0.1 collective-permute-start.15
  32.4 1.1 %collective-permute-done.15 = f32[512]{0:T(512)S(1)} collective-permute-done((f32[512]{0:T(512)S(1)}, f32[512]{0:T(512)S(1)}, u32[]{:S(2)}, u32[]{:S(2)}) %collective-permute-start.15) | collective-permute-done | bytes 2080 | tf_op jit(solution)/shard_map/ppermute | solution.py:19
  33.5 1.5 %collective-permute-start.16 = (f32[512]{0:T(512)S(1)}, f32[512]{0:T(512)S(1)}, u32[]{:S(2)}, u32[]{:S(2)}) collective-permute-start(f32[512]{0:T(512)S(1)} %add.69), channel_id=1, source_target_pairs={{0,8},{4,12},{8,0},{12,4},{16,24},{20,28},{24,16},{28,20},{1,9},{5... | collective-permute-start | bytes 6152 | tf_op jit(solution)/shard_map/ppermute | solution.py:19
  35.1 2.0 %collective-permute-done.16 = f32[512]{0:T(512)S(1)} collective-permute-done((f32[512]{0:T(512)S(1)}, f32[512]{0:T(512)S(1)}, u32[]{:S(2)}, u32[]{:S(2)}) %collective-permute-start.16) | collective-permute-done | bytes 2080 | tf_op jit(solution)/shard_map/ppermute | solution.py:19
  37.1 1.6 %collective-permute-start.17 = (f32[512]{0:T(512)S(1)}, f32[512]{0:T(512)S(1)}, u32[]{:S(2)}, u32[]{:S(2)}) collective-permute-start(f32[512]{0:T(512)S(1)} %add.70), channel_id=1, source_target_pairs={{0,16},{4,20},{8,24},{12,28},{16,0},{20,4},{24,8},{28,12},{1,17},{... | collective-permute-start | bytes 6152 | tf_op jit(solution)/shard_map/ppermute | solution.py:19
  38.7 2.0 %collective-permute-done.17 = f32[512]{0:T(512)S(1)} collective-permute-done((f32[512]{0:T(512)S(1)}, f32[512]{0:T(512)S(1)}, u32[]{:S(2)}, u32[]{:S(2)}) %collective-permute-start.17) | collective-permute-done | bytes 2080 | tf_op jit(solution)/shard_map/ppermute | solution.py:19
  40.7 0.9 %broadcast_multiply_fusion = f32[256,512]{1,0:T(8,128)} fusion(f32[256,512]{1,0:T(8,128)S(1)} %get-tuple-element.14, f32[512]{0:T(512)S(1)} %add_divide_fusion), kind=kLoop, calls=%fused_computation.6 | loop fusion | flops 131072 | bytes 1050624 | tf_op jit(solution)/shard_map/mul | solution.py:103
  (20 shorter events, 0.3 us)
Async XLA Ops:
  0.0 11.4 %copy-start = (f32[256,512]{1,0:T(8,128)S(1)}, f32[256,512]{1,0:T(8,128)}, u32[]{:S(2)}) copy-start(f32[256,512]{1,0:T(8,128)} %param.2) | copy-start | bytes 1572868
  1.9 1.3 %collective-permute-start = (f32[512]{0:T(512)S(1)}, f32[512]{0:T(512)S(1)}, u32[]{:S(2)}, u32[]{:S(2)}) collective-permute-start(f32[512]{0:T(512)S(1)} %multiply_reduce_fusion), channel_id=1, source_target_pairs={{0,4},{4,0},{8,12},{12,8},{16,20},{20,16},{24,28},{28,24},{1,5},{5... | collective-permute-start | bytes 6152 | tf_op jit(solution)/shard_map/ppermute | solution.py:19
  3.2 4.4 %collective-permute-start.1 = (f32[512]{0:T(512)S(1)}, f32[512]{0:T(512)S(1)}, u32[]{:S(2)}, u32[]{:S(2)}) collective-permute-start(f32[512]{0:T(512)S(1)} %add.54), channel_id=1, source_target_pairs={{0,8},{4,12},{8,0},{12,4},{16,24},{20,28},{24,16},{28,20},{1,9},{5... | collective-permute-start | bytes 6152 | tf_op jit(solution)/shard_map/ppermute | solution.py:19
  7.6 3.6 %collective-permute-start.2 = (f32[512]{0:T(512)S(1)}, f32[512]{0:T(512)S(1)}, u32[]{:S(2)}, u32[]{:S(2)}) collective-permute-start(f32[512]{0:T(512)S(1)} %add.55), channel_id=1, source_target_pairs={{0,16},{4,20},{8,24},{12,28},{16,0},{20,4},{24,8},{28,12},{1,17},{... | collective-permute-start | bytes 6152 | tf_op jit(solution)/shard_map/ppermute | solution.py:19
  11.5 8.2 %collective-permute-start.4 = (bf16[144,512]{1,0:T(8,128)(2,1)S(1)}, bf16[144,512]{1,0:T(8,128)(2,1)S(1)}, u32[]{:S(2)}, u32[]{:S(2)}) collective-permute-start(bf16[144,512]{1,0:T(8,128)(2,1)S(1)} %slice.8), channel_id=1, source_target_pairs={{0,2},{1,3},{2,0},{3,1},{4,6},{5,7},{6,4},{7,5},{8,10},{9,11},{10,... | collective-permute-start | bytes 442376 | tf_op jit(solution)/shard_map/ppermute | solution.py:19
  14.7 9.0 %collective-permute-start.3 = (bf16[256,512]{1,0:T(8,128)(2,1)S(1)}, bf16[256,512]{1,0:T(8,128)(2,1)S(1)}, u32[]{:S(2)}, u32[]{:S(2)}) collective-permute-start(bf16[256,512]{1,0:T(8,128)(2,1)S(1)} %get-tuple-element.10), channel_id=1, source_target_pairs={{0,1},{1,0},{2,3},{3,2},{4,5},{5,4},{6,7},{7,6},{8,9},{9,8},{10,11... | collective-permute-start | bytes 786440 | tf_op jit(solution)/shard_map/ppermute | solution.py:19
  16.2 9.5 %collective-permute-start.7 = (bf16[256,512]{1,0:T(8,128)(2,1)S(1)}, bf16[256,512]{1,0:T(8,128)(2,1)S(1)}, u32[]{:S(2)}, u32[]{:S(2)}) collective-permute-start(bf16[256,512]{1,0:T(8,128)(2,1)S(1)} %get-tuple-element.10), channel_id=1, source_target_pairs={{0,8},{4,12},{8,0},{12,4},{16,24},{20,28},{24,16},{28,20},{1,9},{5... | collective-permute-start | bytes 786440 | tf_op jit(solution)/shard_map/ppermute | solution.py:19
  17.7 10.9 %collective-permute-start.11 = (bf16[256,512]{1,0:T(8,128)(2,1)S(1)}, bf16[256,512]{1,0:T(8,128)(2,1)S(1)}, u32[]{:S(2)}, u32[]{:S(2)}) collective-permute-start(bf16[256,512]{1,0:T(8,128)(2,1)S(1)} %get-tuple-element.10), channel_id=1, source_target_pairs={{0,16},{4,20},{8,24},{12,28},{16,0},{20,4},{24,8},{28,12},{1,17},{... | collective-permute-start | bytes 786440 | tf_op jit(solution)/shard_map/ppermute | solution.py:19
  19.2 9.4 %collective-permute-start.13 = (bf16[256,512]{1,0:T(8,128)(2,1)S(1)}, bf16[256,512]{1,0:T(8,128)(2,1)S(1)}, u32[]{:S(2)}, u32[]{:S(2)}) collective-permute-start(bf16[256,512]{1,0:T(8,128)(2,1)S(1)} %get-tuple-element.10), channel_id=1, source_target_pairs={{0,24},{4,28},{8,16},{12,20},{16,8},{20,12},{24,0},{28,4},{1,25},{... | collective-permute-start | bytes 786440 | tf_op jit(solution)/shard_map/ppermute | solution.py:19
  19.7 6.0 %collective-permute-start.5 = (bf16[112,512]{1,0:T(8,128)(2,1)S(1)}, bf16[112,512]{1,0:T(8,128)(2,1)S(1)}, u32[]{:S(2)}, u32[]{:S(2)}) collective-permute-start(bf16[112,512]{1,0:T(8,128)(2,1)S(1)} %slice.7), channel_id=1, source_target_pairs={{0,2},{1,3},{2,0},{3,1},{4,6},{5,7},{6,4},{7,5},{8,10},{9,11},{10,... | collective-permute-start | bytes 344072 | tf_op jit(solution)/shard_map/ppermute | solution.py:19
  23.7 5.7 %collective-permute-start.6 = (bf16[144,512]{1,0:T(8,128)(2,1)S(1)}, bf16[144,512]{1,0:T(8,128)(2,1)S(1)}, u32[]{:S(2)}, u32[]{:S(2)}) collective-permute-start(bf16[144,512]{1,0:T(8,128)(2,1)S(1)} %collective-permute-done.4), channel_id=1, source_target_pairs={{0,1},{1,0},{2,3},{3,2},{4,5},{5,4},{6,7},{7,6},{8,9},{9,8},{10,11... | collective-permute-start | bytes 442376 | tf_op jit(solution)/shard_map/ppermute | solution.py:19
  25.7 5.6 %collective-permute-start.9 = (bf16[256,512]{1,0:T(8,128)(2,1)S(1)}, bf16[256,512]{1,0:T(8,128)(2,1)S(1)}, u32[]{:S(2)}, u32[]{:S(2)}) collective-permute-start(bf16[256,512]{1,0:T(8,128)(2,1)S(1)} %get-tuple-element.10), channel_id=1, source_target_pairs={{0,4},{4,0},{8,12},{12,8},{16,20},{20,16},{24,28},{28,24},{1,5},{5... | collective-permute-start | bytes 786440 | tf_op jit(solution)/shard_map/ppermute | solution.py:19
  25.7 5.6 %collective-permute-start.8 = (bf16[112,512]{1,0:T(8,128)(2,1)S(1)}, bf16[112,512]{1,0:T(8,128)(2,1)S(1)}, u32[]{:S(2)}, u32[]{:S(2)}) collective-permute-start(bf16[112,512]{1,0:T(8,128)(2,1)S(1)} %collective-permute-done.5), channel_id=1, source_target_pairs={{0,1},{1,0},{2,3},{3,2},{4,5},{5,4},{6,7},{7,6},{8,9},{9,8},{10,11... | collective-permute-start | bytes 344072 | tf_op jit(solution)/shard_map/ppermute | solution.py:19
  28.6 2.8 %collective-permute-start.10 = (bf16[256,512]{1,0:T(8,128)(2,1)S(1)}, bf16[256,512]{1,0:T(8,128)(2,1)S(1)}, u32[]{:S(2)}, u32[]{:S(2)}) collective-permute-start(bf16[256,512]{1,0:T(8,128)(2,1)S(1)} %collective-permute-done.7), channel_id=1, source_target_pairs={{0,4},{4,0},{8,12},{12,8},{16,20},{20,16},{24,28},{28,24},{1,5},{5... | collective-permute-start | bytes 786440 | tf_op jit(solution)/shard_map/ppermute | solution.py:19
  28.6 2.9 %collective-permute-start.12 = (bf16[256,512]{1,0:T(8,128)(2,1)S(1)}, bf16[256,512]{1,0:T(8,128)(2,1)S(1)}, u32[]{:S(2)}, u32[]{:S(2)}) collective-permute-start(bf16[256,512]{1,0:T(8,128)(2,1)S(1)} %collective-permute-done.11), channel_id=1, source_target_pairs={{0,4},{4,0},{8,12},{12,8},{16,20},{20,16},{24,28},{28,24},{1,5},{5... | collective-permute-start | bytes 786440 | tf_op jit(solution)/shard_map/ppermute | solution.py:19
  29.4 2.1 %collective-permute-start.14 = (bf16[256,512]{1,0:T(8,128)(2,1)S(1)}, bf16[256,512]{1,0:T(8,128)(2,1)S(1)}, u32[]{:S(2)}, u32[]{:S(2)}) collective-permute-start(bf16[256,512]{1,0:T(8,128)(2,1)S(1)} %collective-permute-done.13), channel_id=1, source_target_pairs={{0,4},{4,0},{8,12},{12,8},{16,20},{20,16},{24,28},{28,24},{1,5},{5... | collective-permute-start | bytes 786440 | tf_op jit(solution)/shard_map/ppermute | solution.py:19
  32.3 1.2 %collective-permute-start.15 = (f32[512]{0:T(512)S(1)}, f32[512]{0:T(512)S(1)}, u32[]{:S(2)}, u32[]{:S(2)}) collective-permute-start(f32[512]{0:T(512)S(1)} %get-tuple-element.13), channel_id=1, source_target_pairs={{0,4},{4,0},{8,12},{12,8},{16,20},{20,16},{24,28},{28,24},{1,5},{5... | collective-permute-start | bytes 6152 | tf_op jit(solution)/shard_map/ppermute | solution.py:19
  33.5 3.6 %collective-permute-start.16 = (f32[512]{0:T(512)S(1)}, f32[512]{0:T(512)S(1)}, u32[]{:S(2)}, u32[]{:S(2)}) collective-permute-start(f32[512]{0:T(512)S(1)} %add.69), channel_id=1, source_target_pairs={{0,8},{4,12},{8,0},{12,4},{16,24},{20,28},{24,16},{28,20},{1,9},{5... | collective-permute-start | bytes 6152 | tf_op jit(solution)/shard_map/ppermute | solution.py:19
  37.1 3.6 %collective-permute-start.17 = (f32[512]{0:T(512)S(1)}, f32[512]{0:T(512)S(1)}, u32[]{:S(2)}, u32[]{:S(2)}) collective-permute-start(f32[512]{0:T(512)S(1)} %add.70), channel_id=1, source_target_pairs={{0,16},{4,20},{8,24},{12,28},{16,0},{20,4},{24,8},{28,12},{1,17},{... | collective-permute-start | bytes 6152 | tf_op jit(solution)/shard_map/ppermute | solution.py:19

commit v6 on v4

--- a/solution.py
+++ b/solution.py
@@ -36,10 +36,10 @@
     return whole
 
 
-def join_columns(blocks):
+def join_columns(blocks, zero=0):
     size, me = lax.axis_size("col"), lax.axis_index("col")
     depth, width = blocks[0].shape
-    whole = jnp.zeros((depth, size * width), blocks[0].dtype)
+    whole = jnp.full((depth, size * width), zero, blocks[0].dtype)
     for mask in range(size):
         whole = lax.dynamic_update_slice(whole, blocks[mask], (0, (me ^ mask) * width))
     return whole
@@ -84,7 +84,8 @@
     for mask in (2, 4, 6):
         rows[mask + 1] = swap(rows[mask], "row", 1)
     columns = [x, near, jnp.concatenate(far), jnp.concatenate(passed)]
-    return join_columns(columns), join_rows(rows)
+    zero = after(jnp.zeros((), x.dtype), far[0])
+    return join_columns(columns, zero), join_rows(rows)
 
 
 def shards(similarity, pattern):

time: 41.9 us -> 41.9 us (level)
  no operation moved by 1% of the time
where the time goes in v6:
time: 41.9 us; the launch traced here: 41.8 us
  starting transfers between devices  24.7 us (59%)
  waiting for transfers between devices  12.7 us (30%)
  other arithmetic  2.83 us (7%)
  matrix products  0.72 us (2%)
  local copies, waits for them, and re-layouts  0.57 us (1%)
    ppermute x18, starting transfers between devices, swap(): return lax.ppermute(x, axis, [(i, i ^ mask) for i in range(size)])  24.7 us
    ppermute x18, waiting for transfers between devices, swap(): return lax.ppermute(x, axis, [(i, i ^ mask) for i in range(size)])  12.7 us
    reduce_sum x1, other arithmetic, shards(): scale = total_rows / total(jnp.sum(held, axis=0), 'row')  1.1 us
    mul x1, other arithmetic, shards(): return inflated * (total_rows / sums)[None, :]  0.87 us
  transfers between devices with their start and end apart: 18, of which 11 were waited for; matrix products, arithmetic and copies ran while one was open for 1% of the time, Pallas kernels for 0%

profile of v6, /device:TPU:0, one launch (start us, length us, event | category | flops | bytes accessed | tf_op | source)
XLA Modules:
  0.0 41.8 jit_solution(4300225286014766103)
XLA Ops:
  0.0 0.0 copy-start
  0.0 0.7 %convert_bitcast_fusion = f32[2]{0:T(128)S(1)} fusion(s32[1,2]{1,0:T(1,128)} %param.3), kind=kLoop, calls=%fused_computation.20 | loop fusion | flops 2 | bytes 16 | tf_op jit(solution)/shard_map/broadcast_in_dim | solution.py:12
  0.7 0.1 broadcast_bitcast_fusion
  0.8 1.1 %multiply_reduce_fusion = f32[512]{0:T(512)S(1)} fusion(f32[256,512]{1,0:T(8,128)} %param.2, f32[512]{0:T(512)S(1)} %bitcast.7), kind=kLoop, calls=%fused_computation.3 | loop fusion | flops 261632 | bytes 528384 | tf_op jit(solution)/shard_map/reduce_sum | solution.py:95
  1.9 0.5 %collective-permute-start = (f32[512]{0:T(512)S(1)}, f32[512]{0:T(512)S(1)}, u32[]{:S(2)}, u32[]{:S(2)}) collective-permute-start(f32[512]{0:T(512)S(1)} %multiply_reduce_fusion), channel_id=1, source_target_pairs={{0,4},{4,0},{8,12},{12,8},{16,20},{20,16},{24,28},{28,24},{1,5},{5... | collective-permute-start | bytes 6152 | tf_op jit(solution)/shard_map/ppermute | solution.py:19
  2.4 0.8 %collective-permute-done = f32[512]{0:T(512)S(1)} collective-permute-done((f32[512]{0:T(512)S(1)}, f32[512]{0:T(512)S(1)}, u32[]{:S(2)}, u32[]{:S(2)}) %collective-permute-start) | collective-permute-done | bytes 2080 | tf_op jit(solution)/shard_map/ppermute | solution.py:19
  3.2 2.8 %collective-permute-start.1 = (f32[512]{0:T(512)S(1)}, f32[512]{0:T(512)S(1)}, u32[]{:S(2)}, u32[]{:S(2)}) collective-permute-start(f32[512]{0:T(512)S(1)} %add.54), channel_id=1, source_target_pairs={{0,8},{4,12},{8,0},{12,4},{16,24},{20,28},{24,16},{28,20},{1,9},{5... | collective-permute-start | bytes 6152 | tf_op jit(solution)/shard_map/ppermute | solution.py:19
  6.1 1.6 %collective-permute-done.1 = f32[512]{0:T(512)S(1)} collective-permute-done((f32[512]{0:T(512)S(1)}, f32[512]{0:T(512)S(1)}, u32[]{:S(2)}, u32[]{:S(2)}) %collective-permute-start.1) | collective-permute-done | bytes 2080 | tf_op jit(solution)/shard_map/ppermute | solution.py:19
  7.6 2.1 %collective-permute-start.2 = (f32[512]{0:T(512)S(1)}, f32[512]{0:T(512)S(1)}, u32[]{:S(2)}, u32[]{:S(2)}) collective-permute-start(f32[512]{0:T(512)S(1)} %add.55), channel_id=1, source_target_pairs={{0,16},{4,20},{8,24},{12,28},{16,0},{20,4},{24,8},{28,12},{1,17},{... | collective-permute-start | bytes 6152 | tf_op jit(solution)/shard_map/ppermute | solution.py:19
  9.7 1.6 %collective-permute-done.2 = f32[512]{0:T(512)S(1)} collective-permute-done((f32[512]{0:T(512)S(1)}, f32[512]{0:T(512)S(1)}, u32[]{:S(2)}, u32[]{:S(2)}) %collective-permute-start.2) | collective-permute-done | bytes 2080 | tf_op jit(solution)/shard_map/ppermute | solution.py:19
  11.2 0.1 broadcast_in_dim.25
  11.4 0.0 copy-done
  11.4 0.1 constant_dynamic-update-slice_fusion.7
  11.5 3.2 %collective-permute-start.3 = (bf16[160,512]{1,0:T(8,128)(2,1)S(1)}, bf16[160,512]{1,0:T(8,128)(2,1)S(1)}, u32[]{:S(2)}, u32[]{:S(2)}) collective-permute-start(bf16[160,512]{1,0:T(8,128)(2,1)S(1)} %slice.8), channel_id=1, source_target_pairs={{0,2},{1,3},{2,0},{3,1},{4,6},{5,7},{6,4},{7,5},{8,10},{9,11},{10,... | collective-permute-start | bytes 491528 | tf_op jit(solution)/shard_map/ppermute | solution.py:19
  14.7 1.6 %collective-permute-start.4 = (bf16[256,512]{1,0:T(8,128)(2,1)S(1)}, bf16[256,512]{1,0:T(8,128)(2,1)S(1)}, u32[]{:S(2)}, u32[]{:S(2)}) collective-permute-start(bf16[256,512]{1,0:T(8,128)(2,1)S(1)} %get-tuple-element.12), channel_id=1, source_target_pairs={{0,1},{1,0},{2,3},{3,2},{4,5},{5,4},{6,7},{7,6},{8,9},{9,8},{10,11... | collective-permute-start | bytes 786440 | tf_op jit(solution)/shard_map/ppermute | solution.py:19
  16.2 1.5 %collective-permute-start.7 = (bf16[256,512]{1,0:T(8,128)(2,1)S(1)}, bf16[256,512]{1,0:T(8,128)(2,1)S(1)}, u32[]{:S(2)}, u32[]{:S(2)}) collective-permute-start(bf16[256,512]{1,0:T(8,128)(2,1)S(1)} %get-tuple-element.12), channel_id=1, source_target_pairs={{0,8},{4,12},{8,0},{12,4},{16,24},{20,28},{24,16},{28,20},{1,9},{5... | collective-permute-start | bytes 786440 | tf_op jit(solution)/shard_map/ppermute | solution.py:19
  17.7 1.5 %collective-permute-start.11 = (bf16[256,512]{1,0:T(8,128)(2,1)S(1)}, bf16[256,512]{1,0:T(8,128)(2,1)S(1)}, u32[]{:S(2)}, u32[]{:S(2)}) collective-permute-start(bf16[256,512]{1,0:T(8,128)(2,1)S(1)} %get-tuple-element.12), channel_id=1, source_target_pairs={{0,16},{4,20},{8,24},{12,28},{16,0},{20,4},{24,8},{28,12},{1,17},{... | collective-permute-start | bytes 786440 | tf_op jit(solution)/shard_map/ppermute | solution.py:19
  19.2 0.5 %collective-permute-start.13 = (bf16[256,512]{1,0:T(8,128)(2,1)S(1)}, bf16[256,512]{1,0:T(8,128)(2,1)S(1)}, u32[]{:S(2)}, u32[]{:S(2)}) collective-permute-start(bf16[256,512]{1,0:T(8,128)(2,1)S(1)} %get-tuple-element.12), channel_id=1, source_target_pairs={{0,24},{4,28},{8,16},{12,20},{16,8},{20,12},{24,0},{28,4},{1,25},{... | collective-permute-start | bytes 786440 | tf_op jit(solution)/shard_map/ppermute | solution.py:19
  19.7 0.1 collective-permute-done.3
  19.8 3.1 %collective-permute-start.5 = (bf16[96,512]{1,0:T(8,128)(2,1)S(1)}, bf16[96,512]{1,0:T(8,128)(2,1)S(1)}, u32[]{:S(2)}, u32[]{:S(2)}) collective-permute-start(bf16[96,512]{1,0:T(8,128)(2,1)S(1)} %slice.7), channel_id=1, source_target_pairs={{0,2},{1,3},{2,0},{3,1},{4,6},{5,7},{6,4},{7,5},{8,10},{9,11},{10,... | collective-permute-start | bytes 294920 | tf_op jit(solution)/shard_map/ppermute | solution.py:19
  22.9 0.1 broadcast_in_dim.24
  23.0 1.0 %collective-permute-done.4 = bf16[256,512]{1,0:T(8,128)(2,1)S(1)} collective-permute-done((bf16[256,512]{1,0:T(8,128)(2,1)S(1)}, bf16[256,512]{1,0:T(8,128)(2,1)S(1)}, u32[]{:S(2)}, u32[]{:S(2)}) %collective-permute-start.4) | collective-permute-done | bytes 262176 | tf_op jit(solution)/shard_map/ppermute | solution.py:19
  24.0 2.0 %collective-permute-start.6 = (bf16[160,512]{1,0:T(8,128)(2,1)S(1)}, bf16[160,512]{1,0:T(8,128)(2,1)S(1)}, u32[]{:S(2)}, u32[]{:S(2)}) collective-permute-start(bf16[160,512]{1,0:T(8,128)(2,1)S(1)} %collective-permute-done.3), channel_id=1, source_target_pairs={{0,1},{1,0},{2,3},{3,2},{4,5},{5,4},{6,7},{7,6},{8,9},{9,8},{10,11... | collective-permute-start | bytes 491528 | tf_op jit(solution)/shard_map/ppermute | solution.py:19
  26.0 0.0 collective-permute-done.7
  26.0 0.0 collective-permute-start.9
  26.0 0.0 collective-permute-done.5
  26.0 2.4 %collective-permute-start.8 = (bf16[96,512]{1,0:T(8,128)(2,1)S(1)}, bf16[96,512]{1,0:T(8,128)(2,1)S(1)}, u32[]{:S(2)}, u32[]{:S(2)}) collective-permute-start(bf16[96,512]{1,0:T(8,128)(2,1)S(1)} %collective-permute-done.5), channel_id=1, source_target_pairs={{0,1},{1,0},{2,3},{3,2},{4,5},{5,4},{6,7},{7,6},{8,9},{9,8},{10,11... | collective-permute-start | bytes 294920 | tf_op jit(solution)/shard_map/ppermute | solution.py:19
  28.4 0.1 collective-permute-done.11
  28.6 0.0 collective-permute-start.10
  28.6 0.0 collective-permute-done.13
  28.6 0.5 %collective-permute-start.12 = (bf16[256,512]{1,0:T(8,128)(2,1)S(1)}, bf16[256,512]{1,0:T(8,128)(2,1)S(1)}, u32[]{:S(2)}, u32[]{:S(2)}) collective-permute-start(bf16[256,512]{1,0:T(8,128)(2,1)S(1)} %collective-permute-done.11), channel_id=1, source_target_pairs={{0,4},{4,0},{8,12},{12,8},{16,20},{20,16},{24,28},{28,24},{1,5},{5... | collective-permute-start | bytes 786440 | tf_op jit(solution)/shard_map/ppermute | solution.py:19
  29.1 0.6 %collective-permute-done.6 = bf16[160,512]{1,0:T(8,128)(2,1)S(1)} collective-permute-done((bf16[160,512]{1,0:T(8,128)(2,1)S(1)}, bf16[160,512]{1,0:T(8,128)(2,1)S(1)}, u32[]{:S(2)}, u32[]{:S(2)}) %collective-permute-start.6) | collective-permute-done | bytes 163872 | tf_op jit(solution)/shard_map/ppermute | solution.py:19
  29.7 0.0 collective-permute-start.14
  29.7 1.7 %collective-permute-done.8 = bf16[96,512]{1,0:T(8,128)(2,1)S(1)} collective-permute-done((bf16[96,512]{1,0:T(8,128)(2,1)S(1)}, bf16[96,512]{1,0:T(8,128)(2,1)S(1)}, u32[]{:S(2)}, u32[]{:S(2)}) %collective-permute-start.8) | collective-permute-done | bytes 98336 | tf_op jit(solution)/shard_map/ppermute | solution.py:19
  31.5 0.0 collective-permute-done.9
  31.6 0.0 collective-permute-done.10
  31.6 0.0 collective-permute-done.12
  31.7 0.0 collective-permute-done.14
  31.8 0.7 %fusion.1 = (f32[512]{0:T(512)S(1)}, f32[256,512]{1,0:T(8,128)S(1)}) fusion(f32[512]{0:T(512)S(1)} %bitcast.9, bf16[256,2048]{1,0:T(8,128)(2,1)S(1)} %maximum_dynamic-update-slice_fusion.1, bf16[2048,512]{1,0:T(8,128)(2,1)S(1)} %constant_dynamic-update-slice_fusion), kind=kOutput, calls=%fused_computation.21 | convolution fusion | flops 537263616 | bytes 3674112 | tf_op jit(solution)/shard_map/dot_general | solution.py:101
  32.5 0.1 collective-permute-start.15
  32.6 1.1 %collective-permute-done.15 = f32[512]{0:T(512)S(1)} collective-permute-done((f32[512]{0:T(512)S(1)}, f32[512]{0:T(512)S(1)}, u32[]{:S(2)}, u32[]{:S(2)}) %collective-permute-start.15) | collective-permute-done | bytes 2080 | tf_op jit(solution)/shard_map/ppermute | solution.py:19
  33.7 1.5 %collective-permute-start.16 = (f32[512]{0:T(512)S(1)}, f32[512]{0:T(512)S(1)}, u32[]{:S(2)}, u32[]{:S(2)}) collective-permute-start(f32[512]{0:T(512)S(1)} %add.69), channel_id=1, source_target_pairs={{0,8},{4,12},{8,0},{12,4},{16,24},{20,28},{24,16},{28,20},{1,9},{5... | collective-permute-start | bytes 6152 | tf_op jit(solution)/shard_map/ppermute | solution.py:19
  35.2 2.0 %collective-permute-done.16 = f32[512]{0:T(512)S(1)} collective-permute-done((f32[512]{0:T(512)S(1)}, f32[512]{0:T(512)S(1)}, u32[]{:S(2)}, u32[]{:S(2)}) %collective-permute-start.16) | collective-permute-done | bytes 2080 | tf_op jit(solution)/shard_map/ppermute | solution.py:19
  37.3 1.6 %collective-permute-start.17 = (f32[512]{0:T(512)S(1)}, f32[512]{0:T(512)S(1)}, u32[]{:S(2)}, u32[]{:S(2)}) collective-permute-start(f32[512]{0:T(512)S(1)} %add.70), channel_id=1, source_target_pairs={{0,16},{4,20},{8,24},{12,28},{16,0},{20,4},{24,8},{28,12},{1,17},{... | collective-permute-start | bytes 6152 | tf_op jit(solution)/shard_map/ppermute | solution.py:19
  38.9 2.0 %collective-permute-done.17 = f32[512]{0:T(512)S(1)} collective-permute-done((f32[512]{0:T(512)S(1)}, f32[512]{0:T(512)S(1)}, u32[]{:S(2)}, u32[]{:S(2)}) %collective-permute-start.17) | collective-permute-done | bytes 2080 | tf_op jit(solution)/shard_map/ppermute | solution.py:19
  40.9 0.9 %broadcast_multiply_fusion = f32[256,512]{1,0:T(8,128)} fusion(f32[256,512]{1,0:T(8,128)S(1)} %get-tuple-element.16, f32[512]{0:T(512)S(1)} %add_divide_fusion), kind=kLoop, calls=%fused_computation.6 | loop fusion | flops 131072 | bytes 1050624 | tf_op jit(solution)/shard_map/mul | solution.py:104
  (20 shorter events, 0.3 us)
Async XLA Ops:
  0.0 11.4 %copy-start = (f32[256,512]{1,0:T(8,128)S(1)}, f32[256,512]{1,0:T(8,128)}, u32[]{:S(2)}) copy-start(f32[256,512]{1,0:T(8,128)} %param.2) | copy-start | bytes 1572868
  1.9 1.3 %collective-permute-start = (f32[512]{0:T(512)S(1)}, f32[512]{0:T(512)S(1)}, u32[]{:S(2)}, u32[]{:S(2)}) collective-permute-start(f32[512]{0:T(512)S(1)} %multiply_reduce_fusion), channel_id=1, source_target_pairs={{0,4},{4,0},{8,12},{12,8},{16,20},{20,16},{24,28},{28,24},{1,5},{5... | collective-permute-start | bytes 6152 | tf_op jit(solution)/shard_map/ppermute | solution.py:19
  3.2 4.4 %collective-permute-start.1 = (f32[512]{0:T(512)S(1)}, f32[512]{0:T(512)S(1)}, u32[]{:S(2)}, u32[]{:S(2)}) collective-permute-start(f32[512]{0:T(512)S(1)} %add.54), channel_id=1, source_target_pairs={{0,8},{4,12},{8,0},{12,4},{16,24},{20,28},{24,16},{28,20},{1,9},{5... | collective-permute-start | bytes 6152 | tf_op jit(solution)/shard_map/ppermute | solution.py:19
  7.6 3.6 %collective-permute-start.2 = (f32[512]{0:T(512)S(1)}, f32[512]{0:T(512)S(1)}, u32[]{:S(2)}, u32[]{:S(2)}) collective-permute-start(f32[512]{0:T(512)S(1)} %add.55), channel_id=1, source_target_pairs={{0,16},{4,20},{8,24},{12,28},{16,0},{20,4},{24,8},{28,12},{1,17},{... | collective-permute-start | bytes 6152 | tf_op jit(solution)/shard_map/ppermute | solution.py:19
  11.5 8.3 %collective-permute-start.3 = (bf16[160,512]{1,0:T(8,128)(2,1)S(1)}, bf16[160,512]{1,0:T(8,128)(2,1)S(1)}, u32[]{:S(2)}, u32[]{:S(2)}) collective-permute-start(bf16[160,512]{1,0:T(8,128)(2,1)S(1)} %slice.8), channel_id=1, source_target_pairs={{0,2},{1,3},{2,0},{3,1},{4,6},{5,7},{6,4},{7,5},{8,10},{9,11},{10,... | collective-permute-start | bytes 491528 | tf_op jit(solution)/shard_map/ppermute | solution.py:19
  14.7 9.4 %collective-permute-start.4 = (bf16[256,512]{1,0:T(8,128)(2,1)S(1)}, bf16[256,512]{1,0:T(8,128)(2,1)S(1)}, u32[]{:S(2)}, u32[]{:S(2)}) collective-permute-start(bf16[256,512]{1,0:T(8,128)(2,1)S(1)} %get-tuple-element.12), channel_id=1, source_target_pairs={{0,1},{1,0},{2,3},{3,2},{4,5},{5,4},{6,7},{7,6},{8,9},{9,8},{10,11... | collective-permute-start | bytes 786440 | tf_op jit(solution)/shard_map/ppermute | solution.py:19
  16.2 9.8 %collective-permute-start.7 = (bf16[256,512]{1,0:T(8,128)(2,1)S(1)}, bf16[256,512]{1,0:T(8,128)(2,1)S(1)}, u32[]{:S(2)}, u32[]{:S(2)}) collective-permute-start(bf16[256,512]{1,0:T(8,128)(2,1)S(1)} %get-tuple-element.12), channel_id=1, source_target_pairs={{0,8},{4,12},{8,0},{12,4},{16,24},{20,28},{24,16},{28,20},{1,9},{5... | collective-permute-start | bytes 786440 | tf_op jit(solution)/shard_map/ppermute | solution.py:19
  17.7 10.9 %collective-permute-start.11 = (bf16[256,512]{1,0:T(8,128)(2,1)S(1)}, bf16[256,512]{1,0:T(8,128)(2,1)S(1)}, u32[]{:S(2)}, u32[]{:S(2)}) collective-permute-start(bf16[256,512]{1,0:T(8,128)(2,1)S(1)} %get-tuple-element.12), channel_id=1, source_target_pairs={{0,16},{4,20},{8,24},{12,28},{16,0},{20,4},{24,8},{28,12},{1,17},{... | collective-permute-start | bytes 786440 | tf_op jit(solution)/shard_map/ppermute | solution.py:19
  19.2 9.4 %collective-permute-start.13 = (bf16[256,512]{1,0:T(8,128)(2,1)S(1)}, bf16[256,512]{1,0:T(8,128)(2,1)S(1)}, u32[]{:S(2)}, u32[]{:S(2)}) collective-permute-start(bf16[256,512]{1,0:T(8,128)(2,1)S(1)} %get-tuple-element.12), channel_id=1, source_target_pairs={{0,24},{4,28},{8,16},{12,20},{16,8},{20,12},{24,0},{28,4},{1,25},{... | collective-permute-start | bytes 786440 | tf_op jit(solution)/shard_map/ppermute | solution.py:19
  19.8 6.2 %collective-permute-start.5 = (bf16[96,512]{1,0:T(8,128)(2,1)S(1)}, bf16[96,512]{1,0:T(8,128)(2,1)S(1)}, u32[]{:S(2)}, u32[]{:S(2)}) collective-permute-start(bf16[96,512]{1,0:T(8,128)(2,1)S(1)} %slice.7), channel_id=1, source_target_pairs={{0,2},{1,3},{2,0},{3,1},{4,6},{5,7},{6,4},{7,5},{8,10},{9,11},{10,... | collective-permute-start | bytes 294920 | tf_op jit(solution)/shard_map/ppermute | solution.py:19
  24.0 5.7 %collective-permute-start.6 = (bf16[160,512]{1,0:T(8,128)(2,1)S(1)}, bf16[160,512]{1,0:T(8,128)(2,1)S(1)}, u32[]{:S(2)}, u32[]{:S(2)}) collective-permute-start(bf16[160,512]{1,0:T(8,128)(2,1)S(1)} %collective-permute-done.3), channel_id=1, source_target_pairs={{0,1},{1,0},{2,3},{3,2},{4,5},{5,4},{6,7},{7,6},{8,9},{9,8},{10,11... | collective-permute-start | bytes 491528 | tf_op jit(solution)/shard_map/ppermute | solution.py:19
  26.0 5.5 %collective-permute-start.9 = (bf16[256,512]{1,0:T(8,128)(2,1)S(1)}, bf16[256,512]{1,0:T(8,128)(2,1)S(1)}, u32[]{:S(2)}, u32[]{:S(2)}) collective-permute-start(bf16[256,512]{1,0:T(8,128)(2,1)S(1)} %get-tuple-element.12), channel_id=1, source_target_pairs={{0,4},{4,0},{8,12},{12,8},{16,20},{20,16},{24,28},{28,24},{1,5},{5... | collective-permute-start | bytes 786440 | tf_op jit(solution)/shard_map/ppermute | solution.py:19
  26.0 5.4 %collective-permute-start.8 = (bf16[96,512]{1,0:T(8,128)(2,1)S(1)}, bf16[96,512]{1,0:T(8,128)(2,1)S(1)}, u32[]{:S(2)}, u32[]{:S(2)}) collective-permute-start(bf16[96,512]{1,0:T(8,128)(2,1)S(1)} %collective-permute-done.5), channel_id=1, source_target_pairs={{0,1},{1,0},{2,3},{3,2},{4,5},{5,4},{6,7},{7,6},{8,9},{9,8},{10,11... | collective-permute-start | bytes 294920 | tf_op jit(solution)/shard_map/ppermute | solution.py:19
  28.6 3.0 %collective-permute-start.10 = (bf16[256,512]{1,0:T(8,128)(2,1)S(1)}, bf16[256,512]{1,0:T(8,128)(2,1)S(1)}, u32[]{:S(2)}, u32[]{:S(2)}) collective-permute-start(bf16[256,512]{1,0:T(8,128)(2,1)S(1)} %collective-permute-done.7), channel_id=1, source_target_pairs={{0,4},{4,0},{8,12},{12,8},{16,20},{20,16},{24,28},{28,24},{1,5},{5... | collective-permute-start | bytes 786440 | tf_op jit(solution)/shard_map/ppermute | solution.py:19
  28.6 3.0 %collective-permute-start.12 = (bf16[256,512]{1,0:T(8,128)(2,1)S(1)}, bf16[256,512]{1,0:T(8,128)(2,1)S(1)}, u32[]{:S(2)}, u32[]{:S(2)}) collective-permute-start(bf16[256,512]{1,0:T(8,128)(2,1)S(1)} %collective-permute-done.11), channel_id=1, source_target_pairs={{0,4},{4,0},{8,12},{12,8},{16,20},{20,16},{24,28},{28,24},{1,5},{5... | collective-permute-start | bytes 786440 | tf_op jit(solution)/shard_map/ppermute | solution.py:19
  29.7 2.0 %collective-permute-start.14 = (bf16[256,512]{1,0:T(8,128)(2,1)S(1)}, bf16[256,512]{1,0:T(8,128)(2,1)S(1)}, u32[]{:S(2)}, u32[]{:S(2)}) collective-permute-start(bf16[256,512]{1,0:T(8,128)(2,1)S(1)} %collective-permute-done.13), channel_id=1, source_target_pairs={{0,4},{4,0},{8,12},{12,8},{16,20},{20,16},{24,28},{28,24},{1,5},{5... | collective-permute-start | bytes 786440 | tf_op jit(solution)/shard_map/ppermute | solution.py:19
  32.5 1.2 %collective-permute-start.15 = (f32[512]{0:T(512)S(1)}, f32[512]{0:T(512)S(1)}, u32[]{:S(2)}, u32[]{:S(2)}) collective-permute-start(f32[512]{0:T(512)S(1)} %get-tuple-element.15), channel_id=1, source_target_pairs={{0,4},{4,0},{8,12},{12,8},{16,20},{20,16},{24,28},{28,24},{1,5},{5... | collective-permute-start | bytes 6152 | tf_op jit(solution)/shard_map/ppermute | solution.py:19
  33.7 3.6 %collective-permute-start.16 = (f32[512]{0:T(512)S(1)}, f32[512]{0:T(512)S(1)}, u32[]{:S(2)}, u32[]{:S(2)}) collective-permute-start(f32[512]{0:T(512)S(1)} %add.69), channel_id=1, source_target_pairs={{0,8},{4,12},{8,0},{12,4},{16,24},{20,28},{24,16},{28,20},{1,9},{5... | collective-permute-start | bytes 6152 | tf_op jit(solution)/shard_map/ppermute | solution.py:19
  37.3 3.6 %collective-permute-start.17 = (f32[512]{0:T(512)S(1)}, f32[512]{0:T(512)S(1)}, u32[]{:S(2)}, u32[]{:S(2)}) collective-permute-start(f32[512]{0:T(512)S(1)} %add.70), channel_id=1, source_target_pairs={{0,16},{4,20},{8,24},{12,28},{16,0},{20,4},{24,8},{28,12},{1,17},{... | collective-permute-start | bytes 6152 | tf_op jit(solution)/shard_map/ppermute | solution.py:19

commit v7 on v5

--- a/solution.py
+++ b/solution.py
@@ -81,7 +81,8 @@
     passed = [swap(far[0], "col", 1)]
     far.append(swap(after(x, far[0])[first:], "col", 2))
     passed.append(swap(after(far[1], rows[2]), "col", 1))
-    for mask in (2, 4, 6):
+    rows[3] = swap(after(rows[2], far[1]), "row", 1)
+    for mask in (4, 6):
         rows[mask + 1] = swap(rows[mask], "row", 1)
     columns = [x, near, jnp.concatenate(far), jnp.concatenate(passed)]
     return join_columns(columns), join_rows(rows)

time: 41.7 us -> 41.7 us (level)
  no operation moved by 1% of the time
where the time goes in v7:
time: 41.7 us; the launch traced here: 41.6 us
  starting transfers between devices  24.4 us (59%)
  waiting for transfers between devices  12.8 us (31%)
  other arithmetic  2.83 us (7%)
  matrix products  0.72 us (2%)
  local copies, waits for them, and re-layouts  0.57 us (1%)
    ppermute x18, starting transfers between devices, swap(): return lax.ppermute(x, axis, [(i, i ^ mask) for i in range(size)])  24.4 us
    ppermute x18, waiting for transfers between devices, swap(): return lax.ppermute(x, axis, [(i, i ^ mask) for i in range(size)])  12.8 us
    reduce_sum x1, other arithmetic, shards(): scale = total_rows / total(jnp.sum(held, axis=0), 'row')  1.1 us
    mul x1, other arithmetic, shards(): return inflated * (total_rows / sums)[None, :]  0.87 us
  transfers between devices with their start and end apart: 18, of which 10 were waited for; matrix products, arithmetic and copies ran while one was open for 1% of the time, Pallas kernels for 0%

profile of v7, /device:TPU:0, one launch (start us, length us, event | category | flops | bytes accessed | tf_op | source)
XLA Modules:
  0.0 41.6 jit_solution(1437668777684594413)
XLA Ops:
  0.0 0.0 copy-start
  0.0 0.7 %convert_bitcast_fusion = f32[2]{0:T(128)S(1)} fusion(s32[1,2]{1,0:T(1,128)} %param.3), kind=kLoop, calls=%fused_computation.20 | loop fusion | flops 2 | bytes 16 | tf_op jit(solution)/shard_map/broadcast_in_dim | solution.py:12
  0.7 0.1 broadcast_bitcast_fusion
  0.8 1.1 %multiply_reduce_fusion = f32[512]{0:T(512)S(1)} fusion(f32[256,512]{1,0:T(8,128)} %param.2, f32[512]{0:T(512)S(1)} %bitcast.7), kind=kLoop, calls=%fused_computation.3 | loop fusion | flops 261632 | bytes 528384 | tf_op jit(solution)/shard_map/reduce_sum | solution.py:95
  1.9 0.5 %collective-permute-start = (f32[512]{0:T(512)S(1)}, f32[512]{0:T(512)S(1)}, u32[]{:S(2)}, u32[]{:S(2)}) collective-permute-start(f32[512]{0:T(512)S(1)} %multiply_reduce_fusion), channel_id=1, source_target_pairs={{0,4},{4,0},{8,12},{12,8},{16,20},{20,16},{24,28},{28,24},{1,5},{5... | collective-permute-start | bytes 6152 | tf_op jit(solution)/shard_map/ppermute | solution.py:19
  2.4 0.8 %collective-permute-done = f32[512]{0:T(512)S(1)} collective-permute-done((f32[512]{0:T(512)S(1)}, f32[512]{0:T(512)S(1)}, u32[]{:S(2)}, u32[]{:S(2)}) %collective-permute-start) | collective-permute-done | bytes 2080 | tf_op jit(solution)/shard_map/ppermute | solution.py:19
  3.2 2.8 %collective-permute-start.1 = (f32[512]{0:T(512)S(1)}, f32[512]{0:T(512)S(1)}, u32[]{:S(2)}, u32[]{:S(2)}) collective-permute-start(f32[512]{0:T(512)S(1)} %add.54), channel_id=1, source_target_pairs={{0,8},{4,12},{8,0},{12,4},{16,24},{20,28},{24,16},{28,20},{1,9},{5... | collective-permute-start | bytes 6152 | tf_op jit(solution)/shard_map/ppermute | solution.py:19
  6.1 1.6 %collective-permute-done.1 = f32[512]{0:T(512)S(1)} collective-permute-done((f32[512]{0:T(512)S(1)}, f32[512]{0:T(512)S(1)}, u32[]{:S(2)}, u32[]{:S(2)}) %collective-permute-start.1) | collective-permute-done | bytes 2080 | tf_op jit(solution)/shard_map/ppermute | solution.py:19
  7.6 2.1 %collective-permute-start.2 = (f32[512]{0:T(512)S(1)}, f32[512]{0:T(512)S(1)}, u32[]{:S(2)}, u32[]{:S(2)}) collective-permute-start(f32[512]{0:T(512)S(1)} %add.55), channel_id=1, source_target_pairs={{0,16},{4,20},{8,24},{12,28},{16,0},{20,4},{24,8},{28,12},{1,17},{... | collective-permute-start | bytes 6152 | tf_op jit(solution)/shard_map/ppermute | solution.py:19
  9.7 1.6 %collective-permute-done.2 = f32[512]{0:T(512)S(1)} collective-permute-done((f32[512]{0:T(512)S(1)}, f32[512]{0:T(512)S(1)}, u32[]{:S(2)}, u32[]{:S(2)}) %collective-permute-start.2) | collective-permute-done | bytes 2080 | tf_op jit(solution)/shard_map/ppermute | solution.py:19
  11.2 0.1 broadcast_in_dim.25
  11.4 0.0 copy-done
  11.4 0.1 constant_dynamic-update-slice_fusion.7
  11.5 3.2 %collective-permute-start.4 = (bf16[144,512]{1,0:T(8,128)(2,1)S(1)}, bf16[144,512]{1,0:T(8,128)(2,1)S(1)}, u32[]{:S(2)}, u32[]{:S(2)}) collective-permute-start(bf16[144,512]{1,0:T(8,128)(2,1)S(1)} %slice.8), channel_id=1, source_target_pairs={{0,2},{1,3},{2,0},{3,1},{4,6},{5,7},{6,4},{7,5},{8,10},{9,11},{10,... | collective-permute-start | bytes 442376 | tf_op jit(solution)/shard_map/ppermute | solution.py:19
  14.7 1.6 %collective-permute-start.3 = (bf16[256,512]{1,0:T(8,128)(2,1)S(1)}, bf16[256,512]{1,0:T(8,128)(2,1)S(1)}, u32[]{:S(2)}, u32[]{:S(2)}) collective-permute-start(bf16[256,512]{1,0:T(8,128)(2,1)S(1)} %get-tuple-element.11), channel_id=1, source_target_pairs={{0,1},{1,0},{2,3},{3,2},{4,5},{5,4},{6,7},{7,6},{8,9},{9,8},{10,11... | collective-permute-start | bytes 786440 | tf_op jit(solution)/shard_map/ppermute | solution.py:19
  16.2 1.5 %collective-permute-start.7 = (bf16[256,512]{1,0:T(8,128)(2,1)S(1)}, bf16[256,512]{1,0:T(8,128)(2,1)S(1)}, u32[]{:S(2)}, u32[]{:S(2)}) collective-permute-start(bf16[256,512]{1,0:T(8,128)(2,1)S(1)} %get-tuple-element.11), channel_id=1, source_target_pairs={{0,8},{4,12},{8,0},{12,4},{16,24},{20,28},{24,16},{28,20},{1,9},{5... | collective-permute-start | bytes 786440 | tf_op jit(solution)/shard_map/ppermute | solution.py:19
  17.7 1.5 %collective-permute-start.11 = (bf16[256,512]{1,0:T(8,128)(2,1)S(1)}, bf16[256,512]{1,0:T(8,128)(2,1)S(1)}, u32[]{:S(2)}, u32[]{:S(2)}) collective-permute-start(bf16[256,512]{1,0:T(8,128)(2,1)S(1)} %get-tuple-element.11), channel_id=1, source_target_pairs={{0,16},{4,20},{8,24},{12,28},{16,0},{20,4},{24,8},{28,12},{1,17},{... | collective-permute-start | bytes 786440 | tf_op jit(solution)/shard_map/ppermute | solution.py:19
  19.2 0.5 %collective-permute-start.13 = (bf16[256,512]{1,0:T(8,128)(2,1)S(1)}, bf16[256,512]{1,0:T(8,128)(2,1)S(1)}, u32[]{:S(2)}, u32[]{:S(2)}) collective-permute-start(bf16[256,512]{1,0:T(8,128)(2,1)S(1)} %get-tuple-element.11), channel_id=1, source_target_pairs={{0,24},{4,28},{8,16},{12,20},{16,8},{20,12},{24,0},{28,4},{1,25},{... | collective-permute-start | bytes 786440 | tf_op jit(solution)/shard_map/ppermute | solution.py:19
  19.7 0.0 collective-permute-done.4
  19.7 2.8 %collective-permute-start.5 = (bf16[112,512]{1,0:T(8,128)(2,1)S(1)}, bf16[112,512]{1,0:T(8,128)(2,1)S(1)}, u32[]{:S(2)}, u32[]{:S(2)}) collective-permute-start(bf16[112,512]{1,0:T(8,128)(2,1)S(1)} %slice.7), channel_id=1, source_target_pairs={{0,2},{1,3},{2,0},{3,1},{4,6},{5,7},{6,4},{7,5},{8,10},{9,11},{10,... | collective-permute-start | bytes 344072 | tf_op jit(solution)/shard_map/ppermute | solution.py:19
  22.5 0.1 broadcast_in_dim.20
  22.7 1.0 %collective-permute-done.3 = bf16[256,512]{1,0:T(8,128)(2,1)S(1)} collective-permute-done((bf16[256,512]{1,0:T(8,128)(2,1)S(1)}, bf16[256,512]{1,0:T(8,128)(2,1)S(1)}, u32[]{:S(2)}, u32[]{:S(2)}) %collective-permute-start.3) | collective-permute-done | bytes 262176 | tf_op jit(solution)/shard_map/ppermute | solution.py:19
  23.7 2.0 %collective-permute-start.6 = (bf16[144,512]{1,0:T(8,128)(2,1)S(1)}, bf16[144,512]{1,0:T(8,128)(2,1)S(1)}, u32[]{:S(2)}, u32[]{:S(2)}) collective-permute-start(bf16[144,512]{1,0:T(8,128)(2,1)S(1)} %collective-permute-done.4), channel_id=1, source_target_pairs={{0,1},{1,0},{2,3},{3,2},{4,5},{5,4},{6,7},{7,6},{8,9},{9,8},{10,11... | collective-permute-start | bytes 442376 | tf_op jit(solution)/shard_map/ppermute | solution.py:19
  25.7 0.0 collective-permute-done.7
  25.7 0.0 collective-permute-start.9
  25.7 0.0 collective-permute-done.5
  25.7 2.4 %collective-permute-start.8 = (bf16[112,512]{1,0:T(8,128)(2,1)S(1)}, bf16[112,512]{1,0:T(8,128)(2,1)S(1)}, u32[]{:S(2)}, u32[]{:S(2)}) collective-permute-start(bf16[112,512]{1,0:T(8,128)(2,1)S(1)} %collective-permute-done.5), channel_id=1, source_target_pairs={{0,1},{1,0},{2,3},{3,2},{4,5},{5,4},{6,7},{7,6},{8,9},{9,8},{10,11... | collective-permute-start | bytes 344072 | tf_op jit(solution)/shard_map/ppermute | solution.py:19
  28.1 0.5 %collective-permute-done.11 = bf16[256,512]{1,0:T(8,128)(2,1)S(1)} collective-permute-done((bf16[256,512]{1,0:T(8,128)(2,1)S(1)}, bf16[256,512]{1,0:T(8,128)(2,1)S(1)}, u32[]{:S(2)}, u32[]{:S(2)}) %collective-permute-start.11) | collective-permute-done | bytes 262176 | tf_op jit(solution)/shard_map/ppermute | solution.py:19
  28.6 0.0 collective-permute-start.10
  28.6 0.0 collective-permute-done.13
  28.6 0.5 %collective-permute-start.12 = (bf16[256,512]{1,0:T(8,128)(2,1)S(1)}, bf16[256,512]{1,0:T(8,128)(2,1)S(1)}, u32[]{:S(2)}, u32[]{:S(2)}) collective-permute-start(bf16[256,512]{1,0:T(8,128)(2,1)S(1)} %collective-permute-done.11), channel_id=1, source_target_pairs={{0,4},{4,0},{8,12},{12,8},{16,20},{20,16},{24,28},{28,24},{1,5},{5... | collective-permute-start | bytes 786440 | tf_op jit(solution)/shard_map/ppermute | solution.py:19
  29.1 0.3 collective-permute-done.6
  29.4 0.0 collective-permute-start.14
  29.4 1.9 %collective-permute-done.8 = bf16[112,512]{1,0:T(8,128)(2,1)S(1)} collective-permute-done((bf16[112,512]{1,0:T(8,128)(2,1)S(1)}, bf16[112,512]{1,0:T(8,128)(2,1)S(1)}, u32[]{:S(2)}, u32[]{:S(2)}) %collective-permute-start.8) | collective-permute-done | bytes 114720 | tf_op jit(solution)/shard_map/ppermute | solution.py:19
  31.3 0.0 collective-permute-done.9
  31.4 0.0 collective-permute-done.10
  31.5 0.0 collective-permute-done.12
  31.6 0.0 collective-permute-done.14
  31.6 0.7 %fusion.1 = (f32[512]{0:T(512)S(1)}, f32[256,512]{1,0:T(8,128)S(1)}) fusion(f32[512]{0:T(512)S(1)} %bitcast.9, bf16[256,2048]{1,0:T(8,128)(2,1)S(1)} %maximum_dynamic-update-slice_fusion.1, bf16[2048,512]{1,0:T(8,128)(2,1)S(1)} %constant_dynamic-update-slice_fusion), kind=kOutput, calls=%fused_computation.21 | convolution fusion | flops 537263616 | bytes 3674112 | tf_op jit(solution)/shard_map/dot_general | solution.py:101
  32.3 0.1 collective-permute-start.15
  32.4 1.1 %collective-permute-done.15 = f32[512]{0:T(512)S(1)} collective-permute-done((f32[512]{0:T(512)S(1)}, f32[512]{0:T(512)S(1)}, u32[]{:S(2)}, u32[]{:S(2)}) %collective-permute-start.15) | collective-permute-done | bytes 2080 | tf_op jit(solution)/shard_map/ppermute | solution.py:19
  33.5 1.5 %collective-permute-start.16 = (f32[512]{0:T(512)S(1)}, f32[512]{0:T(512)S(1)}, u32[]{:S(2)}, u32[]{:S(2)}) collective-permute-start(f32[512]{0:T(512)S(1)} %add.69), channel_id=1, source_target_pairs={{0,8},{4,12},{8,0},{12,4},{16,24},{20,28},{24,16},{28,20},{1,9},{5... | collective-permute-start | bytes 6152 | tf_op jit(solution)/shard_map/ppermute | solution.py:19
  35.1 2.0 %collective-permute-done.16 = f32[512]{0:T(512)S(1)} collective-permute-done((f32[512]{0:T(512)S(1)}, f32[512]{0:T(512)S(1)}, u32[]{:S(2)}, u32[]{:S(2)}) %collective-permute-start.16) | collective-permute-done | bytes 2080 | tf_op jit(solution)/shard_map/ppermute | solution.py:19
  37.1 1.6 %collective-permute-start.17 = (f32[512]{0:T(512)S(1)}, f32[512]{0:T(512)S(1)}, u32[]{:S(2)}, u32[]{:S(2)}) collective-permute-start(f32[512]{0:T(512)S(1)} %add.70), channel_id=1, source_target_pairs={{0,16},{4,20},{8,24},{12,28},{16,0},{20,4},{24,8},{28,12},{1,17},{... | collective-permute-start | bytes 6152 | tf_op jit(solution)/shard_map/ppermute | solution.py:19
  38.7 2.0 %collective-permute-done.17 = f32[512]{0:T(512)S(1)} collective-permute-done((f32[512]{0:T(512)S(1)}, f32[512]{0:T(512)S(1)}, u32[]{:S(2)}, u32[]{:S(2)}) %collective-permute-start.17) | collective-permute-done | bytes 2080 | tf_op jit(solution)/shard_map/ppermute | solution.py:19
  40.7 0.9 %broadcast_multiply_fusion = f32[256,512]{1,0:T(8,128)} fusion(f32[256,512]{1,0:T(8,128)S(1)} %get-tuple-element.16, f32[512]{0:T(512)S(1)} %add_divide_fusion), kind=kLoop, calls=%fused_computation.6 | loop fusion | flops 131072 | bytes 1050624 | tf_op jit(solution)/shard_map/mul | solution.py:104
  (20 shorter events, 0.3 us)
Async XLA Ops:
  0.0 11.4 %copy-start = (f32[256,512]{1,0:T(8,128)S(1)}, f32[256,512]{1,0:T(8,128)}, u32[]{:S(2)}) copy-start(f32[256,512]{1,0:T(8,128)} %param.2) | copy-start | bytes 1572868
  1.9 1.3 %collective-permute-start = (f32[512]{0:T(512)S(1)}, f32[512]{0:T(512)S(1)}, u32[]{:S(2)}, u32[]{:S(2)}) collective-permute-start(f32[512]{0:T(512)S(1)} %multiply_reduce_fusion), channel_id=1, source_target_pairs={{0,4},{4,0},{8,12},{12,8},{16,20},{20,16},{24,28},{28,24},{1,5},{5... | collective-permute-start | bytes 6152 | tf_op jit(solution)/shard_map/ppermute | solution.py:19
  3.2 4.4 %collective-permute-start.1 = (f32[512]{0:T(512)S(1)}, f32[512]{0:T(512)S(1)}, u32[]{:S(2)}, u32[]{:S(2)}) collective-permute-start(f32[512]{0:T(512)S(1)} %add.54), channel_id=1, source_target_pairs={{0,8},{4,12},{8,0},{12,4},{16,24},{20,28},{24,16},{28,20},{1,9},{5... | collective-permute-start | bytes 6152 | tf_op jit(solution)/shard_map/ppermute | solution.py:19
  7.6 3.6 %collective-permute-start.2 = (f32[512]{0:T(512)S(1)}, f32[512]{0:T(512)S(1)}, u32[]{:S(2)}, u32[]{:S(2)}) collective-permute-start(f32[512]{0:T(512)S(1)} %add.55), channel_id=1, source_target_pairs={{0,16},{4,20},{8,24},{12,28},{16,0},{20,4},{24,8},{28,12},{1,17},{... | collective-permute-start | bytes 6152 | tf_op jit(solution)/shard_map/ppermute | solution.py:19
  11.5 8.2 %collective-permute-start.4 = (bf16[144,512]{1,0:T(8,128)(2,1)S(1)}, bf16[144,512]{1,0:T(8,128)(2,1)S(1)}, u32[]{:S(2)}, u32[]{:S(2)}) collective-permute-start(bf16[144,512]{1,0:T(8,128)(2,1)S(1)} %slice.8), channel_id=1, source_target_pairs={{0,2},{1,3},{2,0},{3,1},{4,6},{5,7},{6,4},{7,5},{8,10},{9,11},{10,... | collective-permute-start | bytes 442376 | tf_op jit(solution)/shard_map/ppermute | solution.py:19
  14.7 9.0 %collective-permute-start.3 = (bf16[256,512]{1,0:T(8,128)(2,1)S(1)}, bf16[256,512]{1,0:T(8,128)(2,1)S(1)}, u32[]{:S(2)}, u32[]{:S(2)}) collective-permute-start(bf16[256,512]{1,0:T(8,128)(2,1)S(1)} %get-tuple-element.11), channel_id=1, source_target_pairs={{0,1},{1,0},{2,3},{3,2},{4,5},{5,4},{6,7},{7,6},{8,9},{9,8},{10,11... | collective-permute-start | bytes 786440 | tf_op jit(solution)/shard_map/ppermute | solution.py:19
  16.2 9.5 %collective-permute-start.7 = (bf16[256,512]{1,0:T(8,128)(2,1)S(1)}, bf16[256,512]{1,0:T(8,128)(2,1)S(1)}, u32[]{:S(2)}, u32[]{:S(2)}) collective-permute-start(bf16[256,512]{1,0:T(8,128)(2,1)S(1)} %get-tuple-element.11), channel_id=1, source_target_pairs={{0,8},{4,12},{8,0},{12,4},{16,24},{20,28},{24,16},{28,20},{1,9},{5... | collective-permute-start | bytes 786440 | tf_op jit(solution)/shard_map/ppermute | solution.py:19
  17.7 10.9 %collective-permute-start.11 = (bf16[256,512]{1,0:T(8,128)(2,1)S(1)}, bf16[256,512]{1,0:T(8,128)(2,1)S(1)}, u32[]{:S(2)}, u32[]{:S(2)}) collective-permute-start(bf16[256,512]{1,0:T(8,128)(2,1)S(1)} %get-tuple-element.11), channel_id=1, source_target_pairs={{0,16},{4,20},{8,24},{12,28},{16,0},{20,4},{24,8},{28,12},{1,17},{... | collective-permute-start | bytes 786440 | tf_op jit(solution)/shard_map/ppermute | solution.py:19
  19.2 9.4 %collective-permute-start.13 = (bf16[256,512]{1,0:T(8,128)(2,1)S(1)}, bf16[256,512]{1,0:T(8,128)(2,1)S(1)}, u32[]{:S(2)}, u32[]{:S(2)}) collective-permute-start(bf16[256,512]{1,0:T(8,128)(2,1)S(1)} %get-tuple-element.11), channel_id=1, source_target_pairs={{0,24},{4,28},{8,16},{12,20},{16,8},{20,12},{24,0},{28,4},{1,25},{... | collective-permute-start | bytes 786440 | tf_op jit(solution)/shard_map/ppermute | solution.py:19
  19.7 6.0 %collective-permute-start.5 = (bf16[112,512]{1,0:T(8,128)(2,1)S(1)}, bf16[112,512]{1,0:T(8,128)(2,1)S(1)}, u32[]{:S(2)}, u32[]{:S(2)}) collective-permute-start(bf16[112,512]{1,0:T(8,128)(2,1)S(1)} %slice.7), channel_id=1, source_target_pairs={{0,2},{1,3},{2,0},{3,1},{4,6},{5,7},{6,4},{7,5},{8,10},{9,11},{10,... | collective-permute-start | bytes 344072 | tf_op jit(solution)/shard_map/ppermute | solution.py:19
  23.7 5.7 %collective-permute-start.6 = (bf16[144,512]{1,0:T(8,128)(2,1)S(1)}, bf16[144,512]{1,0:T(8,128)(2,1)S(1)}, u32[]{:S(2)}, u32[]{:S(2)}) collective-permute-start(bf16[144,512]{1,0:T(8,128)(2,1)S(1)} %collective-permute-done.4), channel_id=1, source_target_pairs={{0,1},{1,0},{2,3},{3,2},{4,5},{5,4},{6,7},{7,6},{8,9},{9,8},{10,11... | collective-permute-start | bytes 442376 | tf_op jit(solution)/shard_map/ppermute | solution.py:19
  25.7 5.6 %collective-permute-start.9 = (bf16[256,512]{1,0:T(8,128)(2,1)S(1)}, bf16[256,512]{1,0:T(8,128)(2,1)S(1)}, u32[]{:S(2)}, u32[]{:S(2)}) collective-permute-start(bf16[256,512]{1,0:T(8,128)(2,1)S(1)} %get-tuple-element.11), channel_id=1, source_target_pairs={{0,4},{4,0},{8,12},{12,8},{16,20},{20,16},{24,28},{28,24},{1,5},{5... | collective-permute-start | bytes 786440 | tf_op jit(solution)/shard_map/ppermute | solution.py:19
  25.7 5.6 %collective-permute-start.8 = (bf16[112,512]{1,0:T(8,128)(2,1)S(1)}, bf16[112,512]{1,0:T(8,128)(2,1)S(1)}, u32[]{:S(2)}, u32[]{:S(2)}) collective-permute-start(bf16[112,512]{1,0:T(8,128)(2,1)S(1)} %collective-permute-done.5), channel_id=1, source_target_pairs={{0,1},{1,0},{2,3},{3,2},{4,5},{5,4},{6,7},{7,6},{8,9},{9,8},{10,11... | collective-permute-start | bytes 344072 | tf_op jit(solution)/shard_map/ppermute | solution.py:19
  28.6 2.8 %collective-permute-start.10 = (bf16[256,512]{1,0:T(8,128)(2,1)S(1)}, bf16[256,512]{1,0:T(8,128)(2,1)S(1)}, u32[]{:S(2)}, u32[]{:S(2)}) collective-permute-start(bf16[256,512]{1,0:T(8,128)(2,1)S(1)} %collective-permute-done.7), channel_id=1, source_target_pairs={{0,4},{4,0},{8,12},{12,8},{16,20},{20,16},{24,28},{28,24},{1,5},{5... | collective-permute-start | bytes 786440 | tf_op jit(solution)/shard_map/ppermute | solution.py:19
  28.6 2.9 %collective-permute-start.12 = (bf16[256,512]{1,0:T(8,128)(2,1)S(1)}, bf16[256,512]{1,0:T(8,128)(2,1)S(1)}, u32[]{:S(2)}, u32[]{:S(2)}) collective-permute-start(bf16[256,512]{1,0:T(8,128)(2,1)S(1)} %collective-permute-done.11), channel_id=1, source_target_pairs={{0,4},{4,0},{8,12},{12,8},{16,20},{20,16},{24,28},{28,24},{1,5},{5... | collective-permute-start | bytes 786440 | tf_op jit(solution)/shard_map/ppermute | solution.py:19
  29.4 2.1 %collective-permute-start.14 = (bf16[256,512]{1,0:T(8,128)(2,1)S(1)}, bf16[256,512]{1,0:T(8,128)(2,1)S(1)}, u32[]{:S(2)}, u32[]{:S(2)}) collective-permute-start(bf16[256,512]{1,0:T(8,128)(2,1)S(1)} %collective-permute-done.13), channel_id=1, source_target_pairs={{0,4},{4,0},{8,12},{12,8},{16,20},{20,16},{24,28},{28,24},{1,5},{5... | collective-permute-start | bytes 786440 | tf_op jit(solution)/shard_map/ppermute | solution.py:19
  32.3 1.2 %collective-permute-start.15 = (f32[512]{0:T(512)S(1)}, f32[512]{0:T(512)S(1)}, u32[]{:S(2)}, u32[]{:S(2)}) collective-permute-start(f32[512]{0:T(512)S(1)} %get-tuple-element.15), channel_id=1, source_target_pairs={{0,4},{4,0},{8,12},{12,8},{16,20},{20,16},{24,28},{28,24},{1,5},{5... | collective-permute-start | bytes 6152 | tf_op jit(solution)/shard_map/ppermute | solution.py:19
  33.5 3.6 %collective-permute-start.16 = (f32[512]{0:T(512)S(1)}, f32[512]{0:T(512)S(1)}, u32[]{:S(2)}, u32[]{:S(2)}) collective-permute-start(f32[512]{0:T(512)S(1)} %add.69), channel_id=1, source_target_pairs={{0,8},{4,12},{8,0},{12,4},{16,24},{20,28},{24,16},{28,20},{1,9},{5... | collective-permute-start | bytes 6152 | tf_op jit(solution)/shard_map/ppermute | solution.py:19
  37.1 3.6 %collective-permute-start.17 = (f32[512]{0:T(512)S(1)}, f32[512]{0:T(512)S(1)}, u32[]{:S(2)}, u32[]{:S(2)}) collective-permute-start(f32[512]{0:T(512)S(1)} %add.70), channel_id=1, source_target_pairs={{0,16},{4,20},{8,24},{12,28},{16,0},{20,4},{24,8},{28,12},{1,17},{... | collective-permute-start | bytes 6152 | tf_op jit(solution)/shard_map/ppermute | solution.py:19
